TPU v7x, 256 devices: a whole 4x4x8 slice. The times are simulated.
256 devices in a mesh: frame: 8 (over y_hi, x), tile: 32 (over z, y_lo, core).
Axes of the slice: x: 4, y: 4 (y_hi: 2, y_lo: 2; y = y_hi * 2 + y_lo), z: 8, core: 2. Of those that a mesh axis runs over, the one named last changes fastest.
Arguments:
- query_s: bfloat16 [16, 2048, 2048], P('frame', 'tile'), may hold values from -6 to 6
- key_s: bfloat16 [16, 2048, 2048], P('frame', 'tile'), may hold values from -6 to 6
- value_s: bfloat16 [16, 2048, 2048], P('frame', 'tile'), may hold values from -6 to 6
- grad_out_s: bfloat16 [16, 2048, 2048], P('frame', 'tile'), may hold values from -6 to 6
- query_t: bfloat16 [16, 2048, 2048], P('frame', 'tile'), may hold values from -6 to 6
- key_t: bfloat16 [16, 2048, 2048], P('frame', 'tile'), may hold values from -6 to 6
- value_t: bfloat16 [16, 2048, 2048], P('frame', 'tile'), may hold values from -6 to 6
- grad_out_t: bfloat16 [16, 2048, 2048], P('frame', 'tile'), may hold values from -6 to 6
- gains: float32 [4, 128], replicated, may hold values from 0.1 to 1.9
Outputs:
- out_s: bfloat16 [16, 2048, 2048], P('frame', 'tile')
- dquery_s: bfloat16 [16, 2048, 2048], P('frame', 'tile')
- dkey_s: bfloat16 [16, 2048, 2048], P('frame', 'tile')
- dvalue_s: bfloat16 [16, 2048, 2048], P('frame', 'tile')
- out_t: bfloat16 [16, 2048, 2048], P('frame', 'tile')
- dquery_t: bfloat16 [16, 2048, 2048], P('frame', 'tile')
- dkey_t: bfloat16 [16, 2048, 2048], P('frame', 'tile')
- dvalue_t: bfloat16 [16, 2048, 2048], P('frame', 'tile')
- gain_grads: float32 [4, 128], replicated
All inputs are finite; a program needn't handle non-finite values.
Results may differ from a plain program's by a relative error of at most 0.014.
Values may be sent and summed in bfloat16 or wider, within the bound.
No kernel may reach another device: no remote copies, remote signals or barrier semaphores. Data moves between devices by JAX's collectives and lax.ppermute only.
A program may use at most 128 MiB of HBM per device.

v0:
```python
import functools

import jax
import jax.numpy as jnp
from jax import lax
from jax.experimental import pallas as pl
from jax.experimental.pallas import tpu as pltpu
from jax.sharding import PartitionSpec as P

HEADS = 16
HEAD_DIM = 128
EPS = 1e-06
SCALE = HEAD_DIM**-0.5
LOG2E = 1.4426950408889634
BF16 = jnp.bfloat16
F32 = jnp.float32
SEQ = 2048
BLOCK = 256
ONES = 16
STEPS = ((0, 0), (0, 1), (0, 3), (1, 0), (1, 1), (1, 3), (0, 2), (1, 2))


def dot(a, b, ca, cb):
    return lax.dot_general(a, b, (((ca,), (cb,)), ((), ())), preferred_element_type=F32)


def params(mib):
    return pltpu.CompilerParams(vmem_limit_bytes=mib << 20)


def cost(flops, nbytes, trans=0):
    return pl.CostEstimate(flops=flops, bytes_accessed=nbytes, transcendentals=trans)


def inverse_rms(xf):
    return lax.rsqrt(jnp.mean(xf * xf, axis=-1, keepdims=True) + EPS)


def norm_back(grad_hat, x, gain):
    xf = x.astype(F32)
    inverse = inverse_rms(xf)
    unit = xf * inverse
    scaled = grad_hat * gain
    dgain = jnp.sum(grad_hat * unit, axis=0, keepdims=True)
    dx = inverse * (scaled - unit * jnp.mean(scaled * unit, axis=-1, keepdims=True))
    return dx.astype(BF16), dgain


def pack_s_kernel(q_ref, k_ref, v_ref, d_ref, o_ref):
    heads = o_ref.shape[1]
    for a, ref in enumerate((q_ref, k_ref, v_ref, d_ref)):
        for f in range(2):
            for h in range(heads):
                o_ref[f, h, a] = ref[f, :, h * HEAD_DIM : (h + 1) * HEAD_DIM]


def pack_s(arrays):
    frames, places, width = arrays[0].shape
    group = 4
    out = pl.pallas_call(
        pack_s_kernel,
        out_shape=jax.ShapeDtypeStruct((frames, HEADS, 4, places, HEAD_DIM), BF16),
        grid=(HEADS // group,),
        in_specs=[pl.BlockSpec((frames, places, group * HEAD_DIM), lambda i: (0, 0, i))] * 4,
        out_specs=pl.BlockSpec((frames, group, 4, places, HEAD_DIM), lambda i: (0, i, 0, 0, 0)),
        compiler_params=params(16),
        cost_estimate=cost(0, 4 << 20),
        name="pack_spatial",
    )(*arrays)
    return out.reshape(frames * HEADS, 4, places, HEAD_DIM)


def unpack_s_kernel(x_ref, *out_refs):
    heads = x_ref.shape[1]
    for a, ref in enumerate(out_refs):
        for f in range(2):
            for h in range(heads):
                ref[f, :, h * HEAD_DIM : (h + 1) * HEAD_DIM] = x_ref[f, h, a]


def unpack_s(x, frames):
    places = x.shape[2]
    group = 4
    return pl.pallas_call(
        unpack_s_kernel,
        out_shape=[jax.ShapeDtypeStruct((frames, places, HEADS * HEAD_DIM), BF16)] * 4,
        grid=(HEADS // group,),
        in_specs=[pl.BlockSpec((frames, group, 4, places, HEAD_DIM), lambda i: (0, i, 0, 0, 0))],
        out_specs=[pl.BlockSpec((frames, places, group * HEAD_DIM), lambda i: (0, 0, i))] * 4,
        compiler_params=params(16),
        cost_estimate=cost(0, 4 << 20),
        name="unpack_spatial",
    )(x.reshape(frames, HEADS, 4, places, HEAD_DIM))


def lanes_of(at_ref, j, width):
    return pl.ds(pl.multiple_of(at_ref[j] * width, width), width)


def pack_t_kernel(at_ref, q_ref, k_ref, v_ref, d_ref, *out_refs):
    width = out_refs[0].shape[-1]
    for j, out in enumerate(out_refs):
        lanes = lanes_of(at_ref, j, width)
        for a, ref in enumerate((q_ref, k_ref, v_ref, d_ref)):
            out[a] = ref[:, :, lanes]


def pack_t(at, arrays):
    frames, places, width = arrays[0].shape
    part = width // len(STEPS)
    return pl.pallas_call(
        pack_t_kernel,
        out_shape=[jax.ShapeDtypeStruct((4, frames, places, part), BF16)] * len(STEPS),
        in_specs=[pl.BlockSpec(memory_space=pltpu.SMEM)] + [pl.BlockSpec(memory_space=pltpu.VMEM)] * 4,
        out_specs=[pl.BlockSpec(memory_space=pltpu.VMEM)] * len(STEPS),
        compiler_params=params(16),
        cost_estimate=cost(0, 4 << 20),
        name="pack_temporal",
    )(at, *arrays)


def unpack_t_kernel(at_ref, *refs):
    parts, outs = refs[: len(STEPS)], refs[len(STEPS) :]
    width = parts[0].shape[-1]
    for j, part in enumerate(parts):
        lanes = lanes_of(at_ref, j, width)
        for a, out in enumerate(outs):
            out[:, :, lanes] = part[a]


def unpack_t(at, parts):
    _, frames, places, part = parts[0].shape
    return pl.pallas_call(
        unpack_t_kernel,
        out_shape=[jax.ShapeDtypeStruct((frames, places, part * len(STEPS)), BF16)] * 4,
        in_specs=[pl.BlockSpec(memory_space=pltpu.SMEM)]
        + [pl.BlockSpec(memory_space=pltpu.VMEM)] * len(STEPS),
        out_specs=[pl.BlockSpec(memory_space=pltpu.VMEM)] * 4,
        compiler_params=params(16),
        cost_estimate=cost(0, 4 << 20),
        name="unpack_temporal",
    )(at, *parts)


def temporal_kernel(gains_ref, *refs):
    count = len(STEPS)
    ins, outs, dgain_ref = refs[:count], refs[count : 2 * count], refs[2 * count]
    _, frames, places, width = ins[0].shape
    rows = count * frames * 16
    gain_q, gain_k = gains_ref[2:3, :], gains_ref[3:4, :]
    row = lax.broadcasted_iota(jnp.int32, (rows, rows), 0)
    column = lax.broadcasted_iota(jnp.int32, (rows, rows), 1)
    same = (row % 16) == (column % 16)
    dgain_ref[...] = jnp.zeros_like(dgain_ref)

    def step(block, _):
        at = pl.ds(pl.multiple_of(block * 16, 16), 16)
        for h in range(width // HEAD_DIM):
            lanes = slice(h * HEAD_DIM, (h + 1) * HEAD_DIM)

            def take(a):
                return jnp.concatenate([ref[a, f, at, lanes] for ref in ins for f in range(frames)], axis=0)

            query, key, value, dout = take(0), take(1), take(2), take(3)
            qf, kf = query.astype(F32), key.astype(F32)
            qh = (qf * inverse_rms(qf) * gain_q).astype(BF16)
            kh = (kf * inverse_rms(kf) * gain_k).astype(BF16)
            expo = jnp.where(same, jnp.exp(dot(qh, kh, 1, 1) * SCALE), 0.0)
            probs = expo / jnp.sum(expo, axis=-1, keepdims=True)
            probs_b = probs.astype(BF16)
            out = dot(probs_b, value, 1, 0)
            dprob = dot(dout, value, 1, 1)
            delta = jnp.sum(dout.astype(F32) * out, axis=-1, keepdims=True)
            dscore = (probs * (dprob - delta)).astype(BF16)
            dqh = dot(dscore, kh, 1, 0) * SCALE
            dkh = dot(dscore, qh, 0, 0) * SCALE
            dvalue = dot(probs_b, dout, 0, 0)
            dquery, dgain_q = norm_back(dqh, query, gain_q)
            dkey, dgain_k = norm_back(dkh, key, gain_k)
            dgain_ref[0:1, :] += dgain_q
            dgain_ref[1:2, :] += dgain_k
            for a, res in enumerate((out.astype(BF16), dquery, dkey, dvalue.astype(BF16))):
                for j, ref in enumerate(outs):
                    for f in range(frames):
                        first = (j * frames + f) * 16
                        ref[a, f, at, lanes] = res[first : first + 16]
        return 0

    lax.fori_loop(0, places // 16, step, 0)


def temporal(gains, parts):
    whole = pl.BlockSpec(memory_space=pltpu.VMEM)
    res = pl.pallas_call(
        temporal_kernel,
        out_shape=[jax.ShapeDtypeStruct(p.shape, BF16) for p in parts] + [jax.ShapeDtypeStruct((2, HEAD_DIM), F32)],
        in_specs=[whole] * (1 + len(parts)),
        out_specs=[whole] * (1 + len(parts)),
        compiler_params=params(24),
        cost_estimate=cost(8 * 6 * 2 * 256 * 256 * 128, 4 << 20, 8 * 65536),
        name="temporal_attention",
    )(gains, *parts)
    return res[:-1], res[-1]


def spatial_kernel(gains_ref, x_ref, out_ref, dgain_ref, qh, kh, kh_t, v_t, expo, dscore, out_t, dp_t, dp_n, dq_t):
    tiles, _, places, depth = x_ref.shape
    seq = tiles * places
    per = BLOCK // places
    gain_q, gain_k = gains_ref[0:1, :], gains_ref[1:2, :]

    def rows_of(b):
        return pl.ds(pl.multiple_of(b * BLOCK, BLOCK), BLOCK)

    def read(a, b):
        return x_ref[pl.ds(b * per, per), a].reshape(BLOCK, depth)

    def write(a, b, value):
        out_ref[pl.ds(b * per, per), a] = value.astype(BF16).reshape(per, places, depth)

    def prepare(b, _):
        rows = rows_of(b)
        qf = read(0, b).astype(F32)
        qh[rows, :] = (qf * inverse_rms(qf) * gain_q).astype(BF16)
        kf = read(1, b).astype(F32)
        k_hat = (kf * inverse_rms(kf) * gain_k).astype(BF16)
        kh[rows, :] = k_hat
        kh_t[:, rows] = k_hat.T
        v_t[0:depth, rows] = read(2, b).T
        v_t[depth:, rows] = jnp.ones((ONES, BLOCK), BF16)
        return 0

    lax.fori_loop(0, seq // BLOCK, prepare, 0)

    def forward(b, _):
        rows = rows_of(b)
        q_b = qh[rows, :]
        for c in range(seq // BLOCK):
            keys = slice(c * BLOCK, (c + 1) * BLOCK)
            scores = dot(kh[keys, :], q_b, 1, 1)
            expo[keys, rows] = jnp.exp2(scores * (SCALE * LOG2E)).astype(BF16)
        out_t[...] = dot(v_t[...], expo[:, rows], 1, 0)
        inverse = 1.0 / out_t[depth : depth + 1, :]
        o_t = out_t[0:depth, :] * inverse
        write(0, b, o_t.astype(BF16).T)
        d_t = (read(3, b).T.astype(F32) * inverse).astype(BF16)
        delta = jnp.sum(d_t.astype(F32) * o_t, axis=0, keepdims=True)
        dp_t[:, rows] = d_t
        dp_n[rows, :] = d_t.T
        for c in range(seq // BLOCK):
            keys = slice(c * BLOCK, (c + 1) * BLOCK)
            value = x_ref[c * per : (c + 1) * per, 2].reshape(BLOCK, depth)
            grad = dot(value, d_t, 1, 0)
            dscore[keys, rows] = (expo[keys, rows].astype(F32) * (grad - delta)).astype(BF16)
        dq_t[...] = dot(kh_t[...], dscore[:, rows], 1, 0) * SCALE
        dquery, dgain = norm_back(dq_t[...].T, read(0, b), gain_q)
        write(1, b, dquery)
        dgain_ref[0:1, :] += dgain
        return 0

    dgain_ref[...] = jnp.zeros_like(dgain_ref)
    lax.fori_loop(0, seq // BLOCK, forward, 0)

    def backward(b, _):
        rows = rows_of(b)
        dkh = dot(dscore[rows, :], qh[...], 1, 0) * SCALE
        dkey, dgain = norm_back(dkh, read(1, b), gain_k)
        write(2, b, dkey)
        dgain_ref[1:2, :] += dgain
        write(3, b, dot(expo[rows, :], dp_n[...], 1, 0))
        return 0

    lax.fori_loop(0, seq // BLOCK, backward, 0)


def spatial(gains, x):
    tiles, _, places, depth = x.shape
    seq = tiles * places
    whole = pl.BlockSpec(memory_space=pltpu.VMEM)
    return pl.pallas_call(
        spatial_kernel,
        out_shape=[jax.ShapeDtypeStruct(x.shape, BF16), jax.ShapeDtypeStruct((2, depth), F32)],
        in_specs=[whole, whole],
        out_specs=[whole, whole],
        scratch_shapes=[
            pltpu.VMEM((seq, depth), BF16),
            pltpu.VMEM((seq, depth), BF16),
            pltpu.VMEM((depth, seq), BF16),
            pltpu.VMEM((depth + ONES, seq), BF16),
            pltpu.VMEM((seq, seq), BF16),
            pltpu.VMEM((seq, seq), BF16),
            pltpu.VMEM((depth + ONES, BLOCK), F32),
            pltpu.VMEM((depth, seq), BF16),
            pltpu.VMEM((seq, depth), BF16),
            pltpu.VMEM((depth, BLOCK), F32),
        ],
        compiler_params=params(40),
        cost_estimate=cost(6 * 2 * seq * seq * depth, 4 << 20, seq * seq),
        name="spatial_attention",
    )(gains, x)


def shift(step):
    return [(i, ((i // 4 + step[0]) % 2) * 4 + (i % 4 + step[1]) % 4) for i in range(8)]


def exchange(parts, back):
    sent = [parts[0]]
    for part, step in zip(parts[1:], STEPS[1:]):
        step = tuple(-s for s in step) if back else step
        sent.append(lax.ppermute(part, "frame", shift(step)))
    return sent


def total(x):
    for axis, size in (("frame", 8), ("tile", 32)):
        bit = 1
        while bit < size:
            x = x + lax.ppermute(x, axis, [(i, i ^ bit) for i in range(size)])
            bit *= 2
    return x


def local(query_s, key_s, value_s, grad_out_s, query_t, key_t, value_t, grad_out_t, gains):
    frames = query_s.shape[0]
    me = lax.axis_index("frame")
    at = jnp.stack([((me // 4 + dy) % 2) * 4 + (me % 4 + dx) % 4 for dy, dx in STEPS]).astype(jnp.int32)

    sent = pack_s((query_s, key_s, value_s, grad_out_s))
    items = lax.all_to_all(sent, "tile", split_axis=0, concat_axis=0, tiled=True)

    parts = exchange(pack_t(at, (query_t, key_t, value_t, grad_out_t)), False)
    parts, grads_t = temporal(gains, parts)
    outs_t = unpack_t(at, exchange(parts, True))

    res, grads_s = spatial(gains, items)
    home = lax.all_to_all(res, "tile", split_axis=0, concat_axis=0, tiled=True)
    outs_s = unpack_s(home, frames)

    gain_grads = total(jnp.concatenate([grads_s, grads_t], axis=0))
    return (*outs_s, *outs_t, gain_grads)


def solution(mesh):
    split = P("frame", "tile", None)
    return jax.shard_map(
        local,
        mesh=mesh,
        in_specs=(split,) * 8 + (P(),),
        out_specs=(split,) * 8 + (P(),),
        check_vma=False,
    )
```

profile of v0, /device:TPU:2, one launch (start us, length us, event | category | flops | bytes accessed | tf_op | source)
XLA Modules:
  0.0 215.1 jit_solution(7334135542801241375)
XLA Ops:
  0.7 1.0 copy-done.5
  1.7 1.0 copy-done.6
  2.7 1.0 copy-done.7
  3.8 1.0 copy-done.8
  4.8 0.7 pack_spatial.1
  5.6 0.0 copy-start.9
  5.6 61.2 %all_to_all.10.x_ref = bf16[32,4,64,128]{3,2,1,0:T(8,128)(2,1)S(1)} all-to-all(bf16[32,4,64,128]{3,2,1,0:T(8,128)(2,1)S(1)} %bitcast.11), channel_id=1, replica_groups=mesh['frame'=8,'tile'=32] {'tile'}, dimensions={0} | all-to-all | bytes 4194304 | tf_op jit(solution)/shard_map/all_to_all | solution.py:330
  66.8 22.2 %spatial_attention.1 = (bf16[32,4,64,128]{3,2,1,0:T(8,128)(2,1)S(1)}, f32[2,128]{1,0:T(2,128)S(1)}) custom-call(f32[4,128]{1,0:T(4,128)S(1)} %copy-done.9, bf16[32,4,64,128]{3,2,1,0:T(8,128)(2,1)S(1)} %all_to_all.10.x_ref), custom_call_target="tpu_custom_call" | custom-call | flops 6442450944 | bytes 4194304 | tf_op jit(solution)/shard_map/spatial_attention/pallas_call | solution.py:280
  89.0 1.4 copy-done
  90.4 4.1 %all-to-all-start.1 = ((bf16[32,4,64,128]{3,2,1,0:T(8,128)(2,1)}), bf16[32,4,64,128]{3,2,1,0:T(8,128)(2,1)S(1)}, u32[]{:S(2)}, u32[]{:S(2)}) async-start(bf16[32,4,64,128]{3,2,1,0:T(8,128)(2,1)} %copy-done), calls=%async_computation.1 | async-start | bytes 4194304 | tf_op jit(solution)/shard_map/all_to_all | solution.py:337
  94.7 0.1 stack.35.at_ref
  94.7 0.0 copy-start.3
  94.8 1.0 copy-done.3
  95.8 1.0 copy-done.4
  96.8 0.8 pack_temporal.1
  97.7 1.6 collective-permute-start
  99.2 0.5 collective-permute-start.1
  99.8 2.9 %collective-permute-start.2 = (bf16[4,2,64,256]{3,2,1,0:T(8,128)(2,1)S(1)}, bf16[4,2,64,256]{3,2,1,0:T(8,128)(2,1)S(1)}, u32[]{:S(2)}, u32[]{:S(2)}) collective-permute-start(bf16[4,2,64,256]{3,2,1,0:T(8,128)(2,1)S(1)} %get-tuple-element.44), channel_id=1, source_target_pairs={{0,128},{32,160},{64,192},{96,224},{128,0},{160,32},{192,64},{224,... | collective-permute-start | bytes 786440 | tf_op jit(solution)/shard_map/ppermute | solution.py:311
  102.7 1.6 collective-permute-start.3
  104.2 2.9 %collective-permute-start.4 = (bf16[4,2,64,256]{3,2,1,0:T(8,128)(2,1)S(1)}, bf16[4,2,64,256]{3,2,1,0:T(8,128)(2,1)S(1)}, u32[]{:S(2)}, u32[]{:S(2)}) collective-permute-start(bf16[4,2,64,256]{3,2,1,0:T(8,128)(2,1)S(1)} %get-tuple-element.46), channel_id=1, source_target_pairs={{0,224},{32,128},{64,160},{96,192},{128,96},{160,0},{192,32},{224,... | collective-permute-start | bytes 786440 | tf_op jit(solution)/shard_map/ppermute | solution.py:311
  107.1 0.0 collective-permute-done.refs_1_
  107.1 2.1 collective-permute-start.5
  109.2 0.0 collective-permute-done.1.refs_2_
  109.2 3.5 %collective-permute-start.6 = (bf16[4,2,64,256]{3,2,1,0:T(8,128)(2,1)S(1)}, bf16[4,2,64,256]{3,2,1,0:T(8,128)(2,1)S(1)}, u32[]{:S(2)}, u32[]{:S(2)}) collective-permute-start(bf16[4,2,64,256]{3,2,1,0:T(8,128)(2,1)S(1)} %get-tuple-element.48), channel_id=1, source_target_pairs={{0,192},{32,224},{64,128},{96,160},{128,64},{160,96},{192,0},{224,... | collective-permute-start | bytes 786440 | tf_op jit(solution)/shard_map/ppermute | solution.py:311
  112.8 30.7 %collective-permute-done.2.refs_3_ = bf16[4,2,64,256]{3,2,1,0:T(8,128)(2,1)S(1)} collective-permute-done((bf16[4,2,64,256]{3,2,1,0:T(8,128)(2,1)S(1)}, bf16[4,2,64,256]{3,2,1,0:T(8,128)(2,1)S(1)}, u32[]{:S(2)}, u32[]{:S(2)}) %collective-permute-start.2) | collective-permute-done | bytes 262176 | tf_op jit(solution)/shard_map/ppermute | solution.py:311
  143.5 0.0 collective-permute-done.3.refs_4_
  143.5 0.0 collective-permute-done.4.refs_5_
  143.5 0.0 collective-permute-done.5.refs_6_
  143.5 0.0 collective-permute-done.6.refs_7_
  143.5 6.2 %temporal_attention.1 = (bf16[4,2,64,256]{3,2,1,0:T(8,128)(2,1)S(1)}, bf16[4,2,64,256]{3,2,1,0:T(8,128)(2,1)S(1)}, bf16[4,2,64,256]{3,2,1,0:T(8,128)(2,1)S(1)}, ...) custom-call(f32[4,128]{1,0:T(4,128)S(1)} %copy-done.9, ...), custom_call_target="tpu_custom_call" | custom-call | flops 805306368 | bytes 4194304 | tf_op jit(solution)/shard_map/temporal_attention/pallas_call | solution.py:194
  149.7 0.6 collective-permute-start.7
  150.3 1.5 collective-permute-start.8
  151.8 0.5 collective-permute-start.14
  152.3 5.5 %collective-permute-done.14 = f32[4,128]{1,0:T(4,128)S(1)} collective-permute-done((f32[4,128]{1,0:T(4,128)S(1)}, f32[4,128]{1,0:T(4,128)S(1)}, u32[]{:S(2)}, u32[]{:S(2)}) %collective-permute-start.14) | collective-permute-done | bytes 2080 | tf_op jit(solution)/shard_map/ppermute | solution.py:319
  157.9 2.6 %collective-permute-start.15 = (f32[4,128]{1,0:T(4,128)S(1)}, f32[4,128]{1,0:T(4,128)S(1)}, u32[]{:S(2)}, u32[]{:S(2)}) collective-permute-start(f32[4,128]{1,0:T(4,128)S(1)} %fusion), channel_id=1, source_target_pairs={{0,64},{32,96},{64,0},{96,32},{128,192},{160,224},{192,128},{224,1... | collective-permute-start | bytes 6152 | tf_op jit(solution)/shard_map/ppermute | solution.py:319
  160.5 2.7 %collective-permute-done.15 = f32[4,128]{1,0:T(4,128)S(1)} collective-permute-done((f32[4,128]{1,0:T(4,128)S(1)}, f32[4,128]{1,0:T(4,128)S(1)}, u32[]{:S(2)}, u32[]{:S(2)}) %collective-permute-start.15) | collective-permute-done | bytes 2080 | tf_op jit(solution)/shard_map/ppermute | solution.py:319
  163.2 2.1 collective-permute-start.16
  165.3 3.0 %collective-permute-done.16 = f32[4,128]{1,0:T(4,128)S(1)} collective-permute-done((f32[4,128]{1,0:T(4,128)S(1)}, f32[4,128]{1,0:T(4,128)S(1)}, u32[]{:S(2)}, u32[]{:S(2)}) %collective-permute-start.16) | collective-permute-done | bytes 2080 | tf_op jit(solution)/shard_map/ppermute | solution.py:319
  168.3 0.0 collective-permute-start.17
  168.3 1.2 collective-permute-done.17
  169.5 3.6 %collective-permute-start.18 = (f32[4,128]{1,0:T(4,128)S(1)}, f32[4,128]{1,0:T(4,128)S(1)}, u32[]{:S(2)}, u32[]{:S(2)}) collective-permute-start(f32[4,128]{1,0:T(4,128)S(1)} %add.128), channel_id=1, source_target_pairs={{0,2},{1,3},{2,0},{3,1},{4,6},{5,7},{6,4},{7,5},{8,10},{9,11},{10,... | collective-permute-start | bytes 6152 | tf_op jit(solution)/shard_map/ppermute | solution.py:319
  173.0 1.6 collective-permute-done.18
  174.6 0.1 collective-permute-start.19
  174.7 3.5 %collective-permute-done.19 = f32[4,128]{1,0:T(4,128)S(1)} collective-permute-done((f32[4,128]{1,0:T(4,128)S(1)}, f32[4,128]{1,0:T(4,128)S(1)}, u32[]{:S(2)}, u32[]{:S(2)}) %collective-permute-start.19) | collective-permute-done | bytes 2080 | tf_op jit(solution)/shard_map/ppermute | solution.py:319
  178.2 2.2 %collective-permute-start.20 = (f32[4,128]{1,0:T(4,128)S(1)}, f32[4,128]{1,0:T(4,128)S(1)}, u32[]{:S(2)}, u32[]{:S(2)}) collective-permute-start(f32[4,128]{1,0:T(4,128)S(1)} %add.130), channel_id=1, source_target_pairs={{0,8},{1,9},{2,10},{3,11},{4,12},{5,13},{6,14},{7,15},{8,0},{9,1},... | collective-permute-start | bytes 6152 | tf_op jit(solution)/shard_map/ppermute | solution.py:319
  180.4 2.2 %collective-permute-start.9 = (bf16[4,2,64,256]{3,2,1,0:T(8,128)(2,1)S(1)}, bf16[4,2,64,256]{3,2,1,0:T(8,128)(2,1)S(1)}, u32[]{:S(2)}, u32[]{:S(2)}) collective-permute-start(bf16[4,2,64,256]{3,2,1,0:T(8,128)(2,1)S(1)} %get-tuple-element.52), channel_id=1, source_target_pairs={{0,128},{32,160},{64,192},{96,224},{128,0},{160,32},{192,64},{224,... | collective-permute-start | bytes 786440 | tf_op jit(solution)/shard_map/ppermute | solution.py:311
  182.5 0.5 collective-permute-start.10
  183.1 0.0 collective-permute-done.7.refs_1_
  183.1 3.9 %collective-permute-start.11 = (bf16[4,2,64,256]{3,2,1,0:T(8,128)(2,1)S(1)}, bf16[4,2,64,256]{3,2,1,0:T(8,128)(2,1)S(1)}, u32[]{:S(2)}, u32[]{:S(2)}) collective-permute-start(bf16[4,2,64,256]{3,2,1,0:T(8,128)(2,1)S(1)} %get-tuple-element.54), channel_id=1, source_target_pairs={{0,160},{32,192},{64,224},{96,128},{128,32},{160,64},{192,96},{224... | collective-permute-start | bytes 786440 | tf_op jit(solution)/shard_map/ppermute | solution.py:311
  187.0 0.0 collective-permute-done.8.refs_2_
  187.0 2.6 %collective-permute-start.12 = (bf16[4,2,64,256]{3,2,1,0:T(8,128)(2,1)S(1)}, bf16[4,2,64,256]{3,2,1,0:T(8,128)(2,1)S(1)}, u32[]{:S(2)}, u32[]{:S(2)}) collective-permute-start(bf16[4,2,64,256]{3,2,1,0:T(8,128)(2,1)S(1)} %get-tuple-element.55), channel_id=1, source_target_pairs={{0,64},{32,96},{64,0},{96,32},{128,192},{160,224},{192,128},{224,1... | collective-permute-start | bytes 786440 | tf_op jit(solution)/shard_map/ppermute | solution.py:311
  189.6 0.0 collective-permute-done.20
  189.6 1.7 collective-permute-start.13
  191.3 13.7 %collective-permute-done.9.refs_3_ = bf16[4,2,64,256]{3,2,1,0:T(8,128)(2,1)S(1)} collective-permute-done((bf16[4,2,64,256]{3,2,1,0:T(8,128)(2,1)S(1)}, bf16[4,2,64,256]{3,2,1,0:T(8,128)(2,1)S(1)}, u32[]{:S(2)}, u32[]{:S(2)}) %collective-permute-start.9) | collective-permute-done | bytes 262176 | tf_op jit(solution)/shard_map/ppermute | solution.py:311
  205.0 4.7 %collective-permute-start.21 = (f32[4,128]{1,0:T(4,128)S(1)}, f32[4,128]{1,0:T(4,128)S(1)}, u32[]{:S(2)}, u32[]{:S(2)}) collective-permute-start(f32[4,128]{1,0:T(4,128)S(1)} %add.131), channel_id=1, source_target_pairs={{0,16},{1,17},{2,18},{3,19},{4,20},{5,21},{6,22},{7,23},{8,24},{9,... | collective-permute-start | bytes 6152 | tf_op jit(solution)/shard_map/ppermute | solution.py:319
  209.7 0.0 collective-permute-done.10.refs_4_
  209.7 0.0 collective-permute-done.11.refs_5_
  209.7 0.0 collective-permute-done.12.refs_6_
  209.7 0.0 collective-permute-done.13.refs_7_
  209.7 2.1 unpack_temporal.1
  211.9 0.6 collective-permute-done.21
  212.5 0.6 add.132
  213.1 0.0 all-to-all-done.1
  213.1 2.1 unpack_spatial.1
  (19 shorter events, 0.1 us)
Async XLA Ops:
  0.6 1.0 copy-start.5
  1.7 1.0 copy-start.6
  2.7 1.0 copy-start.7
  3.8 1.0 copy-start.8
  5.6 61.3 %copy-start.9 = (f32[4,128]{1,0:T(4,128)S(1)}, f32[4,128]{1,0:T(4,128)}, u32[]{:S(2)}) copy-start(f32[4,128]{1,0:T(4,128)} %gains_ref.3) | copy-start | bytes 6148
  89.0 1.4 copy-start
  90.4 4.4 %copy-start.1 = (bf16[2,64,2048]{2,1,0:T(8,128)(2,1)S(1)}, bf16[2,64,2048]{2,1,0:T(8,128)(2,1)}, u32[]{:S(2)}) copy-start(bf16[2,64,2048]{2,1,0:T(8,128)(2,1)} %q_ref.3) | copy-start | bytes 1572868
  90.4 4.4 %copy-start.2 = (bf16[2,64,2048]{2,1,0:T(8,128)(2,1)S(1)}, bf16[2,64,2048]{2,1,0:T(8,128)(2,1)}, u32[]{:S(2)}) copy-start(bf16[2,64,2048]{2,1,0:T(8,128)(2,1)} %k_ref.3) | copy-start | bytes 1572868
  90.4 122.7 %all-to-all-start.1 = ((bf16[32,4,64,128]{3,2,1,0:T(8,128)(2,1)}), bf16[32,4,64,128]{3,2,1,0:T(8,128)(2,1)S(1)}, u32[]{:S(2)}, u32[]{:S(2)}) async-start(bf16[32,4,64,128]{3,2,1,0:T(8,128)(2,1)} %copy-done), calls=%async_computation.1 | async-start | bytes 4194304 | tf_op jit(solution)/shard_map/all_to_all | solution.py:337
  94.7 1.0 copy-start.3
  95.8 1.0 copy-start.4
  97.7 9.4 %collective-permute-start = (bf16[4,2,64,256]{3,2,1,0:T(8,128)(2,1)S(1)}, bf16[4,2,64,256]{3,2,1,0:T(8,128)(2,1)S(1)}, u32[]{:S(2)}, u32[]{:S(2)}) collective-permute-start(bf16[4,2,64,256]{3,2,1,0:T(8,128)(2,1)S(1)} %get-tuple-element.42), channel_id=1, source_target_pairs={{0,32},{32,64},{64,96},{96,0},{128,160},{160,192},{192,224},{224,1... | collective-permute-start | bytes 786440 | tf_op jit(solution)/shard_map/ppermute | solution.py:311
  99.2 10.0 %collective-permute-start.1 = (bf16[4,2,64,256]{3,2,1,0:T(8,128)(2,1)S(1)}, bf16[4,2,64,256]{3,2,1,0:T(8,128)(2,1)S(1)}, u32[]{:S(2)}, u32[]{:S(2)}) collective-permute-start(bf16[4,2,64,256]{3,2,1,0:T(8,128)(2,1)S(1)} %get-tuple-element.43), channel_id=1, source_target_pairs={{0,96},{32,0},{64,32},{96,64},{128,224},{160,128},{192,160},{224,1... | collective-permute-start | bytes 786440 | tf_op jit(solution)/shard_map/ppermute | solution.py:311
  99.8 43.7 %collective-permute-start.2 = (bf16[4,2,64,256]{3,2,1,0:T(8,128)(2,1)S(1)}, bf16[4,2,64,256]{3,2,1,0:T(8,128)(2,1)S(1)}, u32[]{:S(2)}, u32[]{:S(2)}) collective-permute-start(bf16[4,2,64,256]{3,2,1,0:T(8,128)(2,1)S(1)} %get-tuple-element.44), channel_id=1, source_target_pairs={{0,128},{32,160},{64,192},{96,224},{128,0},{160,32},{192,64},{224,... | collective-permute-start | bytes 786440 | tf_op jit(solution)/shard_map/ppermute | solution.py:311
  102.7 40.8 %collective-permute-start.3 = (bf16[4,2,64,256]{3,2,1,0:T(8,128)(2,1)S(1)}, bf16[4,2,64,256]{3,2,1,0:T(8,128)(2,1)S(1)}, u32[]{:S(2)}, u32[]{:S(2)}) collective-permute-start(bf16[4,2,64,256]{3,2,1,0:T(8,128)(2,1)S(1)} %get-tuple-element.45), channel_id=1, source_target_pairs={{0,160},{32,192},{64,224},{96,128},{128,32},{160,64},{192,96},{224... | collective-permute-start | bytes 786440 | tf_op jit(solution)/shard_map/ppermute | solution.py:311
  104.2 39.3 %collective-permute-start.4 = (bf16[4,2,64,256]{3,2,1,0:T(8,128)(2,1)S(1)}, bf16[4,2,64,256]{3,2,1,0:T(8,128)(2,1)S(1)}, u32[]{:S(2)}, u32[]{:S(2)}) collective-permute-start(bf16[4,2,64,256]{3,2,1,0:T(8,128)(2,1)S(1)} %get-tuple-element.46), channel_id=1, source_target_pairs={{0,224},{32,128},{64,160},{96,192},{128,96},{160,0},{192,32},{224,... | collective-permute-start | bytes 786440 | tf_op jit(solution)/shard_map/ppermute | solution.py:311
  107.1 36.4 %collective-permute-start.5 = (bf16[4,2,64,256]{3,2,1,0:T(8,128)(2,1)S(1)}, bf16[4,2,64,256]{3,2,1,0:T(8,128)(2,1)S(1)}, u32[]{:S(2)}, u32[]{:S(2)}) collective-permute-start(bf16[4,2,64,256]{3,2,1,0:T(8,128)(2,1)S(1)} %get-tuple-element.47), channel_id=1, source_target_pairs={{0,64},{32,96},{64,0},{96,32},{128,192},{160,224},{192,128},{224,1... | collective-permute-start | bytes 786440 | tf_op jit(solution)/shard_map/ppermute | solution.py:311
  109.2 34.3 %collective-permute-start.6 = (bf16[4,2,64,256]{3,2,1,0:T(8,128)(2,1)S(1)}, bf16[4,2,64,256]{3,2,1,0:T(8,128)(2,1)S(1)}, u32[]{:S(2)}, u32[]{:S(2)}) collective-permute-start(bf16[4,2,64,256]{3,2,1,0:T(8,128)(2,1)S(1)} %get-tuple-element.48), channel_id=1, source_target_pairs={{0,192},{32,224},{64,128},{96,160},{128,64},{160,96},{192,0},{224,... | collective-permute-start | bytes 786440 | tf_op jit(solution)/shard_map/ppermute | solution.py:311
  149.7 33.3 %collective-permute-start.7 = (bf16[4,2,64,256]{3,2,1,0:T(8,128)(2,1)S(1)}, bf16[4,2,64,256]{3,2,1,0:T(8,128)(2,1)S(1)}, u32[]{:S(2)}, u32[]{:S(2)}) collective-permute-start(bf16[4,2,64,256]{3,2,1,0:T(8,128)(2,1)S(1)} %get-tuple-element.50), channel_id=1, source_target_pairs={{0,96},{32,0},{64,32},{96,64},{128,224},{160,128},{192,160},{224,1... | collective-permute-start | bytes 786440 | tf_op jit(solution)/shard_map/ppermute | solution.py:311
  150.3 36.7 %collective-permute-start.8 = (bf16[4,2,64,256]{3,2,1,0:T(8,128)(2,1)S(1)}, bf16[4,2,64,256]{3,2,1,0:T(8,128)(2,1)S(1)}, u32[]{:S(2)}, u32[]{:S(2)}) collective-permute-start(bf16[4,2,64,256]{3,2,1,0:T(8,128)(2,1)S(1)} %get-tuple-element.51), channel_id=1, source_target_pairs={{0,32},{32,64},{64,96},{96,0},{128,160},{160,192},{192,224},{224,1... | collective-permute-start | bytes 786440 | tf_op jit(solution)/shard_map/ppermute | solution.py:311
  151.8 6.0 %collective-permute-start.14 = (f32[4,128]{1,0:T(4,128)S(1)}, f32[4,128]{1,0:T(4,128)S(1)}, u32[]{:S(2)}, u32[]{:S(2)}) collective-permute-start(f32[4,128]{1,0:T(4,128)S(1)} %pad_maximum_fusion), channel_id=1, source_target_pairs={{0,32},{32,0},{64,96},{96,64},{128,160},{160,128},{192,224},{224,1... | collective-permute-start | bytes 6152 | tf_op jit(solution)/shard_map/ppermute | solution.py:319
  157.9 5.4 %collective-permute-start.15 = (f32[4,128]{1,0:T(4,128)S(1)}, f32[4,128]{1,0:T(4,128)S(1)}, u32[]{:S(2)}, u32[]{:S(2)}) collective-permute-start(f32[4,128]{1,0:T(4,128)S(1)} %fusion), channel_id=1, source_target_pairs={{0,64},{32,96},{64,0},{96,32},{128,192},{160,224},{192,128},{224,1... | collective-permute-start | bytes 6152 | tf_op jit(solution)/shard_map/ppermute | solution.py:319
  163.2 5.1 %collective-permute-start.16 = (f32[4,128]{1,0:T(4,128)S(1)}, f32[4,128]{1,0:T(4,128)S(1)}, u32[]{:S(2)}, u32[]{:S(2)}) collective-permute-start(f32[4,128]{1,0:T(4,128)S(1)} %add.126), channel_id=1, source_target_pairs={{0,128},{32,160},{64,192},{96,224},{128,0},{160,32},{192,64},{224,... | collective-permute-start | bytes 6152 | tf_op jit(solution)/shard_map/ppermute | solution.py:319
  168.3 1.2 collective-permute-start.17
  169.5 5.1 %collective-permute-start.18 = (f32[4,128]{1,0:T(4,128)S(1)}, f32[4,128]{1,0:T(4,128)S(1)}, u32[]{:S(2)}, u32[]{:S(2)}) collective-permute-start(f32[4,128]{1,0:T(4,128)S(1)} %add.128), channel_id=1, source_target_pairs={{0,2},{1,3},{2,0},{3,1},{4,6},{5,7},{6,4},{7,5},{8,10},{9,11},{10,... | collective-permute-start | bytes 6152 | tf_op jit(solution)/shard_map/ppermute | solution.py:319
  174.6 3.6 %collective-permute-start.19 = (f32[4,128]{1,0:T(4,128)S(1)}, f32[4,128]{1,0:T(4,128)S(1)}, u32[]{:S(2)}, u32[]{:S(2)}) collective-permute-start(f32[4,128]{1,0:T(4,128)S(1)} %add.129), channel_id=1, source_target_pairs={{0,4},{1,5},{2,6},{3,7},{4,0},{5,1},{6,2},{7,3},{8,12},{9,13},{10,... | collective-permute-start | bytes 6152 | tf_op jit(solution)/shard_map/ppermute | solution.py:319
  178.2 11.4 %collective-permute-start.20 = (f32[4,128]{1,0:T(4,128)S(1)}, f32[4,128]{1,0:T(4,128)S(1)}, u32[]{:S(2)}, u32[]{:S(2)}) collective-permute-start(f32[4,128]{1,0:T(4,128)S(1)} %add.130), channel_id=1, source_target_pairs={{0,8},{1,9},{2,10},{3,11},{4,12},{5,13},{6,14},{7,15},{8,0},{9,1},... | collective-permute-start | bytes 6152 | tf_op jit(solution)/shard_map/ppermute | solution.py:319
  180.4 24.6 %collective-permute-start.9 = (bf16[4,2,64,256]{3,2,1,0:T(8,128)(2,1)S(1)}, bf16[4,2,64,256]{3,2,1,0:T(8,128)(2,1)S(1)}, u32[]{:S(2)}, u32[]{:S(2)}) collective-permute-start(bf16[4,2,64,256]{3,2,1,0:T(8,128)(2,1)S(1)} %get-tuple-element.52), channel_id=1, source_target_pairs={{0,128},{32,160},{64,192},{96,224},{128,0},{160,32},{192,64},{224,... | collective-permute-start | bytes 786440 | tf_op jit(solution)/shard_map/ppermute | solution.py:311
  182.5 27.2 %collective-permute-start.10 = (bf16[4,2,64,256]{3,2,1,0:T(8,128)(2,1)S(1)}, bf16[4,2,64,256]{3,2,1,0:T(8,128)(2,1)S(1)}, u32[]{:S(2)}, u32[]{:S(2)}) collective-permute-start(bf16[4,2,64,256]{3,2,1,0:T(8,128)(2,1)S(1)} %get-tuple-element.53), channel_id=1, source_target_pairs={{0,224},{32,128},{64,160},{96,192},{128,96},{160,0},{192,32},{224,... | collective-permute-start | bytes 786440 | tf_op jit(solution)/shard_map/ppermute | solution.py:311
  183.1 26.6 %collective-permute-start.11 = (bf16[4,2,64,256]{3,2,1,0:T(8,128)(2,1)S(1)}, bf16[4,2,64,256]{3,2,1,0:T(8,128)(2,1)S(1)}, u32[]{:S(2)}, u32[]{:S(2)}) collective-permute-start(bf16[4,2,64,256]{3,2,1,0:T(8,128)(2,1)S(1)} %get-tuple-element.54), channel_id=1, source_target_pairs={{0,160},{32,192},{64,224},{96,128},{128,32},{160,64},{192,96},{224... | collective-permute-start | bytes 786440 | tf_op jit(solution)/shard_map/ppermute | solution.py:311
  187.0 22.7 %collective-permute-start.12 = (bf16[4,2,64,256]{3,2,1,0:T(8,128)(2,1)S(1)}, bf16[4,2,64,256]{3,2,1,0:T(8,128)(2,1)S(1)}, u32[]{:S(2)}, u32[]{:S(2)}) collective-permute-start(bf16[4,2,64,256]{3,2,1,0:T(8,128)(2,1)S(1)} %get-tuple-element.55), channel_id=1, source_target_pairs={{0,64},{32,96},{64,0},{96,32},{128,192},{160,224},{192,128},{224,1... | collective-permute-start | bytes 786440 | tf_op jit(solution)/shard_map/ppermute | solution.py:311
  189.6 20.1 %collective-permute-start.13 = (bf16[4,2,64,256]{3,2,1,0:T(8,128)(2,1)S(1)}, bf16[4,2,64,256]{3,2,1,0:T(8,128)(2,1)S(1)}, u32[]{:S(2)}, u32[]{:S(2)}) collective-permute-start(bf16[4,2,64,256]{3,2,1,0:T(8,128)(2,1)S(1)} %get-tuple-element.56), channel_id=1, source_target_pairs={{0,192},{32,224},{64,128},{96,160},{128,64},{160,96},{192,0},{224,... | collective-permute-start | bytes 786440 | tf_op jit(solution)/shard_map/ppermute | solution.py:311
  205.0 7.5 %collective-permute-start.21 = (f32[4,128]{1,0:T(4,128)S(1)}, f32[4,128]{1,0:T(4,128)S(1)}, u32[]{:S(2)}, u32[]{:S(2)}) collective-permute-start(f32[4,128]{1,0:T(4,128)S(1)} %add.131), channel_id=1, source_target_pairs={{0,16},{1,17},{2,18},{3,19},{4,20},{5,21},{6,22},{7,23},{8,24},{9,... | collective-permute-start | bytes 6152 | tf_op jit(solution)/shard_map/ppermute | solution.py:319
where the time goes:
time: 216 us; the launch traced here: 215 us
  waiting for transfers between devices  62.5 us (29%)
  blocking collectives  61.2 us (28%)
  starting transfers between devices  48 us (22%)
  Pallas kernels  34.1 us (16%)
  local copies, waits for them, and re-layouts  7.7 us (4%)
    all_to_all x1, blocking collectives, local(): lax.all_to_all(sent, 'tile', split_axis=0, concat_axis=0, tiled=True)  61.2 us
    ppermute x14, waiting for transfers between devices, exchange(): sent.append(lax.ppermute(part, 'frame', shift(step)))  44.5 us
    ppermute x14, starting transfers between devices, exchange(): sent.append(lax.ppermute(part, 'frame', shift(step)))  28.1 us
    pallas_call x1, Pallas kernels, spatial(): pl.pallas_call(spatial_kernel, out_shape=[jax.ShapeDtypeStruct(x.shape, B...  22.2 us
    ppermute x8, waiting for transfers between devices, total(): x = x + lax.ppermute(x, axis, [(i, i ^ bit) for i in range(size)])  18.1 us
    ppermute x8, starting transfers between devices, total(): x = x + lax.ppermute(x, axis, [(i, i ^ bit) for i in range(size)])  15.8 us
    unnamed x20, local copies, waits for them, and re-layouts  7.61 us
    pallas_call x1, Pallas kernels, temporal(): pl.pallas_call(temporal_kernel, out_shape=[jax.ShapeDtypeStruct(p.shape,...  6.17 us
  transfers between devices with their start and end apart: 23, of which 9 were waited for; matrix products, arithmetic and copies ran while one was open for 0% of the time, Pallas kernels for 4%

commit v1 on v0

--- a/solution.py
+++ b/solution.py
@@ -15,9 +15,10 @@
 BF16 = jnp.bfloat16
 F32 = jnp.float32
 SEQ = 2048
-BLOCK = 256
+BLOCK = 1024
 ONES = 16
-STEPS = ((0, 0), (0, 1), (0, 3), (1, 0), (1, 1), (1, 3), (0, 2), (1, 2))
+TEMPORAL_FLOPS = 23 * 10**9
+XSTEPS = (1, 3, 2)
 
 
 def dot(a, b, ca, cb):
@@ -56,14 +57,14 @@
 
 def pack_s(arrays):
     frames, places, width = arrays[0].shape
-    group = 4
+    group = 8
     out = pl.pallas_call(
         pack_s_kernel,
         out_shape=jax.ShapeDtypeStruct((frames, HEADS, 4, places, HEAD_DIM), BF16),
         grid=(HEADS // group,),
         in_specs=[pl.BlockSpec((frames, places, group * HEAD_DIM), lambda i: (0, 0, i))] * 4,
         out_specs=pl.BlockSpec((frames, group, 4, places, HEAD_DIM), lambda i: (0, i, 0, 0, 0)),
-        compiler_params=params(16),
+        compiler_params=params(60),
         cost_estimate=cost(0, 4 << 20),
         name="pack_spatial",
     )(*arrays)
@@ -99,54 +100,61 @@
 
 def pack_t_kernel(at_ref, q_ref, k_ref, v_ref, d_ref, *out_refs):
     width = out_refs[0].shape[-1]
-    for j, out in enumerate(out_refs):
+    slots = [ref.at[i] for ref in out_refs for i in range(ref.shape[0])]
+    for j, slot in enumerate(slots):
         lanes = lanes_of(at_ref, j, width)
         for a, ref in enumerate((q_ref, k_ref, v_ref, d_ref)):
-            out[a] = ref[:, :, lanes]
-
-
-def pack_t(at, arrays):
+            slot[a] = ref[:, :, lanes]
+
+
+def pack_t(at, arrays, sizes):
     frames, places, width = arrays[0].shape
-    part = width // len(STEPS)
+    part = width // 8
     return pl.pallas_call(
         pack_t_kernel,
-        out_shape=[jax.ShapeDtypeStruct((4, frames, places, part), BF16)] * len(STEPS),
-        in_specs=[pl.BlockSpec(memory_space=pltpu.SMEM)] + [pl.BlockSpec(memory_space=pltpu.VMEM)] * 4,
-        out_specs=[pl.BlockSpec(memory_space=pltpu.VMEM)] * len(STEPS),
-        compiler_params=params(16),
-        cost_estimate=cost(0, 4 << 20),
+        out_shape=[jax.ShapeDtypeStruct((n, 4, frames, places, part), BF16) for n in sizes],
+        grid_spec=pltpu.PrefetchScalarGridSpec(
+            num_scalar_prefetch=1,
+            grid=(frames,),
+            in_specs=[pl.BlockSpec((1, places, width // 2), lambda f, at: (f, 0, at[4]))] * 4,
+            out_specs=[pl.BlockSpec((n, 4, 1, places, part), lambda f, at: (0, 0, f, 0, 0)) for n in sizes],
+        ),
+        compiler_params=params(60),
+        cost_estimate=cost(0, 2 << 20),
         name="pack_temporal",
     )(at, *arrays)
 
 
-def unpack_t_kernel(at_ref, *refs):
-    parts, outs = refs[: len(STEPS)], refs[len(STEPS) :]
+def unpack_t_kernel(at_ref, grads_ref, *refs):
+    parts, outs, grads_out = refs[:8], refs[8:12], refs[12]
+    grads_out[...] = grads_ref[...]
     width = parts[0].shape[-1]
     for j, part in enumerate(parts):
         lanes = lanes_of(at_ref, j, width)
         for a, out in enumerate(outs):
-            out[:, :, lanes] = part[a]
-
-
-def unpack_t(at, parts):
-    _, frames, places, part = parts[0].shape
+            out[:, :, lanes] = part[0, a]
+
+
+def unpack_t(at, grads, parts):
+    _, _, frames, places, part = parts[0].shape
     return pl.pallas_call(
         unpack_t_kernel,
-        out_shape=[jax.ShapeDtypeStruct((frames, places, part * len(STEPS)), BF16)] * 4,
-        in_specs=[pl.BlockSpec(memory_space=pltpu.SMEM)]
-        + [pl.BlockSpec(memory_space=pltpu.VMEM)] * len(STEPS),
-        out_specs=[pl.BlockSpec(memory_space=pltpu.VMEM)] * 4,
+        out_shape=[jax.ShapeDtypeStruct((frames, places, part * 8), BF16)] * 4
+        + [jax.ShapeDtypeStruct(grads.shape, F32)],
+        in_specs=[pl.BlockSpec(memory_space=pltpu.SMEM)] + [pl.BlockSpec(memory_space=pltpu.VMEM)] * 9,
+        out_specs=[pl.BlockSpec(memory_space=pltpu.VMEM)] * 5,
         compiler_params=params(16),
         cost_estimate=cost(0, 4 << 20),
         name="unpack_temporal",
-    )(at, *parts)
+    )(at, grads, *parts)
 
 
 def temporal_kernel(gains_ref, *refs):
-    count = len(STEPS)
-    ins, outs, dgain_ref = refs[:count], refs[count : 2 * count], refs[2 * count]
+    ins = [ref.at[0] for ref in refs[:8]]
+    outs = [ref.at[0] for ref in refs[8:13]] + [refs[9].at[i] for i in range(1, 4)]
+    dgain_ref = refs[13]
     _, frames, places, width = ins[0].shape
-    rows = count * frames * 16
+    rows = 8 * frames * 16
     gain_q, gain_k = gains_ref[2:3, :], gains_ref[3:4, :]
     row = lax.broadcasted_iota(jnp.int32, (rows, rows), 0)
     column = lax.broadcasted_iota(jnp.int32, (rows, rows), 1)
@@ -186,24 +194,29 @@
                         ref[a, f, at, lanes] = res[first : first + 16]
         return 0
 
-    lax.fori_loop(0, places // 16, step, 0)
+    lax.fori_loop(0, places // 16, step, 0, unroll=True)
 
 
 def temporal(gains, parts):
     whole = pl.BlockSpec(memory_space=pltpu.VMEM)
+    shape = parts[0].shape
+    sizes = (1, 4, 1, 1, 1)
     res = pl.pallas_call(
         temporal_kernel,
-        out_shape=[jax.ShapeDtypeStruct(p.shape, BF16) for p in parts] + [jax.ShapeDtypeStruct((2, HEAD_DIM), F32)],
-        in_specs=[whole] * (1 + len(parts)),
-        out_specs=[whole] * (1 + len(parts)),
+        out_shape=[jax.ShapeDtypeStruct((n, *shape[1:]), BF16) for n in sizes]
+        + [jax.ShapeDtypeStruct((2, HEAD_DIM), F32)],
+        in_specs=[whole] * 9,
+        out_specs=[whole] * 6,
         compiler_params=params(24),
-        cost_estimate=cost(8 * 6 * 2 * 256 * 256 * 128, 4 << 20, 8 * 65536),
+        cost_estimate=cost(TEMPORAL_FLOPS, 4 << 20, 8 * 65536),
         name="temporal_attention",
     )(gains, *parts)
-    return res[:-1], res[-1]
-
-
-def spatial_kernel(gains_ref, x_ref, out_ref, dgain_ref, qh, kh, kh_t, v_t, expo, dscore, out_t, dp_t, dp_n, dq_t):
+    return res[0], res[1], res[2:5], res[5]
+
+
+def spatial_kernel(
+    gains_ref, grads_t_ref, x_ref, out_ref, dgain_ref, qh, kh, kh_t, v_t, expo, dscore, out_t, dp_t, dp_n, dq_t
+):
     tiles, _, places, depth = x_ref.shape
     seq = tiles * places
     per = BLOCK // places
@@ -258,7 +271,8 @@
         dgain_ref[0:1, :] += dgain
         return 0
 
-    dgain_ref[...] = jnp.zeros_like(dgain_ref)
+    dgain_ref[0:2, :] = jnp.zeros((2, depth), F32)
+    dgain_ref[2:4, :] = grads_t_ref[...]
     lax.fori_loop(0, seq // BLOCK, forward, 0)
 
     def backward(b, _):
@@ -273,14 +287,14 @@
     lax.fori_loop(0, seq // BLOCK, backward, 0)
 
 
-def spatial(gains, x):
+def spatial(gains, grads_t, x):
     tiles, _, places, depth = x.shape
     seq = tiles * places
     whole = pl.BlockSpec(memory_space=pltpu.VMEM)
     return pl.pallas_call(
         spatial_kernel,
-        out_shape=[jax.ShapeDtypeStruct(x.shape, BF16), jax.ShapeDtypeStruct((2, depth), F32)],
-        in_specs=[whole, whole],
+        out_shape=[jax.ShapeDtypeStruct(x.shape, BF16), jax.ShapeDtypeStruct((4, depth), F32)],
+        in_specs=[whole, whole, whole],
         out_specs=[whole, whole],
         scratch_shapes=[
             pltpu.VMEM((seq, depth), BF16),
@@ -294,50 +308,99 @@
             pltpu.VMEM((seq, depth), BF16),
             pltpu.VMEM((depth, BLOCK), F32),
         ],
-        compiler_params=params(40),
+        compiler_params=params(36),
         cost_estimate=cost(6 * 2 * seq * seq * depth, 4 << 20, seq * seq),
         name="spatial_attention",
-    )(gains, x)
-
-
-def shift(step):
-    return [(i, ((i // 4 + step[0]) % 2) * 4 + (i % 4 + step[1]) % 4) for i in range(8)]
-
-
-def exchange(parts, back):
-    sent = [parts[0]]
-    for part, step in zip(parts[1:], STEPS[1:]):
-        step = tuple(-s for s in step) if back else step
-        sent.append(lax.ppermute(part, "frame", shift(step)))
-    return sent
-
-
-def total(x):
-    for axis, size in (("frame", 8), ("tile", 32)):
-        bit = 1
-        while bit < size:
-            x = x + lax.ppermute(x, axis, [(i, i ^ bit) for i in range(size)])
-            bit *= 2
+    )(gains, grads_t, x)
+
+
+def after_kernel(x_ref, *refs):
+    pass
+
+
+def after(x, others):
+    anywhere = pl.BlockSpec(memory_space=pl.ANY)
+    return pl.pallas_call(
+        after_kernel,
+        out_shape=jax.ShapeDtypeStruct(x.shape, x.dtype),
+        in_specs=[anywhere] * (1 + len(others)),
+        out_specs=anywhere,
+        input_output_aliases={0: 0},
+        compiler_params=params(1),
+        cost_estimate=cost(0, 1024),
+        name="after",
+    )(x, *others)
+
+
+def over_tile(x):
+    count, arrays, places, depth = x.shape
+    x = x.reshape(count, arrays * places, depth)
+    return lax.all_to_all(x, "tile", split_axis=0, concat_axis=0, tiled=True).reshape(count, arrays, places, depth)
+
+
+def along_x(x, step):
+    return lax.ppermute(x, "frame", [(i, i // 4 * 4 + (i + step) % 4) for i in range(8)])
+
+
+def across(x):
+    return lax.ppermute(x, "frame", [(i, (i + 4) % 8) for i in range(8)])
+
+
+def from_partner(x, axis, bit):
+    size = 8 if axis == "frame" else 32
+    return lax.ppermute(x, axis, [(i, i ^ bit) for i in range(size)])
+
+
+def total_off_z(x):
+    for axis, bit in (("frame", 1), ("frame", 2), ("frame", 4), ("tile", 1), ("tile", 2)):
+        x = x + from_partner(x, axis, bit)
     return x
+
+
+def total_z(x):
+    got = []
+    for near, far in ((None, 4), (1, 5), (2, 6), (3, 7)):
+        perm = [(i, i ^ (4 * far)) for i in range(1, 32, 2)]
+        if near is not None:
+            perm += [(i, i ^ (4 * near)) for i in range(0, 32, 2)]
+        got.append(lax.ppermute(x, "tile", perm))
+    got[0] = jnp.where(lax.axis_index("tile") % 2 == 0, x, got[0])
+    half = (got[0] + got[1]) + (got[2] + got[3])
+    return half + from_partner(half, "tile", 1)
 
 
 def local(query_s, key_s, value_s, grad_out_s, query_t, key_t, value_t, grad_out_t, gains):
     frames = query_s.shape[0]
     me = lax.axis_index("frame")
-    at = jnp.stack([((me // 4 + dy) % 2) * 4 + (me % 4 + dx) % 4 for dy, dx in STEPS]).astype(jnp.int32)
-
+    row, x = me // 4, me % 4
+    order = (0, *XSTEPS)
+    places = [(x + step) % 4 for step in order]
+    at_here = jnp.stack(places + [row]).astype(jnp.int32)
+    at_there = jnp.stack(places + [1 - row]).astype(jnp.int32)
+    at_all = jnp.stack([4 * row + p for p in places] + [4 * (1 - row) + p for p in places]).astype(jnp.int32)
+    given_t = (query_t, key_t, value_t, grad_out_t)
+
+    (there,) = pack_t(at_there, given_t, (4,))
+    there = across(there)
     sent = pack_s((query_s, key_s, value_s, grad_out_s))
-    items = lax.all_to_all(sent, "tile", split_axis=0, concat_axis=0, tiled=True)
-
-    parts = exchange(pack_t(at, (query_t, key_t, value_t, grad_out_t)), False)
-    parts, grads_t = temporal(gains, parts)
-    outs_t = unpack_t(at, exchange(parts, True))
-
-    res, grads_s = spatial(gains, items)
-    home = lax.all_to_all(res, "tile", split_axis=0, concat_axis=0, tiled=True)
+    items = over_tile(sent)
+    here = pack_t(at_here, given_t, (1, 1, 1, 1))
+    parts = [here[0], there]
+    for i, step in enumerate(XSTEPS):
+        parts.append(along_x(here[i + 1], step))
+    for i, step in enumerate(XSTEPS):
+        parts.append(along_x(there[i + 1 : i + 2], step))
+
+    own, there, here, grads_t = temporal(gains, parts)
+    there = across(there)
+    here = [along_x(part, -step) for part, step in zip(here, XSTEPS)]
+    there_x = [along_x(there[i + 1 : i + 2], -step) for i, step in enumerate(XSTEPS)]
+
+    res, grads = spatial(gains, grads_t, items)
+    home = over_tile(after(res, [there, *here]))
+    *outs_t, grads = unpack_t(at_all, total_off_z(grads), [own, *here, there, *there_x])
+    gain_grads = total_z(grads)
     outs_s = unpack_s(home, frames)
-
-    gain_grads = total(jnp.concatenate([grads_s, grads_t], axis=0))
     return (*outs_s, *outs_t, gain_grads)
 
 

time: 216 us -> 154 us (0.71)
  blocking collectives: 61.2 us -> 0 us
  waiting for transfers between devices: 62.5 us -> 51.4 us
  starting transfers between devices: 48 us -> 58.4 us
  local copies, waits for them, and re-layouts: 7.7 us -> 4.84 us
    all_to_all x1 -> x0, blocking collectives: 61.2 us -> none  [local(): lax.all_to_all(sent, 'tile', split_axis=0, concat_axis=0, tiled=True)]
    all_to_all x1 -> x2, starting transfers between devices: 4.14 us -> 20.3 us  [over_tile(): lax.all_to_all(x, 'tile', split_axis=0, concat_axis=0, tiled=True)]
    ppermute x22 -> x24, waiting for transfers between devices: 62.5 us -> 51.4 us  [the longest x6 20.6 us: from_partner(): return lax.ppermute(x, axis, [(i, i ^ bit) for i in range(size)])]
    pallas_call x1, Pallas kernels: 22.2 us -> 15.1 us  [spatial(): pl.pallas_call(spatial_kernel, out_shape=[jax.ShapeDtypeStruct(x.shape, B...]
    ppermute x22 -> x24, starting transfers between devices: 43.9 us -> 38.2 us  [the longest x12 17.9 us: along_x(): lax.ppermute(x, 'frame', [(i, i // 4 * 4 + (i + step) % 4) for i in range...]
    pallas_call x2 -> x4, Pallas kernels: 7 us -> 12.4 us  [the longest x1 6.7 us: temporal(): pl.pallas_call(temporal_kernel, out_shape=[jax.ShapeDtypeStruct((n, *shap...]
    unnamed x20 -> x8, local copies, waits for them, and re-layouts: 7.61 us -> 2.6 us
  transfers between devices with their start and end apart: 23 -> 26, of which waited for: 9 -> 12; matrix products, arithmetic and copies ran while one was open for 0% -> 1% of each run, Pallas kernels for 4% -> 20%
where the time goes in v1:
time: 154 us; the launch traced here: 151 us
  starting transfers between devices  58.4 us (38%)
  waiting for transfers between devices  51.4 us (33%)
  Pallas kernels  35.2 us (23%)
  local copies, waits for them, and re-layouts  4.84 us (3%)
    ppermute x6, waiting for transfers between devices, from_partner(): return lax.ppermute(x, axis, [(i, i ^ bit) for i in range(size)])  20.6 us
    all_to_all x2, starting transfers between devices, over_tile(): lax.all_to_all(x, 'tile', split_axis=0, concat_axis=0, tiled=True)  20.3 us
    ppermute x12, starting transfers between devices, along_x(): lax.ppermute(x, 'frame', [(i, i // 4 * 4 + (i + step) % 4) for i in range...  17.9 us
    pallas_call x1, Pallas kernels, spatial(): pl.pallas_call(spatial_kernel, out_shape=[jax.ShapeDtypeStruct(x.shape, B...  15.1 us
    ppermute x2, waiting for transfers between devices, across(): return lax.ppermute(x, 'frame', [(i, (i + 4) % 8) for i in range(8)])  14.6 us
    ppermute x6, starting transfers between devices, from_partner(): return lax.ppermute(x, axis, [(i, i ^ bit) for i in range(size)])  8.91 us
    ppermute x4, waiting for transfers between devices, total_z(): got.append(lax.ppermute(x, 'tile', perm))  8.43 us
    ppermute x12, waiting for transfers between devices, along_x(): lax.ppermute(x, 'frame', [(i, i // 4 * 4 + (i + step) % 4) for i in range...  7.71 us
  transfers between devices with their start and end apart: 26, of which 12 were waited for; matrix products, arithmetic and copies ran while one was open for 1% of the time, Pallas kernels for 20%

profile of v1, /device:TPU:2, one launch (start us, length us, event | category | flops | bytes accessed | tf_op | source)
XLA Modules:
  0.0 151.3 jit_solution(9601728223659233194)
XLA Ops:
  0.7 0.6 stack.62.at_ref
  1.3 2.9 %pack_temporal.3 = bf16[4,4,2,64,256]{4,3,2,1,0:T(8,128)(2,1)} custom-call(s32[5]{0:T(128)} %stack.62.at_ref, bf16[2,64,2048]{2,1,0:T(8,128)(2,1)} %q_ref.4, bf16[2,64,2048]{2,1,0:T(8,128)(2,1)} %k_ref.4, bf16[2,64,2048]{2,1,0:T(8,128)(2,1)} %v_ref.4, bf16[2,64,2048]{2,1,0:T(8,128)(2,1)} %d_ref.4), custom_call_target="tpu_custom_call" | custom-call | bytes 2097152 | tf_op jit(solution)/shard_map/pack_temporal/pallas_call | solution.py:113
  4.2 3.2 %collective-permute-start = (bf16[4,4,2,64,256]{4,3,2,1,0:T(8,128)(2,1)}, bf16[4,4,2,64,256]{4,3,2,1,0:T(8,128)(2,1)S(1)}, u32[]{:S(2)}, u32[]{:S(2)}) collective-permute-start(bf16[4,4,2,64,256]{4,3,2,1,0:T(8,128)(2,1)} %pack_temporal.3), channel_id=1, source_target_pairs={{0,128},{32,160},{64,192},{96,224},{128,0},{160,32},{192,64},{224,... | collective-permute-start | bytes 3145736 | tf_op jit(solution)/shard_map/ppermute | solution.py:346
  7.4 2.7 %pack_spatial.1 = bf16[2,16,4,64,128]{4,3,2,1,0:T(8,128)(2,1)} custom-call(bf16[2,64,2048]{2,1,0:T(8,128)(2,1)} %q_ref.5, bf16[2,64,2048]{2,1,0:T(8,128)(2,1)} %k_ref.5, bf16[2,64,2048]{2,1,0:T(8,128)(2,1)} %v_ref.5, bf16[2,64,2048]{2,1,0:T(8,128)(2,1)} %d_ref.5), custom_call_target="tpu_custom_call" | custom-call | bytes 4194304 | tf_op jit(solution)/shard_map/pack_spatial/pallas_call | solution.py:61
  10.1 9.0 %all-to-all-start = ((bf16[32,256,128]{2,1,0:T(8,128)(2,1)}), bf16[32,256,128]{2,1,0:T(8,128)(2,1)S(1)}, u32[]{:S(2)}, u32[]{:S(2)}) async-start(bf16[32,256,128]{2,1,0:T(8,128)(2,1)} %bitcast.20), calls=%async_computation | async-start | bytes 4194304 | tf_op jit(solution)/shard_map/all_to_all | solution.py:338
  19.1 0.0 copy-start.3
  19.1 0.6 stack.60.at_ref
  19.7 2.8 %pack_temporal.2 = (bf16[1,4,2,64,256]{4,3,2,1,0:T(8,128)(2,1)}, bf16[1,4,2,64,256]{4,3,2,1,0:T(8,128)(2,1)}, bf16[1,4,2,64,256]{4,3,2,1,0:T(8,128)(2,1)}, bf16[1,4,2,64,256]{4,3,2,1,0:T(8,128)(2,1)}) custom-call(s32[5]{0:T(128)} %stack.60.at_ref, bf16[2,64,2048]{2,1,0:T(8,128)(2,1)} %q_ref.4, bf16[2,64,2048]{2,1,0:T(8,128)(2,1)} %k_ref.4, ...), custom_call_target="tpu_custom_call" | custom-call | bytes 2097152 | tf_op jit(solution)/shard_map/pack_temporal/pallas_call | solution.py:113
  22.6 1.5 collective-permute-start.1
  24.1 0.5 collective-permute-start.2
  24.6 2.1 %collective-permute-start.3 = (bf16[1,4,2,64,256]{4,3,2,1,0:T(8,128)(2,1)}, bf16[1,4,2,64,256]{4,3,2,1,0:T(8,128)(2,1)S(1)}, u32[]{:S(2)}, u32[]{:S(2)}) collective-permute-start(bf16[1,4,2,64,256]{4,3,2,1,0:T(8,128)(2,1)} %get-tuple-element.33), channel_id=1, source_target_pairs={{0,64},{32,96},{64,0},{96,32},{128,192},{160,224},{192,128},{224,1... | collective-permute-start | bytes 786440 | tf_op jit(solution)/shard_map/ppermute | solution.py:342
  26.7 14.6 %collective-permute-done.refs_1_ = bf16[4,4,2,64,256]{4,3,2,1,0:T(8,128)(2,1)S(1)} collective-permute-done((bf16[4,4,2,64,256]{4,3,2,1,0:T(8,128)(2,1)}, bf16[4,4,2,64,256]{4,3,2,1,0:T(8,128)(2,1)S(1)}, u32[]{:S(2)}, u32[]{:S(2)}) %collective-permute-start) | collective-permute-done | bytes 1048608 | tf_op jit(solution)/shard_map/ppermute | solution.py:346
  41.3 0.1 fusion.1
  41.4 1.6 %collective-permute-start.4 = (bf16[1,4,2,64,256]{4,3,2,1,0:T(8,128)(2,1)S(1)}, bf16[1,4,2,64,256]{4,3,2,1,0:T(8,128)(2,1)S(1)}, u32[]{:S(2)}, u32[]{:S(2)}) collective-permute-start(bf16[1,4,2,64,256]{4,3,2,1,0:T(8,128)(2,1)S(1)} %get-tuple-element.56), channel_id=1, source_target_pairs={{0,32},{32,64},{64,96},{96,0},{128,160},{160,192},{192,224},{224,1... | collective-permute-start | bytes 786440 | tf_op jit(solution)/shard_map/ppermute | solution.py:342
  42.9 0.5 collective-permute-start.5
  43.5 0.0 collective-permute-done.1.refs_2_
  43.5 2.1 %collective-permute-start.6 = (bf16[1,4,2,64,256]{4,3,2,1,0:T(8,128)(2,1)S(1)}, bf16[1,4,2,64,256]{4,3,2,1,0:T(8,128)(2,1)S(1)}, u32[]{:S(2)}, u32[]{:S(2)}) collective-permute-start(bf16[1,4,2,64,256]{4,3,2,1,0:T(8,128)(2,1)S(1)} %get-tuple-element.54), channel_id=1, source_target_pairs={{0,64},{32,96},{64,0},{96,32},{128,192},{160,224},{192,128},{224,1... | collective-permute-start | bytes 786440 | tf_op jit(solution)/shard_map/ppermute | solution.py:342
  45.6 0.0 collective-permute-done.2.refs_3_
  45.6 0.0 collective-permute-done.3.refs_4_
  45.6 3.2 %collective-permute-done.4.refs_5_ = bf16[1,4,2,64,256]{4,3,2,1,0:T(8,128)(2,1)S(1)} collective-permute-done((bf16[1,4,2,64,256]{4,3,2,1,0:T(8,128)(2,1)S(1)}, bf16[1,4,2,64,256]{4,3,2,1,0:T(8,128)(2,1)S(1)}, u32[]{:S(2)}, u32[]{:S(2)}) %collective-permute-start.4) | collective-permute-done | bytes 262176 | tf_op jit(solution)/shard_map/ppermute | solution.py:342
  48.8 1.7 %collective-permute-done.5.refs_6_ = bf16[1,4,2,64,256]{4,3,2,1,0:T(8,128)(2,1)S(1)} collective-permute-done((bf16[1,4,2,64,256]{4,3,2,1,0:T(8,128)(2,1)S(1)}, bf16[1,4,2,64,256]{4,3,2,1,0:T(8,128)(2,1)S(1)}, u32[]{:S(2)}, u32[]{:S(2)}) %collective-permute-start.5) | collective-permute-done | bytes 262176 | tf_op jit(solution)/shard_map/ppermute | solution.py:342
  50.5 2.8 %collective-permute-done.6.refs_7_ = bf16[1,4,2,64,256]{4,3,2,1,0:T(8,128)(2,1)S(1)} collective-permute-done((bf16[1,4,2,64,256]{4,3,2,1,0:T(8,128)(2,1)S(1)}, bf16[1,4,2,64,256]{4,3,2,1,0:T(8,128)(2,1)S(1)}, u32[]{:S(2)}, u32[]{:S(2)}) %collective-permute-start.6) | collective-permute-done | bytes 262176 | tf_op jit(solution)/shard_map/ppermute | solution.py:342
  53.3 0.9 copy-done.2
  54.3 6.7 %temporal_attention.1 = (bf16[1,4,2,64,256]{4,3,2,1,0:T(8,128)(2,1)S(1)}, bf16[4,4,2,64,256]{4,3,2,1,0:T(8,128)(2,1)}, bf16[1,4,2,64,256]{4,3,2,1,0:T(8,128)(2,1...) custom-call(f32[4,128]{1,0:T(4,128)S(1)} %copy-done.3, ...), custom_call_target="tpu_custom_call" | custom-call | flops 23000000512 | bytes 4194304 | tf_op jit(solution)/shard_map/temporal_attention/pallas_call | solution.py:204
  61.0 0.7 copy-done
  61.7 3.5 %collective-permute-start.7 = (bf16[4,4,2,64,256]{4,3,2,1,0:T(8,128)(2,1)}, bf16[4,4,2,64,256]{4,3,2,1,0:T(8,128)(2,1)S(1)}, u32[]{:S(2)}, u32[]{:S(2)}) collective-permute-start(bf16[4,4,2,64,256]{4,3,2,1,0:T(8,128)(2,1)} %get-tuple-element.36), channel_id=1, source_target_pairs={{0,128},{32,160},{64,192},{96,224},{128,0},{160,32},{192,64},{224,... | collective-permute-start | bytes 3145736 | tf_op jit(solution)/shard_map/ppermute | solution.py:346
  65.1 0.6 collective-permute-start.8
  65.7 1.4 collective-permute-start.9
  67.2 2.9 %collective-permute-start.10 = (bf16[1,4,2,64,256]{4,3,2,1,0:T(8,128)(2,1)}, bf16[1,4,2,64,256]{4,3,2,1,0:T(8,128)(2,1)}, u32[]{:S(2)}, u32[]{:S(2)}) collective-permute-start(bf16[1,4,2,64,256]{4,3,2,1,0:T(8,128)(2,1)} %get-tuple-element.39), channel_id=1, source_target_pairs={{0,64},{32,96},{64,0},{96,32},{128,192},{160,224},{192,128},{224,1... | collective-permute-start | bytes 786440 | tf_op jit(solution)/shard_map/ppermute | solution.py:342
  70.1 15.1 %spatial_attention.1 = (bf16[32,4,64,128]{3,2,1,0:T(8,128)(2,1)}, f32[4,128]{1,0:T(4,128)S(1)}) custom-call(f32[4,128]{1,0:T(4,128)S(1)} %copy-done.3, f32[2,128]{1,0:T(2,128)S(1)} %get-tuple-element.34.grads_t_ref, bf16[32,4,64,128]{3,2,1,0:T(8,128)(2,1)S(1)} %bitcast.19), custom_call_target="tpu_custom_call" | custom-call | flops 6442450944 | bytes 4194304 | tf_op jit(solution)/shard_map/spatial_attention/pallas_call | solution.py:294
  85.2 0.0 collective-permute-done.8.refs_1_
  85.2 0.0 collective-permute-done.7.refs_0_.refs_4_
  85.2 11.3 %all-to-all-start.1 = ((bf16[32,256,128]{2,1,0:T(8,128)(2,1)}), bf16[32,256,128]{2,1,0:T(8,128)(2,1)S(1)}, u32[]{:S(2)}, u32[]{:S(2)}) async-start(bf16[32,256,128]{2,1,0:T(8,128)(2,1)} %bitcast.8), calls=%async_computation.1 | async-start | bytes 4194304 | tf_op jit(solution)/shard_map/all_to_all | solution.py:338
  96.5 0.9 fusion
  97.4 1.1 collective-permute-start.16
  98.5 0.9 collective-permute-start.17
  99.5 2.5 %collective-permute-start.18 = (bf16[1,4,2,64,256]{4,3,2,1,0:T(8,128)(2,1)}, bf16[1,4,2,64,256]{4,3,2,1,0:T(8,128)(2,1)}, u32[]{:S(2)}, u32[]{:S(2)}) collective-permute-start(bf16[1,4,2,64,256]{4,3,2,1,0:T(8,128)(2,1)} %get-tuple-element.51), channel_id=1, source_target_pairs={{0,64},{32,96},{64,0},{96,32},{128,192},{160,224},{192,128},{224,1... | collective-permute-start | bytes 786440 | tf_op jit(solution)/shard_map/ppermute | solution.py:342
  102.0 0.0 collective-permute-start.11
  102.0 10.6 %collective-permute-done.11 = f32[4,128]{1,0:T(4,128)S(1)} collective-permute-done((f32[4,128]{1,0:T(4,128)S(1)}, f32[4,128]{1,0:T(4,128)S(1)}, u32[]{:S(2)}, u32[]{:S(2)}) %collective-permute-start.11) | collective-permute-done | bytes 2080 | tf_op jit(solution)/shard_map/ppermute | solution.py:351
  112.6 0.7 collective-permute-start.12
  113.3 4.4 %collective-permute-done.12 = f32[4,128]{1,0:T(4,128)S(1)} collective-permute-done((f32[4,128]{1,0:T(4,128)S(1)}, f32[4,128]{1,0:T(4,128)S(1)}, u32[]{:S(2)}, u32[]{:S(2)}) %collective-permute-start.12) | collective-permute-done | bytes 2080 | tf_op jit(solution)/shard_map/ppermute | solution.py:351
  117.7 3.2 %collective-permute-start.13 = (f32[4,128]{1,0:T(4,128)S(1)}, f32[4,128]{1,0:T(4,128)S(1)}, u32[]{:S(2)}, u32[]{:S(2)}) collective-permute-start(f32[4,128]{1,0:T(4,128)S(1)} %add.97), channel_id=1, source_target_pairs={{0,128},{32,160},{64,192},{96,224},{128,0},{160,32},{192,64},{224,... | collective-permute-start | bytes 6152 | tf_op jit(solution)/shard_map/ppermute | solution.py:351
  121.0 1.8 %collective-permute-done.13 = f32[4,128]{1,0:T(4,128)S(1)} collective-permute-done((f32[4,128]{1,0:T(4,128)S(1)}, f32[4,128]{1,0:T(4,128)S(1)}, u32[]{:S(2)}, u32[]{:S(2)}) %collective-permute-start.13) | collective-permute-done | bytes 2080 | tf_op jit(solution)/shard_map/ppermute | solution.py:351
  122.8 0.0 collective-permute-start.14
  122.8 1.2 collective-permute-done.14
  124.0 1.7 %collective-permute-start.15 = (f32[4,128]{1,0:T(4,128)S(1)}, f32[4,128]{1,0:T(4,128)S(1)}, u32[]{:S(2)}, u32[]{:S(2)}) collective-permute-start(f32[4,128]{1,0:T(4,128)S(1)} %add.99), channel_id=1, source_target_pairs={{0,2},{1,3},{2,0},{3,1},{4,6},{5,7},{6,4},{7,5},{8,10},{9,11},{10,... | collective-permute-start | bytes 6152 | tf_op jit(solution)/shard_map/ppermute | solution.py:351
  125.6 0.1 stack.71.at_ref
  125.7 1.8 %collective-permute-done.15 = f32[4,128]{1,0:T(4,128)S(1)} collective-permute-done((f32[4,128]{1,0:T(4,128)S(1)}, f32[4,128]{1,0:T(4,128)S(1)}, u32[]{:S(2)}, u32[]{:S(2)}) %collective-permute-start.15) | collective-permute-done | bytes 2080 | tf_op jit(solution)/shard_map/ppermute | solution.py:351
  127.6 0.0 collective-permute-done.16.refs_5_
  127.6 0.0 collective-permute-done.17.refs_6_
  127.6 0.0 collective-permute-done.18.refs_7_
  127.6 0.0 copy-start.1
  127.6 0.9 copy-done.1
  128.5 2.8 %unpack_temporal.1 = (bf16[2,64,2048]{2,1,0:T(8,128)(2,1)}, bf16[2,64,2048]{2,1,0:T(8,128)(2,1)}, bf16[2,64,2048]{2,1,0:T(8,128)(2,1)}, bf16[2,64,2048]{2,1,0:T(8,128)(2,1)}, f32[4,128]{1,0:T(4,128)S(1)}) custom-call(s32[8]{0:T(128)S(1)} %stack.71.at_ref, f32[4,128]{1,0:T(4,128)S(1)} %add.100.grads_ref, bf16[1,4,2,64,256]{4,3,2,1,0:T(8,128)(2,1)S(1)} %copy-done.1, ...), custom_call_target="tpu_custom_call" | custom-call | bytes 4194304 | tf_op jit(solution)/shard_map/unpack_temporal/pallas_call | solution.py:140
  131.4 2.6 %collective-permute-start.21 = (f32[4,128]{1,0:T(4,128)S(1)}, f32[4,128]{1,0:T(4,128)S(1)}, u32[]{:S(2)}, u32[]{:S(2)}) collective-permute-start(f32[4,128]{1,0:T(4,128)S(1)} %get-tuple-element.50), channel_id=1, source_target_pairs={{1,25},{3,27},{5,29},{7,31},{9,17},{11,19},{13,21},{15,23},{17,9},... | collective-permute-start | bytes 6152 | tf_op jit(solution)/shard_map/ppermute | solution.py:366
  134.0 1.4 collective-permute-start.22
  135.4 0.0 collective-permute-start.20
  135.4 0.6 collective-permute-start.19
  136.1 6.8 %collective-permute-done.21 = f32[4,128]{1,0:T(4,128)S(1)} collective-permute-done((f32[4,128]{1,0:T(4,128)S(1)}, f32[4,128]{1,0:T(4,128)S(1)}, u32[]{:S(2)}, u32[]{:S(2)}) %collective-permute-start.21) | collective-permute-done | bytes 2080 | tf_op jit(solution)/shard_map/ppermute | solution.py:366
  142.9 1.6 %collective-permute-done.20 = f32[4,128]{1,0:T(4,128)S(1)} collective-permute-done((f32[4,128]{1,0:T(4,128)S(1)}, f32[4,128]{1,0:T(4,128)S(1)}, u32[]{:S(2)}, u32[]{:S(2)}) %collective-permute-start.20) | collective-permute-done | bytes 2080 | tf_op jit(solution)/shard_map/ppermute | solution.py:366
  144.5 3.3 %collective-permute-start.23 = (f32[4,128]{1,0:T(4,128)S(1)}, f32[4,128]{1,0:T(4,128)S(1)}, u32[]{:S(2)}, u32[]{:S(2)}) collective-permute-start(f32[4,128]{1,0:T(4,128)S(1)} %add_add_fusion), channel_id=1, source_target_pairs={{0,1},{1,0},{2,3},{3,2},{4,5},{5,4},{6,7},{7,6},{8,9},{9,8},{10,11... | collective-permute-start | bytes 6152 | tf_op jit(solution)/shard_map/ppermute | solution.py:351
  147.8 0.8 collective-permute-done.23
  148.7 0.6 add.105
  149.2 2.1 %unpack_spatial.1 = (bf16[2,64,2048]{2,1,0:T(8,128)(2,1)}, bf16[2,64,2048]{2,1,0:T(8,128)(2,1)}, bf16[2,64,2048]{2,1,0:T(8,128)(2,1)}, bf16[2,64,2048]{2,1,0:T(8,128)(2,1)}) custom-call(bf16[2,16,4,64,128]{4,3,2,1,0:T(8,128)(2,1)S(1)} %bitcast.18), custom_call_target="tpu_custom_call" | custom-call | bytes 4194304 | tf_op jit(solution)/shard_map/unpack_spatial/pallas_call | solution.py:85
  (16 shorter events, 0.0 us)
Async XLA Ops:
  4.2 37.1 %collective-permute-start = (bf16[4,4,2,64,256]{4,3,2,1,0:T(8,128)(2,1)}, bf16[4,4,2,64,256]{4,3,2,1,0:T(8,128)(2,1)S(1)}, u32[]{:S(2)}, u32[]{:S(2)}) collective-permute-start(bf16[4,4,2,64,256]{4,3,2,1,0:T(8,128)(2,1)} %pack_temporal.3), channel_id=1, source_target_pairs={{0,128},{32,160},{64,192},{96,224},{128,0},{160,32},{192,64},{224,... | collective-permute-start | bytes 3145736 | tf_op jit(solution)/shard_map/ppermute | solution.py:346
  10.1 59.9 %all-to-all-start = ((bf16[32,256,128]{2,1,0:T(8,128)(2,1)}), bf16[32,256,128]{2,1,0:T(8,128)(2,1)S(1)}, u32[]{:S(2)}, u32[]{:S(2)}) async-start(bf16[32,256,128]{2,1,0:T(8,128)(2,1)} %bitcast.20), calls=%async_computation | async-start | bytes 4194304 | tf_op jit(solution)/shard_map/all_to_all | solution.py:338
  19.1 34.2 %copy-start.3 = (f32[4,128]{1,0:T(4,128)S(1)}, f32[4,128]{1,0:T(4,128)}, u32[]{:S(2)}) copy-start(f32[4,128]{1,0:T(4,128)} %gains_ref.3) | copy-start | bytes 6148
  22.6 20.9 %collective-permute-start.1 = (bf16[1,4,2,64,256]{4,3,2,1,0:T(8,128)(2,1)}, bf16[1,4,2,64,256]{4,3,2,1,0:T(8,128)(2,1)S(1)}, u32[]{:S(2)}, u32[]{:S(2)}) collective-permute-start(bf16[1,4,2,64,256]{4,3,2,1,0:T(8,128)(2,1)} %get-tuple-element.31), channel_id=1, source_target_pairs={{0,32},{32,64},{64,96},{96,0},{128,160},{160,192},{192,224},{224,1... | collective-permute-start | bytes 786440 | tf_op jit(solution)/shard_map/ppermute | solution.py:342
  24.1 21.6 %collective-permute-start.2 = (bf16[1,4,2,64,256]{4,3,2,1,0:T(8,128)(2,1)}, bf16[1,4,2,64,256]{4,3,2,1,0:T(8,128)(2,1)S(1)}, u32[]{:S(2)}, u32[]{:S(2)}) collective-permute-start(bf16[1,4,2,64,256]{4,3,2,1,0:T(8,128)(2,1)} %get-tuple-element.32), channel_id=1, source_target_pairs={{0,96},{32,0},{64,32},{96,64},{128,224},{160,128},{192,160},{224,1... | collective-permute-start | bytes 786440 | tf_op jit(solution)/shard_map/ppermute | solution.py:342
  24.6 21.0 %collective-permute-start.3 = (bf16[1,4,2,64,256]{4,3,2,1,0:T(8,128)(2,1)}, bf16[1,4,2,64,256]{4,3,2,1,0:T(8,128)(2,1)S(1)}, u32[]{:S(2)}, u32[]{:S(2)}) collective-permute-start(bf16[1,4,2,64,256]{4,3,2,1,0:T(8,128)(2,1)} %get-tuple-element.33), channel_id=1, source_target_pairs={{0,64},{32,96},{64,0},{96,32},{128,192},{160,224},{192,128},{224,1... | collective-permute-start | bytes 786440 | tf_op jit(solution)/shard_map/ppermute | solution.py:342
  41.4 7.5 %collective-permute-start.4 = (bf16[1,4,2,64,256]{4,3,2,1,0:T(8,128)(2,1)S(1)}, bf16[1,4,2,64,256]{4,3,2,1,0:T(8,128)(2,1)S(1)}, u32[]{:S(2)}, u32[]{:S(2)}) collective-permute-start(bf16[1,4,2,64,256]{4,3,2,1,0:T(8,128)(2,1)S(1)} %get-tuple-element.56), channel_id=1, source_target_pairs={{0,32},{32,64},{64,96},{96,0},{128,160},{160,192},{192,224},{224,1... | collective-permute-start | bytes 786440 | tf_op jit(solution)/shard_map/ppermute | solution.py:342
  42.9 7.6 %collective-permute-start.5 = (bf16[1,4,2,64,256]{4,3,2,1,0:T(8,128)(2,1)S(1)}, bf16[1,4,2,64,256]{4,3,2,1,0:T(8,128)(2,1)S(1)}, u32[]{:S(2)}, u32[]{:S(2)}) collective-permute-start(bf16[1,4,2,64,256]{4,3,2,1,0:T(8,128)(2,1)S(1)} %get-tuple-element.55), channel_id=1, source_target_pairs={{0,96},{32,0},{64,32},{96,64},{128,224},{160,128},{192,160},{224,1... | collective-permute-start | bytes 786440 | tf_op jit(solution)/shard_map/ppermute | solution.py:342
  43.5 9.8 %collective-permute-start.6 = (bf16[1,4,2,64,256]{4,3,2,1,0:T(8,128)(2,1)S(1)}, bf16[1,4,2,64,256]{4,3,2,1,0:T(8,128)(2,1)S(1)}, u32[]{:S(2)}, u32[]{:S(2)}) collective-permute-start(bf16[1,4,2,64,256]{4,3,2,1,0:T(8,128)(2,1)S(1)} %get-tuple-element.54), channel_id=1, source_target_pairs={{0,64},{32,96},{64,0},{96,32},{128,192},{160,224},{192,128},{224,1... | collective-permute-start | bytes 786440 | tf_op jit(solution)/shard_map/ppermute | solution.py:342
  53.3 1.0 copy-start.2
  61.0 0.7 copy-start
  61.7 23.6 %collective-permute-start.7 = (bf16[4,4,2,64,256]{4,3,2,1,0:T(8,128)(2,1)}, bf16[4,4,2,64,256]{4,3,2,1,0:T(8,128)(2,1)S(1)}, u32[]{:S(2)}, u32[]{:S(2)}) collective-permute-start(bf16[4,4,2,64,256]{4,3,2,1,0:T(8,128)(2,1)} %get-tuple-element.36), channel_id=1, source_target_pairs={{0,128},{32,160},{64,192},{96,224},{128,0},{160,32},{192,64},{224,... | collective-permute-start | bytes 3145736 | tf_op jit(solution)/shard_map/ppermute | solution.py:346
  65.1 20.1 %collective-permute-start.8 = (bf16[1,4,2,64,256]{4,3,2,1,0:T(8,128)(2,1)}, bf16[1,4,2,64,256]{4,3,2,1,0:T(8,128)(2,1)S(1)}, u32[]{:S(2)}, u32[]{:S(2)}) collective-permute-start(bf16[1,4,2,64,256]{4,3,2,1,0:T(8,128)(2,1)} %get-tuple-element.37), channel_id=1, source_target_pairs={{0,96},{32,0},{64,32},{96,64},{128,224},{160,128},{192,160},{224,1... | collective-permute-start | bytes 786440 | tf_op jit(solution)/shard_map/ppermute | solution.py:342
  65.7 19.5 %collective-permute-start.9 = (bf16[1,4,2,64,256]{4,3,2,1,0:T(8,128)(2,1)}, bf16[1,4,2,64,256]{4,3,2,1,0:T(8,128)(2,1)}, u32[]{:S(2)}, u32[]{:S(2)}) collective-permute-start(bf16[1,4,2,64,256]{4,3,2,1,0:T(8,128)(2,1)} %get-tuple-element.38), channel_id=1, source_target_pairs={{0,32},{32,64},{64,96},{96,0},{128,160},{160,192},{192,224},{224,1... | collective-permute-start | bytes 786440 | tf_op jit(solution)/shard_map/ppermute | solution.py:342
  67.2 18.1 %collective-permute-start.10 = (bf16[1,4,2,64,256]{4,3,2,1,0:T(8,128)(2,1)}, bf16[1,4,2,64,256]{4,3,2,1,0:T(8,128)(2,1)}, u32[]{:S(2)}, u32[]{:S(2)}) collective-permute-start(bf16[1,4,2,64,256]{4,3,2,1,0:T(8,128)(2,1)} %get-tuple-element.39), channel_id=1, source_target_pairs={{0,64},{32,96},{64,0},{96,32},{128,192},{160,224},{192,128},{224,1... | collective-permute-start | bytes 786440 | tf_op jit(solution)/shard_map/ppermute | solution.py:342
  85.2 64.0 %all-to-all-start.1 = ((bf16[32,256,128]{2,1,0:T(8,128)(2,1)}), bf16[32,256,128]{2,1,0:T(8,128)(2,1)S(1)}, u32[]{:S(2)}, u32[]{:S(2)}) async-start(bf16[32,256,128]{2,1,0:T(8,128)(2,1)} %bitcast.8), calls=%async_computation.1 | async-start | bytes 4194304 | tf_op jit(solution)/shard_map/all_to_all | solution.py:338
  97.4 30.1 %collective-permute-start.16 = (bf16[1,4,2,64,256]{4,3,2,1,0:T(8,128)(2,1)}, bf16[1,4,2,64,256]{4,3,2,1,0:T(8,128)(2,1)}, u32[]{:S(2)}, u32[]{:S(2)}) collective-permute-start(bf16[1,4,2,64,256]{4,3,2,1,0:T(8,128)(2,1)} %get-tuple-element.53), channel_id=1, source_target_pairs={{0,96},{32,0},{64,32},{96,64},{128,224},{160,128},{192,160},{224,1... | collective-permute-start | bytes 786440 | tf_op jit(solution)/shard_map/ppermute | solution.py:342
  98.5 29.0 %collective-permute-start.17 = (bf16[1,4,2,64,256]{4,3,2,1,0:T(8,128)(2,1)}, bf16[1,4,2,64,256]{4,3,2,1,0:T(8,128)(2,1)}, u32[]{:S(2)}, u32[]{:S(2)}) collective-permute-start(bf16[1,4,2,64,256]{4,3,2,1,0:T(8,128)(2,1)} %get-tuple-element.52), channel_id=1, source_target_pairs={{0,32},{32,64},{64,96},{96,0},{128,160},{160,192},{192,224},{224,1... | collective-permute-start | bytes 786440 | tf_op jit(solution)/shard_map/ppermute | solution.py:342
  99.5 28.1 %collective-permute-start.18 = (bf16[1,4,2,64,256]{4,3,2,1,0:T(8,128)(2,1)}, bf16[1,4,2,64,256]{4,3,2,1,0:T(8,128)(2,1)}, u32[]{:S(2)}, u32[]{:S(2)}) collective-permute-start(bf16[1,4,2,64,256]{4,3,2,1,0:T(8,128)(2,1)} %get-tuple-element.51), channel_id=1, source_target_pairs={{0,64},{32,96},{64,0},{96,32},{128,192},{160,224},{192,128},{224,1... | collective-permute-start | bytes 786440 | tf_op jit(solution)/shard_map/ppermute | solution.py:342
  102.0 10.6 %collective-permute-start.11 = (f32[4,128]{1,0:T(4,128)S(1)}, f32[4,128]{1,0:T(4,128)S(1)}, u32[]{:S(2)}, u32[]{:S(2)}) collective-permute-start(f32[4,128]{1,0:T(4,128)S(1)} %get-tuple-element.44), channel_id=1, source_target_pairs={{0,32},{32,0},{64,96},{96,64},{128,160},{160,128},{192,224},{224,1... | collective-permute-start | bytes 6152 | tf_op jit(solution)/shard_map/ppermute | solution.py:351
  112.6 5.1 %collective-permute-start.12 = (f32[4,128]{1,0:T(4,128)S(1)}, f32[4,128]{1,0:T(4,128)S(1)}, u32[]{:S(2)}, u32[]{:S(2)}) collective-permute-start(f32[4,128]{1,0:T(4,128)S(1)} %add.96), channel_id=1, source_target_pairs={{0,64},{32,96},{64,0},{96,32},{128,192},{160,224},{192,128},{224,1... | collective-permute-start | bytes 6152 | tf_op jit(solution)/shard_map/ppermute | solution.py:351
  117.7 5.1 %collective-permute-start.13 = (f32[4,128]{1,0:T(4,128)S(1)}, f32[4,128]{1,0:T(4,128)S(1)}, u32[]{:S(2)}, u32[]{:S(2)}) collective-permute-start(f32[4,128]{1,0:T(4,128)S(1)} %add.97), channel_id=1, source_target_pairs={{0,128},{32,160},{64,192},{96,224},{128,0},{160,32},{192,64},{224,... | collective-permute-start | bytes 6152 | tf_op jit(solution)/shard_map/ppermute | solution.py:351
  122.8 1.2 collective-permute-start.14
  124.0 3.6 %collective-permute-start.15 = (f32[4,128]{1,0:T(4,128)S(1)}, f32[4,128]{1,0:T(4,128)S(1)}, u32[]{:S(2)}, u32[]{:S(2)}) collective-permute-start(f32[4,128]{1,0:T(4,128)S(1)} %add.99), channel_id=1, source_target_pairs={{0,2},{1,3},{2,0},{3,1},{4,6},{5,7},{6,4},{7,5},{8,10},{9,11},{10,... | collective-permute-start | bytes 6152 | tf_op jit(solution)/shard_map/ppermute | solution.py:351
  127.6 1.0 copy-start.1
  131.4 11.5 %collective-permute-start.21 = (f32[4,128]{1,0:T(4,128)S(1)}, f32[4,128]{1,0:T(4,128)S(1)}, u32[]{:S(2)}, u32[]{:S(2)}) collective-permute-start(f32[4,128]{1,0:T(4,128)S(1)} %get-tuple-element.50), channel_id=1, source_target_pairs={{1,25},{3,27},{5,29},{7,31},{9,17},{11,19},{13,21},{15,23},{17,9},... | collective-permute-start | bytes 6152 | tf_op jit(solution)/shard_map/ppermute | solution.py:366
  134.0 8.9 %collective-permute-start.22 = (f32[4,128]{1,0:T(4,128)S(1)}, f32[4,128]{1,0:T(4,128)S(1)}, u32[]{:S(2)}, u32[]{:S(2)}) collective-permute-start(f32[4,128]{1,0:T(4,128)S(1)} %get-tuple-element.50), channel_id=1, source_target_pairs={{1,29},{3,31},{5,25},{7,27},{9,21},{11,23},{13,17},{15,19},{17,13}... | collective-permute-start | bytes 6152 | tf_op jit(solution)/shard_map/ppermute | solution.py:366
  135.4 9.1 %collective-permute-start.20 = (f32[4,128]{1,0:T(4,128)S(1)}, f32[4,128]{1,0:T(4,128)S(1)}, u32[]{:S(2)}, u32[]{:S(2)}) collective-permute-start(f32[4,128]{1,0:T(4,128)S(1)} %get-tuple-element.50), channel_id=1, source_target_pairs={{1,21},{3,23},{5,17},{7,19},{9,29},{11,31},{13,25},{15,27},{17,5},... | collective-permute-start | bytes 6152 | tf_op jit(solution)/shard_map/ppermute | solution.py:366
  135.4 9.1 %collective-permute-start.19 = (f32[4,128]{1,0:T(4,128)S(1)}, f32[4,128]{1,0:T(4,128)S(1)}, u32[]{:S(2)}, u32[]{:S(2)}) collective-permute-start(f32[4,128]{1,0:T(4,128)S(1)} %get-tuple-element.50), channel_id=1, source_target_pairs={{1,17},{3,19},{5,21},{7,23},{9,25},{11,27},{13,29},{15,31},{17,1},... | collective-permute-start | bytes 6152 | tf_op jit(solution)/shard_map/ppermute | solution.py:366
  144.5 4.1 %collective-permute-start.23 = (f32[4,128]{1,0:T(4,128)S(1)}, f32[4,128]{1,0:T(4,128)S(1)}, u32[]{:S(2)}, u32[]{:S(2)}) collective-permute-start(f32[4,128]{1,0:T(4,128)S(1)} %add_add_fusion), channel_id=1, source_target_pairs={{0,1},{1,0},{2,3},{3,2},{4,5},{5,4},{6,7},{7,6},{8,9},{9,8},{10,11... | collective-permute-start | bytes 6152 | tf_op jit(solution)/shard_map/ppermute | solution.py:351

commit v2 on v1

v2 whole, which is shorter than its diff:
```python
import functools

import jax
import jax.numpy as jnp
from jax import lax
from jax.experimental import pallas as pl
from jax.experimental.pallas import tpu as pltpu
from jax.sharding import PartitionSpec as P

HEADS = 16
HEAD_DIM = 128
EPS = 1e-06
SCALE = HEAD_DIM**-0.5
LOG2E = 1.4426950408889634
BF16 = jnp.bfloat16
F32 = jnp.float32
SEQ = 2048
BLOCK = 1024
ONES = 16
TEMPORAL_FLOPS = 30 * 10**9
XSTEPS = (1, 3, 2)
TEMPORAL_MIB = 24
UNPACK_MIB = 24
TEMPORAL_ROWS = 32
TOGETHER = 4
HERE_FIRST = 3


def dot(a, b, ca, cb):
    return lax.dot_general(a, b, (((ca,), (cb,)), ((), ())), preferred_element_type=F32)


def params(mib):
    return pltpu.CompilerParams(vmem_limit_bytes=mib << 20)


def cost(flops, nbytes, trans=0):
    return pl.CostEstimate(flops=flops, bytes_accessed=nbytes, transcendentals=trans)


def inverse_rms(xf):
    return lax.rsqrt(jnp.mean(xf * xf, axis=-1, keepdims=True) + EPS)


def norm_back(grad_hat, x, gain):
    xf = x.astype(F32)
    inverse = inverse_rms(xf)
    unit = xf * inverse
    scaled = grad_hat * gain
    dgain = jnp.sum(grad_hat * unit, axis=0, keepdims=True)
    dx = inverse * (scaled - unit * jnp.mean(scaled * unit, axis=-1, keepdims=True))
    return dx.astype(BF16), dgain


def places_of_x(width):
    x = lax.rem(lax.axis_index("frame"), 4)
    return [pl.ds(pl.multiple_of(lax.rem(x + step, 4) * width, width), width) for step in (0, *XSTEPS)]


def row_lanes(other, width):
    row = lax.div(lax.axis_index("frame"), 4)
    row = 1 - row if other else row
    return pl.ds(pl.multiple_of(row * width, width), width)


def pack_kernel(*refs):
    far, near, there_refs, sent_ref = refs[:4], refs[4:8], refs[8:10], refs[10]
    far_in, near_in, there, sent, sem_far, sem_near, sem_there, sem_sent = refs[11:]
    frames, places, half = far_in.shape[1:]
    part = half // 4
    lanes = row_lanes(True, half)

    def fetch_far(a):
        return pltpu.make_async_copy(far[a].at[:, :, lanes], far_in.at[a], sem_far.at[a])

    def fetch_near(a, f):
        return pltpu.make_async_copy(near[a].at[f], near_in.at[a, f], sem_near.at[a, f])

    def send_there(a, i):
        pair = pl.ds(2 * i, 2)
        return pltpu.make_async_copy(there.at[pair, a], there_refs[i].at[:, a], sem_there.at[a, i])

    def send_sent(a, f):
        heads = pl.ds(f * HEADS, HEADS)
        return pltpu.make_async_copy(sent.at[heads, a], sent_ref.at[heads, a], sem_sent.at[a, f])

    for a in range(4):
        fetch_far(a).start()
    for a in range(4):
        for f in range(frames):
            fetch_near(a, f).start()
    spans = places_of_x(part)
    for a in range(4):
        fetch_far(a).wait()
        for i, span in enumerate(spans):
            there[i, a] = far_in[a, :, :, span]
        for i in range(2):
            send_there(a, i).start()
    for a in range(4):
        for f in range(frames):
            fetch_near(a, f).wait()
            for h in range(HEADS):
                sent[f * HEADS + h, a] = near_in[a, f, :, h * HEAD_DIM : (h + 1) * HEAD_DIM]
            send_sent(a, f).start()
    for a in range(4):
        for i in range(2):
            send_there(a, i).wait()
        for f in range(frames):
            send_sent(a, f).wait()


def pack(far, near):
    frames, places, width = near[0].shape
    there = (4, 4, frames, places, width // 8)
    sent = (frames * HEADS, 4, places, HEAD_DIM)
    anywhere = pl.BlockSpec(memory_space=pl.ANY)
    return pl.pallas_call(
        pack_kernel,
        out_shape=[jax.ShapeDtypeStruct((2, *there[1:]), BF16)] * 2 + [jax.ShapeDtypeStruct(sent, BF16)],
        in_specs=[anywhere] * 8,
        out_specs=[anywhere] * 3,
        scratch_shapes=[
            pltpu.VMEM((4, frames, places, width // 2), BF16),
            pltpu.VMEM((4, frames, places, width), BF16),
            pltpu.VMEM(there, BF16),
            pltpu.VMEM(sent, BF16),
            pltpu.SemaphoreType.DMA((4,)),
            pltpu.SemaphoreType.DMA((4, frames)),
            pltpu.SemaphoreType.DMA((4, 2)),
            pltpu.SemaphoreType.DMA((4, frames)),
        ],
        compiler_params=params(60),
        cost_estimate=cost(0, 6 << 20),
        name="pack",
    )(*far, *near)


def pack_here_kernel(q_ref, k_ref, v_ref, d_ref, *refs):
    outs, held, sem = refs[:4], refs[4], refs[5]
    lanes = row_lanes(False, held.shape[-1])
    copies = [
        pltpu.make_async_copy(ref.at[:, :, lanes], held.at[a], sem.at[a])
        for a, ref in enumerate((q_ref, k_ref, v_ref, d_ref))
    ]
    for copy in copies:
        copy.start()
    spans = places_of_x(held.shape[-1] // 4)
    for a, copy in enumerate(copies):
        copy.wait()
        for out, span in zip(outs, spans):
            out[0, a] = held[a, :, :, span]


def pack_here(arrays):
    frames, places, width = arrays[0].shape
    return pl.pallas_call(
        pack_here_kernel,
        out_shape=[jax.ShapeDtypeStruct((1, 4, frames, places, width // 8), BF16)] * 4,
        in_specs=[pl.BlockSpec(memory_space=pl.ANY)] * 4,
        out_specs=[pl.BlockSpec(memory_space=pltpu.VMEM)] * 4,
        scratch_shapes=[pltpu.VMEM((4, frames, places, width // 2), BF16), pltpu.SemaphoreType.DMA((4,))],
        compiler_params=params(56),
        cost_estimate=cost(0, 2 << 20),
        name="pack_here",
    )(*arrays)


def unpack_s_kernel(x_ref, half_ref, other_ref, *out_refs):
    heads = x_ref.shape[1]
    out_refs[4][...] = half_ref[...] + other_ref[...]
    for a, ref in enumerate(out_refs[:4]):
        for f in range(2):
            for h in range(heads):
                ref[f, :, h * HEAD_DIM : (h + 1) * HEAD_DIM] = x_ref[f, h, a]


def unpack_s(x, halves, frames):
    places = x.shape[2]
    group = 4
    whole = pl.BlockSpec(halves[0].shape, lambda i: (0, 0))
    return pl.pallas_call(
        unpack_s_kernel,
        out_shape=[jax.ShapeDtypeStruct((frames, places, HEADS * HEAD_DIM), BF16)] * 4
        + [jax.ShapeDtypeStruct(halves[0].shape, F32)],
        grid=(HEADS // group,),
        in_specs=[pl.BlockSpec((frames, group, 4, places, HEAD_DIM), lambda i: (0, i, 0, 0, 0)), whole, whole],
        out_specs=[pl.BlockSpec((frames, places, group * HEAD_DIM), lambda i: (0, 0, i))] * 4 + [whole],
        compiler_params=params(16),
        cost_estimate=cost(0, 4 << 20),
        name="unpack_spatial",
    )(x.reshape(frames, HEADS, 4, places, HEAD_DIM), *halves)


def unpack_t_kernel(grads_ref, *refs):
    parts, outs, grads_out = refs[:8], refs[8:12], refs[12]
    half = outs[0].shape[-1] // 2
    part = half // 4
    grads_out[...] = grads_ref[...]
    row, x = lax.div(lax.axis_index("frame"), 4), lax.rem(lax.axis_index("frame"), 4)
    for j, ref in enumerate(parts):
        first = (1 - row if j >= 4 else row) * half + lax.rem(x + (0, *XSTEPS)[j % 4], 4) * part
        lanes = pl.ds(pl.multiple_of(first, part), part)
        for a, out in enumerate(outs):
            out[:, :, lanes] = ref[0, a]


def unpack_t(grads, parts):
    _, _, frames, places, part = parts[0].shape
    whole = pl.BlockSpec(grads.shape, lambda f: (0, 0))
    return pl.pallas_call(
        unpack_t_kernel,
        out_shape=[jax.ShapeDtypeStruct((frames, places, part * 8), BF16)] * 4
        + [jax.ShapeDtypeStruct(grads.shape, F32)],
        grid=(frames,),
        in_specs=[whole] + [pl.BlockSpec((1, 4, 1, places, part), lambda f: (0, 0, f, 0, 0))] * 8,
        out_specs=[pl.BlockSpec((1, places, part * 8), lambda f: (f, 0, 0))] * 4 + [whole],
        compiler_params=params(UNPACK_MIB),
        cost_estimate=cost(0, 4 << 20),
        name="unpack_temporal",
    )(grads, *parts)


def temporal_kernel(gains_ref, *refs):
    ins = [ref.at[0] for ref in refs[:8]]
    own, there, here, dgain_ref = refs[8], refs[9], refs[10:13], refs[13]
    there = [there.at[i] for i in range(4)]
    outs = [own.at[0], there[0]] + [ref.at[0] for ref in here] + there[1:]
    _, frames, places, width = ins[0].shape
    rows = 8 * frames * 16
    gain_q, gain_k = gains_ref[2:3, :], gains_ref[3:4, :]

    @pl.when(pl.program_id(0) == 0)
    def _():
        dgain_ref[...] = jnp.zeros_like(dgain_ref)

    row = lax.broadcasted_iota(jnp.int32, (rows, rows), 0)
    column = lax.broadcasted_iota(jnp.int32, (rows, rows), 1)
    same = (row % 16) == (column % 16)

    spots = [
        (slice(first, first + 16), slice(h, h + HEAD_DIM))
        for first in range(0, places, 16)
        for h in range(0, width, HEAD_DIM)
    ]
    for first in range(0, len(spots), TOGETHER):
        temporal_spots(spots[first : first + TOGETHER], ins, outs, dgain_ref, gain_q, gain_k, same)


def temporal_spots(spots, ins, outs, dgain_ref, gain_q, gain_k, same):
    frames = ins[0].shape[1]

    def take(a):
        return [jnp.concatenate([ref[a, f, *spot] for ref in ins for f in range(frames)], axis=0) for spot in spots]

    def each(f, *lists):
        return [f(*items) for items in zip(*lists)]

    def put(a, results):
        for spot, result in zip(spots, results):
            result = result.astype(BF16)
            for j, ref in enumerate(outs):
                for f in range(frames):
                    first = (j * frames + f) * 16
                    ref[a, f, *spot] = result[first : first + 16]

    def hat(x, gain):
        xf = x.astype(F32)
        return (xf * inverse_rms(xf) * gain).astype(BF16)

    query, key, value, dout = take(0), take(1), take(2), take(3)
    qh = each(lambda x: hat(x, gain_q), query)
    kh = each(lambda x: hat(x, gain_k), key)
    expo = each(lambda q, k: jnp.where(same, jnp.exp(dot(q, k, 1, 1) * SCALE), 0.0), qh, kh)
    probs = each(lambda e: e / jnp.sum(e, axis=-1, keepdims=True), expo)
    probs_b = each(lambda p: p.astype(BF16), probs)
    out = each(lambda p, v: dot(p, v, 1, 0), probs_b, value)
    dprob = each(lambda d, v: dot(d, v, 1, 1), dout, value)
    put(0, out)
    delta = each(lambda d, o: jnp.sum(d.astype(F32) * o, axis=-1, keepdims=True), dout, out)
    dscore = each(lambda p, dp, d: (p * (dp - d)).astype(BF16), probs, dprob, delta)
    put(3, each(lambda p, d: dot(p, d, 0, 0), probs_b, dout))
    dqh = each(lambda ds, k: dot(ds, k, 1, 0) * SCALE, dscore, kh)
    dkh = each(lambda ds, q: dot(ds, q, 0, 0) * SCALE, dscore, qh)
    for a, grads, given, gain in ((1, dqh, query, gain_q), (2, dkh, key, gain_k)):
        back = each(lambda g, x, gain=gain: norm_back(g, x, gain), grads, given)
        put(a, [dx for dx, _ in back])
        dgain_ref[a - 1 : a, :] += sum(dgain for _, dgain in back)


def temporal(gains, parts):
    _, arrays, frames, places, width = parts[0].shape
    sizes = (1, 4, 1, 1, 1)

    def block(n):
        return pl.BlockSpec((n, arrays, frames, TEMPORAL_ROWS, width), lambda i: (0, 0, 0, i, 0))

    res = pl.pallas_call(
        temporal_kernel,
        out_shape=[jax.ShapeDtypeStruct((n, arrays, frames, places, width), BF16) for n in sizes]
        + [jax.ShapeDtypeStruct((2, HEAD_DIM), F32)],
        grid=(places // TEMPORAL_ROWS,),
        in_specs=[pl.BlockSpec(gains.shape, lambda i: (0, 0))] + [block(1)] * 8,
        out_specs=[block(n) for n in sizes] + [pl.BlockSpec((2, HEAD_DIM), lambda i: (0, 0))],
        compiler_params=params(TEMPORAL_MIB),
        cost_estimate=cost(TEMPORAL_FLOPS, 4 << 20, 8 * 65536),
        name="temporal_attention",
    )(gains, *parts)
    return res[0], res[1], res[2:5], res[5]


def spatial_kernel(
    gains_ref, grads_t_ref, x_ref, home_ref, dgain_ref, qh, kh, kh_t, v_t, expo, dscore, out_t, dp_t, dp_n, dq_t, out_ref, sem
):
    tiles, _, places, depth = x_ref.shape
    seq = tiles * places
    per = BLOCK // places
    gain_q, gain_k = gains_ref[0:1, :], gains_ref[1:2, :]

    def rows_of(b):
        return pl.ds(pl.multiple_of(b * BLOCK, BLOCK), BLOCK)

    def read(a, b):
        return x_ref[pl.ds(b * per, per), a].reshape(BLOCK, depth)

    def write(a, b, value):
        out_ref[pl.ds(b * per, per), a] = value.astype(BF16).reshape(per, places, depth)

    def prepare(b, _):
        rows = rows_of(b)
        qf = read(0, b).astype(F32)
        qh[rows, :] = (qf * inverse_rms(qf) * gain_q).astype(BF16)
        kf = read(1, b).astype(F32)
        k_hat = (kf * inverse_rms(kf) * gain_k).astype(BF16)
        kh[rows, :] = k_hat
        kh_t[:, rows] = k_hat.T
        v_t[0:depth, rows] = read(2, b).T
        v_t[depth:, rows] = jnp.ones((ONES, BLOCK), BF16)
        return 0

    lax.fori_loop(0, seq // BLOCK, prepare, 0)

    def forward(b, _):
        rows = rows_of(b)
        q_b = qh[rows, :]
        for c in range(seq // BLOCK):
            keys = slice(c * BLOCK, (c + 1) * BLOCK)
            scores = dot(kh[keys, :], q_b, 1, 1)
            expo[keys, rows] = jnp.exp2(scores * (SCALE * LOG2E)).astype(BF16)
        out_t[...] = dot(v_t[...], expo[:, rows], 1, 0)
        inverse = 1.0 / out_t[depth : depth + 1, :]
        o_t = out_t[0:depth, :] * inverse
        write(0, b, o_t.astype(BF16).T)
        d_t = (read(3, b).T.astype(F32) * inverse).astype(BF16)
        delta = jnp.sum(d_t.astype(F32) * o_t, axis=0, keepdims=True)
        dp_t[:, rows] = d_t
        dp_n[rows, :] = d_t.T
        for c in range(seq // BLOCK):
            keys = slice(c * BLOCK, (c + 1) * BLOCK)
            value = x_ref[c * per : (c + 1) * per, 2].reshape(BLOCK, depth)
            grad = dot(value, d_t, 1, 0)
            dscore[keys, rows] = (expo[keys, rows].astype(F32) * (grad - delta)).astype(BF16)
        dq_t[...] = dot(kh_t[...], dscore[:, rows], 1, 0) * SCALE
        dquery, dgain = norm_back(dq_t[...].T, read(0, b), gain_q)
        write(1, b, dquery)
        dgain_ref[0:1, :] += dgain
        sending(b, 0).start()
        return 0

    def sending(b, phase):
        part = (pl.ds(b * per, per), pl.ds(2 * phase, 2))
        return pltpu.make_async_copy(out_ref.at[part], home_ref.at[part], sem.at[phase, b])

    dgain_ref[0:2, :] = jnp.zeros((2, depth), F32)
    dgain_ref[2:4, :] = grads_t_ref[...]
    lax.fori_loop(0, seq // BLOCK, forward, 0)

    def backward(b, _):
        rows = rows_of(b)
        dkh = dot(dscore[rows, :], qh[...], 1, 0) * SCALE
        dkey, dgain = norm_back(dkh, read(1, b), gain_k)
        write(2, b, dkey)
        dgain_ref[1:2, :] += dgain
        write(3, b, dot(expo[rows, :], dp_n[...], 1, 0))
        sending(b, 1).start()
        return 0

    lax.fori_loop(0, seq // BLOCK, backward, 0)
    for phase in range(2):
        for b in range(seq // BLOCK):
            sending(b, phase).wait()


def spatial(gains, grads_t, x):
    tiles, _, places, depth = x.shape
    seq = tiles * places
    whole = pl.BlockSpec(memory_space=pltpu.VMEM)
    return pl.pallas_call(
        spatial_kernel,
        out_shape=[jax.ShapeDtypeStruct(x.shape, BF16), jax.ShapeDtypeStruct((4, depth), F32)],
        in_specs=[whole, whole, whole],
        out_specs=[pl.BlockSpec(memory_space=pl.ANY), whole],
        scratch_shapes=[
            pltpu.VMEM((seq, depth), BF16),
            pltpu.VMEM((seq, depth), BF16),
            pltpu.VMEM((depth, seq), BF16),
            pltpu.VMEM((depth + ONES, seq), BF16),
            pltpu.VMEM((seq, seq), BF16),
            pltpu.VMEM((seq, seq), BF16),
            pltpu.VMEM((depth + ONES, BLOCK), F32),
            pltpu.VMEM((depth, seq), BF16),
            pltpu.VMEM((seq, depth), BF16),
            pltpu.VMEM((depth, BLOCK), F32),
            pltpu.VMEM(x.shape, BF16),
            pltpu.SemaphoreType.DMA((2, seq // BLOCK)),
        ],
        compiler_params=params(36),
        cost_estimate=cost(6 * 2 * seq * seq * depth, 4 << 20, seq * seq),
        name="spatial_attention",
    )(gains, grads_t, x)


def after_kernel(x_ref, *refs):
    pass


def after(x, others):
    anywhere = pl.BlockSpec(memory_space=pl.ANY)
    return pl.pallas_call(
        after_kernel,
        out_shape=jax.ShapeDtypeStruct(x.shape, x.dtype),
        in_specs=[anywhere] * (1 + len(others)),
        out_specs=anywhere,
        input_output_aliases={0: 0},
        compiler_params=params(1),
        cost_estimate=cost(0, 1024),
        name="after",
    )(x, *others)


def over_tile(x):
    count, arrays, places, depth = x.shape
    x = x.reshape(count, arrays * places, depth)
    return lax.all_to_all(x, "tile", split_axis=0, concat_axis=0, tiled=True).reshape(count, arrays, places, depth)


def along_x(x, step):
    return lax.ppermute(x, "frame", [(i, i // 4 * 4 + (i + step) % 4) for i in range(8)])


def across(x):
    return lax.ppermute(x, "frame", [(i, (i + 4) % 8) for i in range(8)])


def three_of(there):
    return [there[0][1:], there[1][:1], there[1][1:]]


def from_partner(x, axis, bit):
    size = 8 if axis == "frame" else 32
    return lax.ppermute(x, axis, [(i, i ^ bit) for i in range(size)])


def total_off_z(x):
    for axis, bit in (("frame", 1), ("frame", 2), ("frame", 4), ("tile", 1), ("tile", 2)):
        x = x + from_partner(x, axis, bit)
    return x


def total_z(x):
    got = []
    for near, far in ((None, 4), (1, 5), (2, 6), (3, 7)):
        perm = [(i, i ^ (4 * far)) for i in range(1, 32, 2)]
        if near is not None:
            perm += [(i, i ^ (4 * near)) for i in range(0, 32, 2)]
        got.append(lax.ppermute(x, "tile", perm))
    got[0] = jnp.where(lax.axis_index("tile") % 2 == 0, x, got[0])
    half = (got[0] + got[1]) + (got[2] + got[3])
    return half, from_partner(half, "tile", 1)


def local(query_s, key_s, value_s, grad_out_s, query_t, key_t, value_t, grad_out_t, gains):
    frames = query_s.shape[0]
    given_t = (query_t, key_t, value_t, grad_out_t)

    *there, sent = pack(given_t, (query_s, key_s, value_s, grad_out_s))
    there = [across(pair) for pair in there]
    items = over_tile(sent)
    here = pack_here(given_t)
    parts = [here[0], there[0]]
    for part, step in zip(here[1:], XSTEPS):
        parts.append(along_x(part, step))
    for part, step in zip(three_of(there), XSTEPS):
        parts.append(along_x(part, step))

    own, there, here, grads_t = temporal(gains, parts)
    there = across(there)
    here = [along_x(part, -step) for part, step in zip(here, XSTEPS)]
    there_x = [along_x(there[i + 1 : i + 2], -step) for i, step in enumerate(XSTEPS)]

    res, grads = spatial(gains, grads_t, items)
    home = over_tile(after(res, [there, *here[:HERE_FIRST]]))
    *outs_t, grads = unpack_t(total_off_z(grads), [own, *here, there, *there_x])
    *outs_s, gain_grads = unpack_s(home, total_z(grads), frames)
    return (*outs_s, *outs_t, gain_grads)


def solution(mesh):
    split = P("frame", "tile", None)
    return jax.shard_map(
        local,
        mesh=mesh,
        in_specs=(split,) * 8 + (P(),),
        out_specs=(split,) * 8 + (P(),),
        check_vma=False,
    )
```

time: 154 us -> 149 us (0.968); the launches traced: 151 us -> 148 us
  Pallas kernels: 35.2 us -> 29 us
  waiting for transfers between devices: 51.4 us -> 55.2 us
    pallas_call x4 -> x3, Pallas kernels: 15.1 us -> 9.91 us  [the longest x1 4.26 us: temporal(): pl.pallas_call(temporal_kernel, out_shape=[jax.ShapeDtypeStruct((n, array...]
    ppermute x2 -> x3, waiting for transfers between devices: 14.6 us -> 16.7 us  [across(): return lax.ppermute(x, 'frame', [(i, (i + 4) % 8) for i in range(8)])]
    ppermute x4, waiting for transfers between devices: 8.43 us -> 10.4 us  [total_z(): got.append(lax.ppermute(x, 'tile', perm))]
    ppermute x2 -> x3, starting transfers between devices: 6.68 us -> 8.34 us  [across(): return lax.ppermute(x, 'frame', [(i, (i + 4) % 8) for i in range(8)])]
  transfers between devices with their start and end apart: 26 -> 27, of which waited for: 12 -> 12; matrix products, arithmetic and copies ran while one was open for 1% -> 1% of each run, Pallas kernels for 20% -> 16%
where the time goes in v2:
time: 149 us; the launch traced here: 148 us
  starting transfers between devices  59.1 us (40%)
  waiting for transfers between devices  55.2 us (37%)
  Pallas kernels  29 us (19%)
  local copies, waits for them, and re-layouts  3.74 us (3%)
    ppermute x6, waiting for transfers between devices, from_partner(): return lax.ppermute(x, axis, [(i, i ^ bit) for i in range(size)])  20.2 us
    all_to_all x2, starting transfers between devices, over_tile(): lax.all_to_all(x, 'tile', split_axis=0, concat_axis=0, tiled=True)  19.6 us
    ppermute x12, starting transfers between devices, along_x(): lax.ppermute(x, 'frame', [(i, i // 4 * 4 + (i + step) % 4) for i in range...  18.4 us
    ppermute x3, waiting for transfers between devices, across(): return lax.ppermute(x, 'frame', [(i, (i + 4) % 8) for i in range(8)])  16.7 us
    pallas_call x1, Pallas kernels, spatial(): pl.pallas_call(spatial_kernel, out_shape=[jax.ShapeDtypeStruct(x.shape, B...  14.6 us
    ppermute x4, waiting for transfers between devices, total_z(): got.append(lax.ppermute(x, 'tile', perm))  10.4 us
    ppermute x3, starting transfers between devices, across(): return lax.ppermute(x, 'frame', [(i, (i + 4) % 8) for i in range(8)])  8.34 us
    ppermute x6, starting transfers between devices, from_partner(): return lax.ppermute(x, axis, [(i, i ^ bit) for i in range(size)])  8.17 us
  transfers between devices with their start and end apart: 27, of which 12 were waited for; matrix products, arithmetic and copies ran while one was open for 1% of the time, Pallas kernels for 16%

profile of v2, /device:TPU:2, one launch (start us, length us, event | category | flops | bytes accessed | tf_op | source)
XLA Modules:
  0.0 148.0 jit_solution(1603586694282000737)
XLA Ops:
  0.6 3.4 %pack.1 = (bf16[2,4,2,64,256]{4,3,2,1,0:T(8,128)(2,1)}, bf16[2,4,2,64,256]{4,3,2,1,0:T(8,128)(2,1)}, bf16[32,4,64,128]{3,2,1,0:T(8,128)(2,1)}) custom-call(bf16[2,64,2048]{2,1,0:T(8,128)(2,1)} %refs_0_.1, bf16[2,64,2048]{2,1,0:T(8,128)(2,1)} %refs_1_.1, bf16[2,64,2048]{2,1,0:T(8,128)(2,1)} %refs_2_.1, bf16[2,64,2048]{2,1,0:T(8,128)(2,1)} %refs_3_.1, ...), custom_call_target="tpu_custom_call" | custom-call | bytes 6291456 | tf_op jit(solution)/shard_map/pack/pallas_call | solution.py:117
  4.1 3.3 %collective-permute-start = (bf16[2,4,2,64,256]{4,3,2,1,0:T(8,128)(2,1)}, bf16[2,4,2,64,256]{4,3,2,1,0:T(8,128)(2,1)S(1)}, u32[]{:S(2)}, u32[]{:S(2)}) collective-permute-start(bf16[2,4,2,64,256]{4,3,2,1,0:T(8,128)(2,1)} %get-tuple-element.35), channel_id=1, source_target_pairs={{0,128},{32,160},{64,192},{96,224},{128,0},{160,32},{192,64},{224,... | collective-permute-start | bytes 1572872 | tf_op jit(solution)/shard_map/ppermute | solution.py:451
  7.4 0.3 collective-permute-start.5
  7.7 9.9 %all-to-all-start = ((bf16[32,256,128]{2,1,0:T(8,128)(2,1)}), bf16[32,256,128]{2,1,0:T(8,128)(2,1)S(1)}, u32[]{:S(2)}, u32[]{:S(2)}) async-start(bf16[32,256,128]{2,1,0:T(8,128)(2,1)} %bitcast.6), calls=%async_computation | async-start | bytes 4194304 | tf_op jit(solution)/shard_map/all_to_all | solution.py:443
  17.6 0.0 copy-start.3
  17.6 2.2 %pack_here.1 = (bf16[1,4,2,64,256]{4,3,2,1,0:T(8,128)(2,1)}, bf16[1,4,2,64,256]{4,3,2,1,0:T(8,128)(2,1)}, bf16[1,4,2,64,256]{4,3,2,1,0:T(8,128)(2,1)}, bf16[1,4,2,64,256]{4,3,2,1,0:T(8,128)(2,1)}) custom-call(bf16[2,64,2048]{2,1,0:T(8,128)(2,1)} %refs_0_.1, bf16[2,64,2048]{2,1,0:T(8,128)(2,1)} %refs_1_.1, bf16[2,64,2048]{2,1,0:T(8,128)(2,1)} %refs_2_.1, ...), custom_call_target="tpu_custom_call" | custom-call | bytes 2097152 | tf_op jit(solution)/shard_map/pack_here/pallas_call | solution.py:156
  19.8 1.6 %collective-permute-start.1 = (bf16[1,4,2,64,256]{4,3,2,1,0:T(8,128)(2,1)}, bf16[1,4,2,64,256]{4,3,2,1,0:T(8,128)(2,1)S(1)}, u32[]{:S(2)}, u32[]{:S(2)}) collective-permute-start(bf16[1,4,2,64,256]{4,3,2,1,0:T(8,128)(2,1)} %get-tuple-element.36), channel_id=1, source_target_pairs={{0,32},{32,64},{64,96},{96,0},{128,160},{160,192},{192,224},{224,1... | collective-permute-start | bytes 786440 | tf_op jit(solution)/shard_map/ppermute | solution.py:447
  21.4 0.5 collective-permute-start.2
  21.9 2.1 %collective-permute-start.3 = (bf16[1,4,2,64,256]{4,3,2,1,0:T(8,128)(2,1)}, bf16[1,4,2,64,256]{4,3,2,1,0:T(8,128)(2,1)S(1)}, u32[]{:S(2)}, u32[]{:S(2)}) collective-permute-start(bf16[1,4,2,64,256]{4,3,2,1,0:T(8,128)(2,1)} %get-tuple-element.38), channel_id=1, source_target_pairs={{0,64},{32,96},{64,0},{96,32},{128,192},{160,224},{192,128},{224,1... | collective-permute-start | bytes 786440 | tf_op jit(solution)/shard_map/ppermute | solution.py:447
  24.0 0.0 collective-permute-done.refs_1_
  24.1 1.2 collective-permute-start.4
  25.2 16.2 %collective-permute-done.5 = bf16[2,4,2,64,256]{4,3,2,1,0:T(8,128)(2,1)} collective-permute-done((bf16[2,4,2,64,256]{4,3,2,1,0:T(8,128)(2,1)}, bf16[2,4,2,64,256]{4,3,2,1,0:T(8,128)(2,1)}, u32[]{:S(2)}, u32[]{:S(2)}) %collective-permute-start.5) | collective-permute-done | bytes 524320 | tf_op jit(solution)/shard_map/ppermute | solution.py:451
  41.4 1.1 fusion.1
  42.5 0.6 collective-permute-start.6
  43.1 0.0 collective-permute-done.1.refs_2_
  43.1 2.4 %collective-permute-start.7 = (bf16[1,4,2,64,256]{4,3,2,1,0:T(8,128)(2,1)S(1)}, bf16[1,4,2,64,256]{4,3,2,1,0:T(8,128)(2,1)S(1)}, u32[]{:S(2)}, u32[]{:S(2)}) collective-permute-start(bf16[1,4,2,64,256]{4,3,2,1,0:T(8,128)(2,1)S(1)} %get-tuple-element.62), channel_id=1, source_target_pairs={{0,64},{32,96},{64,0},{96,32},{128,192},{160,224},{192,128},{224,1... | collective-permute-start | bytes 786440 | tf_op jit(solution)/shard_map/ppermute | solution.py:447
  45.5 0.0 collective-permute-done.2.refs_3_
  45.5 0.0 collective-permute-done.3.refs_4_
  45.5 0.0 collective-permute-done.4.refs_5_
  45.5 5.1 %collective-permute-done.6.refs_6_ = bf16[1,4,2,64,256]{4,3,2,1,0:T(8,128)(2,1)S(1)} collective-permute-done((bf16[1,4,2,64,256]{4,3,2,1,0:T(8,128)(2,1)S(1)}, bf16[1,4,2,64,256]{4,3,2,1,0:T(8,128)(2,1)S(1)}, u32[]{:S(2)}, u32[]{:S(2)}) %collective-permute-start.6) | collective-permute-done | bytes 262176 | tf_op jit(solution)/shard_map/ppermute | solution.py:447
  50.7 2.8 %collective-permute-done.7.refs_7_ = bf16[1,4,2,64,256]{4,3,2,1,0:T(8,128)(2,1)S(1)} collective-permute-done((bf16[1,4,2,64,256]{4,3,2,1,0:T(8,128)(2,1)S(1)}, bf16[1,4,2,64,256]{4,3,2,1,0:T(8,128)(2,1)S(1)}, u32[]{:S(2)}, u32[]{:S(2)}) %collective-permute-start.7) | collective-permute-done | bytes 262176 | tf_op jit(solution)/shard_map/ppermute | solution.py:447
  53.5 0.9 copy-done.2
  54.4 4.3 %temporal_attention.1 = (bf16[1,4,2,64,256]{4,3,2,1,0:T(8,128)(2,1)S(1)}, bf16[4,4,2,64,256]{4,3,2,1,0:T(8,128)(2,1)}, bf16[1,4,2,64,256]{4,3,2,1,0:T(8,128)(2,1...) custom-call(f32[4,128]{1,0:T(4,128)S(1)} %copy-done.3, ...), custom_call_target="tpu_custom_call" | custom-call | flops 30000001024 | bytes 4194304 | tf_op jit(solution)/shard_map/temporal_attention/pallas_call | solution.py:297
  58.7 0.7 copy-done
  59.4 4.7 %collective-permute-start.8 = (bf16[4,4,2,64,256]{4,3,2,1,0:T(8,128)(2,1)}, bf16[4,4,2,64,256]{4,3,2,1,0:T(8,128)(2,1)S(1)}, u32[]{:S(2)}, u32[]{:S(2)}) collective-permute-start(bf16[4,4,2,64,256]{4,3,2,1,0:T(8,128)(2,1)} %get-tuple-element.43), channel_id=1, source_target_pairs={{0,128},{32,160},{64,192},{96,224},{128,0},{160,32},{192,64},{224,... | collective-permute-start | bytes 3145736 | tf_op jit(solution)/shard_map/ppermute | solution.py:451
  64.1 0.0 collective-permute-start.9
  64.1 2.0 %collective-permute-start.10 = (bf16[1,4,2,64,256]{4,3,2,1,0:T(8,128)(2,1)}, bf16[1,4,2,64,256]{4,3,2,1,0:T(8,128)(2,1)}, u32[]{:S(2)}, u32[]{:S(2)}) collective-permute-start(bf16[1,4,2,64,256]{4,3,2,1,0:T(8,128)(2,1)} %get-tuple-element.45), channel_id=1, source_target_pairs={{0,32},{32,64},{64,96},{96,0},{128,160},{160,192},{192,224},{224,1... | collective-permute-start | bytes 786440 | tf_op jit(solution)/shard_map/ppermute | solution.py:447
  66.1 3.6 %collective-permute-start.11 = (bf16[1,4,2,64,256]{4,3,2,1,0:T(8,128)(2,1)}, bf16[1,4,2,64,256]{4,3,2,1,0:T(8,128)(2,1)}, u32[]{:S(2)}, u32[]{:S(2)}) collective-permute-start(bf16[1,4,2,64,256]{4,3,2,1,0:T(8,128)(2,1)} %get-tuple-element.46), channel_id=1, source_target_pairs={{0,64},{32,96},{64,0},{96,32},{128,192},{160,224},{192,128},{224,1... | collective-permute-start | bytes 786440 | tf_op jit(solution)/shard_map/ppermute | solution.py:447
  69.8 0.0 all-to-all-done
  69.8 14.6 %spatial_attention.1 = (bf16[32,4,64,128]{3,2,1,0:T(8,128)(2,1)}, f32[4,128]{1,0:T(4,128)S(1)}) custom-call(f32[4,128]{1,0:T(4,128)S(1)} %copy-done.3, f32[2,128]{1,0:T(2,128)S(1)} %get-tuple-element.40.grads_t_ref, bf16[32,4,64,128]{3,2,1,0:T(8,128)(2,1)S(1)} %bitcast.5), custom_call_target="tpu_custom_call" | custom-call | flops 6442450944 | bytes 4194304 | tf_op jit(solution)/shard_map/spatial_attention/pallas_call | solution.py:397
  84.4 0.0 collective-permute-done.9.refs_1_
  84.4 0.0 collective-permute-done.10.refs_2_
  84.4 0.0 collective-permute-done.11.refs_3_
  84.4 0.5 collective-permute-done.8.refs_0_.refs_4_
  84.9 9.7 %all-to-all-start.1 = ((bf16[32,256,128]{2,1,0:T(8,128)(2,1)}), bf16[32,256,128]{2,1,0:T(8,128)(2,1)S(1)}, u32[]{:S(2)}, u32[]{:S(2)}) async-start(bf16[32,256,128]{2,1,0:T(8,128)(2,1)} %bitcast.2), calls=%async_computation.1 | async-start | bytes 4194304 | tf_op jit(solution)/shard_map/all_to_all | solution.py:443
  94.6 0.1 fusion
  94.7 0.1 collective-permute-start.17
  94.8 2.0 %collective-permute-start.18 = (bf16[1,4,2,64,256]{4,3,2,1,0:T(8,128)(2,1)S(1)}, bf16[1,4,2,64,256]{4,3,2,1,0:T(8,128)(2,1)S(1)}, u32[]{:S(2)}, u32[]{:S(2)}) collective-permute-start(bf16[1,4,2,64,256]{4,3,2,1,0:T(8,128)(2,1)S(1)} %get-tuple-element.60), channel_id=1, source_target_pairs={{0,32},{32,64},{64,96},{96,0},{128,160},{160,192},{192,224},{224,1... | collective-permute-start | bytes 786440 | tf_op jit(solution)/shard_map/ppermute | solution.py:447
  96.8 2.3 %collective-permute-start.19 = (bf16[1,4,2,64,256]{4,3,2,1,0:T(8,128)(2,1)S(1)}, bf16[1,4,2,64,256]{4,3,2,1,0:T(8,128)(2,1)S(1)}, u32[]{:S(2)}, u32[]{:S(2)}) collective-permute-start(bf16[1,4,2,64,256]{4,3,2,1,0:T(8,128)(2,1)S(1)} %get-tuple-element.59), channel_id=1, source_target_pairs={{0,64},{32,96},{64,0},{96,32},{128,192},{160,224},{192,128},{224,1... | collective-permute-start | bytes 786440 | tf_op jit(solution)/shard_map/ppermute | solution.py:447
  99.0 0.0 collective-permute-start.12
  99.0 10.1 %collective-permute-done.12 = f32[4,128]{1,0:T(4,128)S(1)} collective-permute-done((f32[4,128]{1,0:T(4,128)S(1)}, f32[4,128]{1,0:T(4,128)S(1)}, u32[]{:S(2)}, u32[]{:S(2)}) %collective-permute-start.12) | collective-permute-done | bytes 2080 | tf_op jit(solution)/shard_map/ppermute | solution.py:460
  109.1 1.3 collective-permute-start.13
  110.4 3.8 %collective-permute-done.13 = f32[4,128]{1,0:T(4,128)S(1)} collective-permute-done((f32[4,128]{1,0:T(4,128)S(1)}, f32[4,128]{1,0:T(4,128)S(1)}, u32[]{:S(2)}, u32[]{:S(2)}) %collective-permute-start.13) | collective-permute-done | bytes 2080 | tf_op jit(solution)/shard_map/ppermute | solution.py:460
  114.2 2.8 %collective-permute-start.14 = (f32[4,128]{1,0:T(4,128)S(1)}, f32[4,128]{1,0:T(4,128)S(1)}, u32[]{:S(2)}, u32[]{:S(2)}) collective-permute-start(f32[4,128]{1,0:T(4,128)S(1)} %add.30), channel_id=1, source_target_pairs={{0,128},{32,160},{64,192},{96,224},{128,0},{160,32},{192,64},{224,... | collective-permute-start | bytes 6152 | tf_op jit(solution)/shard_map/ppermute | solution.py:460
  117.0 2.3 %collective-permute-done.14 = f32[4,128]{1,0:T(4,128)S(1)} collective-permute-done((f32[4,128]{1,0:T(4,128)S(1)}, f32[4,128]{1,0:T(4,128)S(1)}, u32[]{:S(2)}, u32[]{:S(2)}) %collective-permute-start.14) | collective-permute-done | bytes 2080 | tf_op jit(solution)/shard_map/ppermute | solution.py:460
  119.3 1.2 collective-permute-done.15
  120.5 1.7 %collective-permute-start.16 = (f32[4,128]{1,0:T(4,128)S(1)}, f32[4,128]{1,0:T(4,128)S(1)}, u32[]{:S(2)}, u32[]{:S(2)}) collective-permute-start(f32[4,128]{1,0:T(4,128)S(1)} %add.32), channel_id=1, source_target_pairs={{0,2},{1,3},{2,0},{3,1},{4,6},{5,7},{6,4},{7,5},{8,10},{9,11},{10,... | collective-permute-start | bytes 6152 | tf_op jit(solution)/shard_map/ppermute | solution.py:460
  122.1 2.1 %collective-permute-done.16 = f32[4,128]{1,0:T(4,128)S(1)} collective-permute-done((f32[4,128]{1,0:T(4,128)S(1)}, f32[4,128]{1,0:T(4,128)S(1)}, u32[]{:S(2)}, u32[]{:S(2)}) %collective-permute-start.16) | collective-permute-done | bytes 2080 | tf_op jit(solution)/shard_map/ppermute | solution.py:460
  124.2 0.0 collective-permute-done.17.refs_5_
  124.2 0.0 collective-permute-done.18.refs_6_
  124.2 0.0 copy-start.1
  124.2 0.9 copy-done.1
  125.2 2.5 %unpack_temporal.1 = (bf16[2,64,2048]{2,1,0:T(8,128)(2,1)}, bf16[2,64,2048]{2,1,0:T(8,128)(2,1)}, bf16[2,64,2048]{2,1,0:T(8,128)(2,1)}, bf16[2,64,2048]{2,1,0:T(8,128)(2,1)}, f32[4,128]{1,0:T(4,128)S(1)}) custom-call(f32[4,128]{1,0:T(4,128)S(1)} %add.33.grads_ref, bf16[1,4,2,64,256]{4,3,2,1,0:T(8,128)(2,1)S(1)} %copy-done.1, ...), custom_call_target="tpu_custom_call" | custom-call | bytes 4194304 | tf_op jit(solution)/shard_map/unpack_temporal/pallas_call | solution.py:210
  127.6 2.4 %collective-permute-start.22 = (f32[4,128]{1,0:T(4,128)S(1)}, f32[4,128]{1,0:T(4,128)S(1)}, u32[]{:S(2)}, u32[]{:S(2)}) collective-permute-start(f32[4,128]{1,0:T(4,128)S(1)} %get-tuple-element.49), channel_id=1, source_target_pairs={{1,25},{3,27},{5,29},{7,31},{9,17},{11,19},{13,21},{15,23},{17,9},... | collective-permute-start | bytes 6152 | tf_op jit(solution)/shard_map/ppermute | solution.py:475
  130.0 1.5 collective-permute-start.23
  131.5 0.0 collective-permute-start.21
  131.6 0.6 collective-permute-start.20
  132.2 8.7 %collective-permute-done.22 = f32[4,128]{1,0:T(4,128)S(1)} collective-permute-done((f32[4,128]{1,0:T(4,128)S(1)}, f32[4,128]{1,0:T(4,128)S(1)}, u32[]{:S(2)}, u32[]{:S(2)}) %collective-permute-start.22) | collective-permute-done | bytes 2080 | tf_op jit(solution)/shard_map/ppermute | solution.py:475
  141.0 1.6 %collective-permute-done.21 = f32[4,128]{1,0:T(4,128)S(1)} collective-permute-done((f32[4,128]{1,0:T(4,128)S(1)}, f32[4,128]{1,0:T(4,128)S(1)}, u32[]{:S(2)}, u32[]{:S(2)}) %collective-permute-start.21) | collective-permute-done | bytes 2080 | tf_op jit(solution)/shard_map/ppermute | solution.py:475
  142.6 0.0 collective-permute-done.20
  142.6 2.4 %collective-permute-start.24 = (f32[4,128]{1,0:T(4,128)S(1)}, f32[4,128]{1,0:T(4,128)S(1)}, u32[]{:S(2)}, u32[]{:S(2)}) collective-permute-start(f32[4,128]{1,0:T(4,128)S(1)} %add_add_fusion.half_ref), channel_id=1, source_target_pairs={{0,1},{1,0},{2,3},{3,2},{4,5},{5,4},{6,7},{7,6},{8,9},{9,8},{10,11... | collective-permute-start | bytes 6152 | tf_op jit(solution)/shard_map/ppermute | solution.py:460
  145.0 0.8 collective-permute-done.24.other_ref
  145.8 0.0 all-to-all-done.1
  145.8 2.1 %unpack_spatial.1 = (bf16[2,64,2048]{2,1,0:T(8,128)(2,1)}, bf16[2,64,2048]{2,1,0:T(8,128)(2,1)}, bf16[2,64,2048]{2,1,0:T(8,128)(2,1)}, bf16[2,64,2048]{2,1,0:T(8,128)(2,1)}, f32[4,128]{1,0:T(4,128)}) custom-call(bf16[2,16,4,64,128]{4,3,2,1,0:T(8,128)(2,1)S(1)} %bitcast.4, f32[4,128]{1,0:T(4,128)S(1)} %add_add_fusion.half_ref, ...), custom_call_target="tpu_custom_call" | custom-call | bytes 4194304 | tf_op jit(solution)/shard_map/unpack_spatial/pallas_call | solution.py:181
  (14 shorter events, 0.1 us)
Async XLA Ops:
  4.1 20.0 %collective-permute-start = (bf16[2,4,2,64,256]{4,3,2,1,0:T(8,128)(2,1)}, bf16[2,4,2,64,256]{4,3,2,1,0:T(8,128)(2,1)S(1)}, u32[]{:S(2)}, u32[]{:S(2)}) collective-permute-start(bf16[2,4,2,64,256]{4,3,2,1,0:T(8,128)(2,1)} %get-tuple-element.35), channel_id=1, source_target_pairs={{0,128},{32,160},{64,192},{96,224},{128,0},{160,32},{192,64},{224,... | collective-permute-start | bytes 1572872 | tf_op jit(solution)/shard_map/ppermute | solution.py:451
  7.4 34.1 %collective-permute-start.5 = (bf16[2,4,2,64,256]{4,3,2,1,0:T(8,128)(2,1)}, bf16[2,4,2,64,256]{4,3,2,1,0:T(8,128)(2,1)}, u32[]{:S(2)}, u32[]{:S(2)}) collective-permute-start(bf16[2,4,2,64,256]{4,3,2,1,0:T(8,128)(2,1)} %get-tuple-element.39), channel_id=1, source_target_pairs={{0,128},{32,160},{64,192},{96,224},{128,0},{160,32},{192,64},{224,... | collective-permute-start | bytes 1572872 | tf_op jit(solution)/shard_map/ppermute | solution.py:451
  7.7 62.1 %all-to-all-start = ((bf16[32,256,128]{2,1,0:T(8,128)(2,1)}), bf16[32,256,128]{2,1,0:T(8,128)(2,1)S(1)}, u32[]{:S(2)}, u32[]{:S(2)}) async-start(bf16[32,256,128]{2,1,0:T(8,128)(2,1)} %bitcast.6), calls=%async_computation | async-start | bytes 4194304 | tf_op jit(solution)/shard_map/all_to_all | solution.py:443
  17.6 35.9 %copy-start.3 = (f32[4,128]{1,0:T(4,128)S(1)}, f32[4,128]{1,0:T(4,128)}, u32[]{:S(2)}) copy-start(f32[4,128]{1,0:T(4,128)} %gains_ref.3) | copy-start | bytes 6148
  19.8 23.3 %collective-permute-start.1 = (bf16[1,4,2,64,256]{4,3,2,1,0:T(8,128)(2,1)}, bf16[1,4,2,64,256]{4,3,2,1,0:T(8,128)(2,1)S(1)}, u32[]{:S(2)}, u32[]{:S(2)}) collective-permute-start(bf16[1,4,2,64,256]{4,3,2,1,0:T(8,128)(2,1)} %get-tuple-element.36), channel_id=1, source_target_pairs={{0,32},{32,64},{64,96},{96,0},{128,160},{160,192},{192,224},{224,1... | collective-permute-start | bytes 786440 | tf_op jit(solution)/shard_map/ppermute | solution.py:447
  21.4 24.1 %collective-permute-start.2 = (bf16[1,4,2,64,256]{4,3,2,1,0:T(8,128)(2,1)}, bf16[1,4,2,64,256]{4,3,2,1,0:T(8,128)(2,1)S(1)}, u32[]{:S(2)}, u32[]{:S(2)}) collective-permute-start(bf16[1,4,2,64,256]{4,3,2,1,0:T(8,128)(2,1)} %get-tuple-element.37), channel_id=1, source_target_pairs={{0,96},{32,0},{64,32},{96,64},{128,224},{160,128},{192,160},{224,1... | collective-permute-start | bytes 786440 | tf_op jit(solution)/shard_map/ppermute | solution.py:447
  21.9 23.6 %collective-permute-start.3 = (bf16[1,4,2,64,256]{4,3,2,1,0:T(8,128)(2,1)}, bf16[1,4,2,64,256]{4,3,2,1,0:T(8,128)(2,1)S(1)}, u32[]{:S(2)}, u32[]{:S(2)}) collective-permute-start(bf16[1,4,2,64,256]{4,3,2,1,0:T(8,128)(2,1)} %get-tuple-element.38), channel_id=1, source_target_pairs={{0,64},{32,96},{64,0},{96,32},{128,192},{160,224},{192,128},{224,1... | collective-permute-start | bytes 786440 | tf_op jit(solution)/shard_map/ppermute | solution.py:447
  24.1 21.5 %collective-permute-start.4 = (bf16[1,4,2,64,256]{4,3,2,1,0:T(8,128)(2,1)S(1)}, bf16[1,4,2,64,256]{4,3,2,1,0:T(8,128)(2,1)S(1)}, u32[]{:S(2)}, u32[]{:S(2)}) collective-permute-start(bf16[1,4,2,64,256]{4,3,2,1,0:T(8,128)(2,1)S(1)} %slice.24), channel_id=1, source_target_pairs={{0,32},{32,64},{64,96},{96,0},{128,160},{160,192},{192,224},{224,1... | collective-permute-start | bytes 786440 | tf_op jit(solution)/shard_map/ppermute | solution.py:447
  42.5 8.2 %collective-permute-start.6 = (bf16[1,4,2,64,256]{4,3,2,1,0:T(8,128)(2,1)S(1)}, bf16[1,4,2,64,256]{4,3,2,1,0:T(8,128)(2,1)S(1)}, u32[]{:S(2)}, u32[]{:S(2)}) collective-permute-start(bf16[1,4,2,64,256]{4,3,2,1,0:T(8,128)(2,1)S(1)} %get-tuple-element.63), channel_id=1, source_target_pairs={{0,96},{32,0},{64,32},{96,64},{128,224},{160,128},{192,160},{224,1... | collective-permute-start | bytes 786440 | tf_op jit(solution)/shard_map/ppermute | solution.py:447
  43.1 10.4 %collective-permute-start.7 = (bf16[1,4,2,64,256]{4,3,2,1,0:T(8,128)(2,1)S(1)}, bf16[1,4,2,64,256]{4,3,2,1,0:T(8,128)(2,1)S(1)}, u32[]{:S(2)}, u32[]{:S(2)}) collective-permute-start(bf16[1,4,2,64,256]{4,3,2,1,0:T(8,128)(2,1)S(1)} %get-tuple-element.62), channel_id=1, source_target_pairs={{0,64},{32,96},{64,0},{96,32},{128,192},{160,224},{192,128},{224,1... | collective-permute-start | bytes 786440 | tf_op jit(solution)/shard_map/ppermute | solution.py:447
  53.5 1.0 copy-start.2
  58.7 0.7 copy-start
  59.4 25.5 %collective-permute-start.8 = (bf16[4,4,2,64,256]{4,3,2,1,0:T(8,128)(2,1)}, bf16[4,4,2,64,256]{4,3,2,1,0:T(8,128)(2,1)S(1)}, u32[]{:S(2)}, u32[]{:S(2)}) collective-permute-start(bf16[4,4,2,64,256]{4,3,2,1,0:T(8,128)(2,1)} %get-tuple-element.43), channel_id=1, source_target_pairs={{0,128},{32,160},{64,192},{96,224},{128,0},{160,32},{192,64},{224,... | collective-permute-start | bytes 3145736 | tf_op jit(solution)/shard_map/ppermute | solution.py:451
  64.1 20.3 %collective-permute-start.9 = (bf16[1,4,2,64,256]{4,3,2,1,0:T(8,128)(2,1)}, bf16[1,4,2,64,256]{4,3,2,1,0:T(8,128)(2,1)S(1)}, u32[]{:S(2)}, u32[]{:S(2)}) collective-permute-start(bf16[1,4,2,64,256]{4,3,2,1,0:T(8,128)(2,1)} %get-tuple-element.44), channel_id=1, source_target_pairs={{0,96},{32,0},{64,32},{96,64},{128,224},{160,128},{192,160},{224,1... | collective-permute-start | bytes 786440 | tf_op jit(solution)/shard_map/ppermute | solution.py:447
  64.1 20.3 %collective-permute-start.10 = (bf16[1,4,2,64,256]{4,3,2,1,0:T(8,128)(2,1)}, bf16[1,4,2,64,256]{4,3,2,1,0:T(8,128)(2,1)}, u32[]{:S(2)}, u32[]{:S(2)}) collective-permute-start(bf16[1,4,2,64,256]{4,3,2,1,0:T(8,128)(2,1)} %get-tuple-element.45), channel_id=1, source_target_pairs={{0,32},{32,64},{64,96},{96,0},{128,160},{160,192},{192,224},{224,1... | collective-permute-start | bytes 786440 | tf_op jit(solution)/shard_map/ppermute | solution.py:447
  66.1 18.3 %collective-permute-start.11 = (bf16[1,4,2,64,256]{4,3,2,1,0:T(8,128)(2,1)}, bf16[1,4,2,64,256]{4,3,2,1,0:T(8,128)(2,1)}, u32[]{:S(2)}, u32[]{:S(2)}) collective-permute-start(bf16[1,4,2,64,256]{4,3,2,1,0:T(8,128)(2,1)} %get-tuple-element.46), channel_id=1, source_target_pairs={{0,64},{32,96},{64,0},{96,32},{128,192},{160,224},{192,128},{224,1... | collective-permute-start | bytes 786440 | tf_op jit(solution)/shard_map/ppermute | solution.py:447
  84.9 60.9 %all-to-all-start.1 = ((bf16[32,256,128]{2,1,0:T(8,128)(2,1)}), bf16[32,256,128]{2,1,0:T(8,128)(2,1)S(1)}, u32[]{:S(2)}, u32[]{:S(2)}) async-start(bf16[32,256,128]{2,1,0:T(8,128)(2,1)} %bitcast.2), calls=%async_computation.1 | async-start | bytes 4194304 | tf_op jit(solution)/shard_map/all_to_all | solution.py:443
  94.7 29.5 %collective-permute-start.17 = (bf16[1,4,2,64,256]{4,3,2,1,0:T(8,128)(2,1)S(1)}, bf16[1,4,2,64,256]{4,3,2,1,0:T(8,128)(2,1)S(1)}, u32[]{:S(2)}, u32[]{:S(2)}) collective-permute-start(bf16[1,4,2,64,256]{4,3,2,1,0:T(8,128)(2,1)S(1)} %get-tuple-element.61), channel_id=1, source_target_pairs={{0,96},{32,0},{64,32},{96,64},{128,224},{160,128},{192,160},{224,1... | collective-permute-start | bytes 786440 | tf_op jit(solution)/shard_map/ppermute | solution.py:447
  94.8 29.5 %collective-permute-start.18 = (bf16[1,4,2,64,256]{4,3,2,1,0:T(8,128)(2,1)S(1)}, bf16[1,4,2,64,256]{4,3,2,1,0:T(8,128)(2,1)S(1)}, u32[]{:S(2)}, u32[]{:S(2)}) collective-permute-start(bf16[1,4,2,64,256]{4,3,2,1,0:T(8,128)(2,1)S(1)} %get-tuple-element.60), channel_id=1, source_target_pairs={{0,32},{32,64},{64,96},{96,0},{128,160},{160,192},{192,224},{224,1... | collective-permute-start | bytes 786440 | tf_op jit(solution)/shard_map/ppermute | solution.py:447
  96.8 27.5 %collective-permute-start.19 = (bf16[1,4,2,64,256]{4,3,2,1,0:T(8,128)(2,1)S(1)}, bf16[1,4,2,64,256]{4,3,2,1,0:T(8,128)(2,1)S(1)}, u32[]{:S(2)}, u32[]{:S(2)}) collective-permute-start(bf16[1,4,2,64,256]{4,3,2,1,0:T(8,128)(2,1)S(1)} %get-tuple-element.59), channel_id=1, source_target_pairs={{0,64},{32,96},{64,0},{96,32},{128,192},{160,224},{192,128},{224,1... | collective-permute-start | bytes 786440 | tf_op jit(solution)/shard_map/ppermute | solution.py:447
  99.0 10.1 %collective-permute-start.12 = (f32[4,128]{1,0:T(4,128)S(1)}, f32[4,128]{1,0:T(4,128)S(1)}, u32[]{:S(2)}, u32[]{:S(2)}) collective-permute-start(f32[4,128]{1,0:T(4,128)S(1)} %get-tuple-element.47), channel_id=1, source_target_pairs={{0,32},{32,0},{64,96},{96,64},{128,160},{160,128},{192,224},{224,1... | collective-permute-start | bytes 6152 | tf_op jit(solution)/shard_map/ppermute | solution.py:460
  109.1 5.1 %collective-permute-start.13 = (f32[4,128]{1,0:T(4,128)S(1)}, f32[4,128]{1,0:T(4,128)S(1)}, u32[]{:S(2)}, u32[]{:S(2)}) collective-permute-start(f32[4,128]{1,0:T(4,128)S(1)} %add.29), channel_id=1, source_target_pairs={{0,64},{32,96},{64,0},{96,32},{128,192},{160,224},{192,128},{224,1... | collective-permute-start | bytes 6152 | tf_op jit(solution)/shard_map/ppermute | solution.py:460
  114.2 5.1 %collective-permute-start.14 = (f32[4,128]{1,0:T(4,128)S(1)}, f32[4,128]{1,0:T(4,128)S(1)}, u32[]{:S(2)}, u32[]{:S(2)}) collective-permute-start(f32[4,128]{1,0:T(4,128)S(1)} %add.30), channel_id=1, source_target_pairs={{0,128},{32,160},{64,192},{96,224},{128,0},{160,32},{192,64},{224,... | collective-permute-start | bytes 6152 | tf_op jit(solution)/shard_map/ppermute | solution.py:460
  119.3 1.2 collective-permute-start.15
  120.5 3.7 %collective-permute-start.16 = (f32[4,128]{1,0:T(4,128)S(1)}, f32[4,128]{1,0:T(4,128)S(1)}, u32[]{:S(2)}, u32[]{:S(2)}) collective-permute-start(f32[4,128]{1,0:T(4,128)S(1)} %add.32), channel_id=1, source_target_pairs={{0,2},{1,3},{2,0},{3,1},{4,6},{5,7},{6,4},{7,5},{8,10},{9,11},{10,... | collective-permute-start | bytes 6152 | tf_op jit(solution)/shard_map/ppermute | solution.py:460
  124.2 1.0 copy-start.1
  127.6 13.3 %collective-permute-start.22 = (f32[4,128]{1,0:T(4,128)S(1)}, f32[4,128]{1,0:T(4,128)S(1)}, u32[]{:S(2)}, u32[]{:S(2)}) collective-permute-start(f32[4,128]{1,0:T(4,128)S(1)} %get-tuple-element.49), channel_id=1, source_target_pairs={{1,25},{3,27},{5,29},{7,31},{9,17},{11,19},{13,21},{15,23},{17,9},... | collective-permute-start | bytes 6152 | tf_op jit(solution)/shard_map/ppermute | solution.py:475
  130.0 10.9 %collective-permute-start.23 = (f32[4,128]{1,0:T(4,128)S(1)}, f32[4,128]{1,0:T(4,128)S(1)}, u32[]{:S(2)}, u32[]{:S(2)}) collective-permute-start(f32[4,128]{1,0:T(4,128)S(1)} %get-tuple-element.49), channel_id=1, source_target_pairs={{1,29},{3,31},{5,25},{7,27},{9,21},{11,23},{13,17},{15,19},{17,13}... | collective-permute-start | bytes 6152 | tf_op jit(solution)/shard_map/ppermute | solution.py:475
  131.5 11.1 %collective-permute-start.21 = (f32[4,128]{1,0:T(4,128)S(1)}, f32[4,128]{1,0:T(4,128)S(1)}, u32[]{:S(2)}, u32[]{:S(2)}) collective-permute-start(f32[4,128]{1,0:T(4,128)S(1)} %get-tuple-element.49), channel_id=1, source_target_pairs={{1,21},{3,23},{5,17},{7,19},{9,29},{11,31},{13,25},{15,27},{17,5},... | collective-permute-start | bytes 6152 | tf_op jit(solution)/shard_map/ppermute | solution.py:475
  131.6 11.0 %collective-permute-start.20 = (f32[4,128]{1,0:T(4,128)S(1)}, f32[4,128]{1,0:T(4,128)S(1)}, u32[]{:S(2)}, u32[]{:S(2)}) collective-permute-start(f32[4,128]{1,0:T(4,128)S(1)} %get-tuple-element.49), channel_id=1, source_target_pairs={{1,17},{3,19},{5,21},{7,23},{9,25},{11,27},{13,29},{15,31},{17,1},... | collective-permute-start | bytes 6152 | tf_op jit(solution)/shard_map/ppermute | solution.py:475
  142.6 3.2 %collective-permute-start.24 = (f32[4,128]{1,0:T(4,128)S(1)}, f32[4,128]{1,0:T(4,128)S(1)}, u32[]{:S(2)}, u32[]{:S(2)}) collective-permute-start(f32[4,128]{1,0:T(4,128)S(1)} %add_add_fusion.half_ref), channel_id=1, source_target_pairs={{0,1},{1,0},{2,3},{3,2},{4,5},{5,4},{6,7},{7,6},{8,9},{9,8},{10,11... | collective-permute-start | bytes 6152 | tf_op jit(solution)/shard_map/ppermute | solution.py:460

commit v3 on v2

--- a/solution.py
+++ b/solution.py
@@ -64,8 +64,8 @@
 
 
 def pack_kernel(*refs):
-    far, near, there_refs, sent_ref = refs[:4], refs[4:8], refs[8:10], refs[10]
-    far_in, near_in, there, sent, sem_far, sem_near, sem_there, sem_sent = refs[11:]
+    far, near, there_ref, sent_ref = refs[:4], refs[4:8], refs[8], refs[9]
+    far_in, near_in, there, sent, sem_far, sem_near, sem_there, sem_sent = refs[10:]
     frames, places, half = far_in.shape[1:]
     part = half // 4
     lanes = row_lanes(True, half)
@@ -76,9 +76,8 @@
     def fetch_near(a, f):
         return pltpu.make_async_copy(near[a].at[f], near_in.at[a, f], sem_near.at[a, f])
 
-    def send_there(a, i):
-        pair = pl.ds(2 * i, 2)
-        return pltpu.make_async_copy(there.at[pair, a], there_refs[i].at[:, a], sem_there.at[a, i])
+    def send_there(a):
+        return pltpu.make_async_copy(there.at[:, a], there_ref.at[:, a], sem_there.at[a])
 
     def send_sent(a, f):
         heads = pl.ds(f * HEADS, HEADS)
@@ -92,10 +91,9 @@
     spans = places_of_x(part)
     for a in range(4):
         fetch_far(a).wait()
-        for i, span in enumerate(spans):
+        for i, span in enumerate(spans[1:]):
             there[i, a] = far_in[a, :, :, span]
-        for i in range(2):
-            send_there(a, i).start()
+        send_there(a).start()
     for a in range(4):
         for f in range(frames):
             fetch_near(a, f).wait()
@@ -103,22 +101,21 @@
                 sent[f * HEADS + h, a] = near_in[a, f, :, h * HEAD_DIM : (h + 1) * HEAD_DIM]
             send_sent(a, f).start()
     for a in range(4):
-        for i in range(2):
-            send_there(a, i).wait()
+        send_there(a).wait()
         for f in range(frames):
             send_sent(a, f).wait()
 
 
 def pack(far, near):
     frames, places, width = near[0].shape
-    there = (4, 4, frames, places, width // 8)
+    there = (3, 4, frames, places, width // 8)
     sent = (frames * HEADS, 4, places, HEAD_DIM)
     anywhere = pl.BlockSpec(memory_space=pl.ANY)
     return pl.pallas_call(
         pack_kernel,
-        out_shape=[jax.ShapeDtypeStruct((2, *there[1:]), BF16)] * 2 + [jax.ShapeDtypeStruct(sent, BF16)],
+        out_shape=[jax.ShapeDtypeStruct(there, BF16)] + [jax.ShapeDtypeStruct(sent, BF16)],
         in_specs=[anywhere] * 8,
-        out_specs=[anywhere] * 3,
+        out_specs=[anywhere] * 2,
         scratch_shapes=[
             pltpu.VMEM((4, frames, places, width // 2), BF16),
             pltpu.VMEM((4, frames, places, width), BF16),
@@ -126,7 +123,7 @@
             pltpu.VMEM(sent, BF16),
             pltpu.SemaphoreType.DMA((4,)),
             pltpu.SemaphoreType.DMA((4, frames)),
-            pltpu.SemaphoreType.DMA((4, 2)),
+            pltpu.SemaphoreType.DMA((4,)),
             pltpu.SemaphoreType.DMA((4, frames)),
         ],
         compiler_params=params(60),
@@ -136,29 +133,42 @@
 
 
 def pack_here_kernel(q_ref, k_ref, v_ref, d_ref, *refs):
-    outs, held, sem = refs[:4], refs[4], refs[5]
+    outs, far_out, held, sem, sem_far = refs[:4], refs[4], refs[5], refs[6], refs[7]
     lanes = row_lanes(False, held.shape[-1])
+    part = held.shape[-1] // 4
+    row, x = lax.div(lax.axis_index("frame"), 4), lax.rem(lax.axis_index("frame"), 4)
+    far = pl.ds(pl.multiple_of(((1 - row) * 4 + x) * part, part), part)
     copies = [
         pltpu.make_async_copy(ref.at[:, :, lanes], held.at[a], sem.at[a])
         for a, ref in enumerate((q_ref, k_ref, v_ref, d_ref))
     ]
-    for copy in copies:
+    far_copies = [
+        pltpu.make_async_copy(ref.at[:, :, far], far_out.at[0, a], sem_far.at[a])
+        for a, ref in enumerate((q_ref, k_ref, v_ref, d_ref))
+    ]
+    for copy in copies + far_copies:
         copy.start()
-    spans = places_of_x(held.shape[-1] // 4)
+    spans = places_of_x(part)
     for a, copy in enumerate(copies):
         copy.wait()
         for out, span in zip(outs, spans):
             out[0, a] = held[a, :, :, span]
+    for copy in far_copies:
+        copy.wait()
 
 
 def pack_here(arrays):
     frames, places, width = arrays[0].shape
     return pl.pallas_call(
         pack_here_kernel,
-        out_shape=[jax.ShapeDtypeStruct((1, 4, frames, places, width // 8), BF16)] * 4,
+        out_shape=[jax.ShapeDtypeStruct((1, 4, frames, places, width // 8), BF16)] * 5,
         in_specs=[pl.BlockSpec(memory_space=pl.ANY)] * 4,
-        out_specs=[pl.BlockSpec(memory_space=pltpu.VMEM)] * 4,
-        scratch_shapes=[pltpu.VMEM((4, frames, places, width // 2), BF16), pltpu.SemaphoreType.DMA((4,))],
+        out_specs=[pl.BlockSpec(memory_space=pltpu.VMEM)] * 5,
+        scratch_shapes=[
+            pltpu.VMEM((4, frames, places, width // 2), BF16),
+            pltpu.SemaphoreType.DMA((4,)),
+            pltpu.SemaphoreType.DMA((4,)),
+        ],
         compiler_params=params(56),
         cost_estimate=cost(0, 2 << 20),
         name="pack_here",
@@ -224,7 +234,7 @@
     ins = [ref.at[0] for ref in refs[:8]]
     own, there, here, dgain_ref = refs[8], refs[9], refs[10:13], refs[13]
     there = [there.at[i] for i in range(4)]
-    outs = [own.at[0], there[0]] + [ref.at[0] for ref in here] + there[1:]
+    outs = [own.at[0]] + [ref.at[0] for ref in here] + there[1:] + there[:1]
     _, frames, places, width = ins[0].shape
     rows = 8 * frames * 16
     gain_q, gain_k = gains_ref[2:3, :], gains_ref[3:4, :]
@@ -451,10 +461,6 @@
     return lax.ppermute(x, "frame", [(i, (i + 4) % 8) for i in range(8)])
 
 
-def three_of(there):
-    return [there[0][1:], there[1][:1], there[1][1:]]
-
-
 def from_partner(x, axis, bit):
     size = 8 if axis == "frame" else 32
     return lax.ppermute(x, axis, [(i, i ^ bit) for i in range(size)])
@@ -482,15 +488,15 @@
     frames = query_s.shape[0]
     given_t = (query_t, key_t, value_t, grad_out_t)
 
-    *there, sent = pack(given_t, (query_s, key_s, value_s, grad_out_s))
-    there = [across(pair) for pair in there]
+    onward, sent = pack(given_t, (query_s, key_s, value_s, grad_out_s))
+    onward = across(onward)
     items = over_tile(sent)
-    here = pack_here(given_t)
-    parts = [here[0], there[0]]
-    for part, step in zip(here[1:], XSTEPS):
-        parts.append(along_x(part, step))
-    for part, step in zip(three_of(there), XSTEPS):
-        parts.append(along_x(part, step))
+    *here, there = pack_here(given_t)
+    here = [here[0]] + [along_x(part, step) for part, step in zip(here[1:], XSTEPS)]
+    parts = here
+    for i, step in enumerate(XSTEPS):
+        parts.append(along_x(onward[i : i + 1], step))
+    parts.append(across(there))
 
     own, there, here, grads_t = temporal(gains, parts)
     there = across(there)

time: 149 us -> 145 us (0.973)
  waiting for transfers between devices: 55.2 us -> 50.8 us
    all_to_all x2, waiting for transfers between devices: 0.01 us -> 5.92 us  [over_tile(): lax.all_to_all(x, 'tile', split_axis=0, concat_axis=0, tiled=True)]
    ppermute x12, waiting for transfers between devices: 7.95 us -> 2.85 us  [along_x(): lax.ppermute(x, 'frame', [(i, i // 4 * 4 + (i + step) % 4) for i in range...]
    ppermute x3, waiting for transfers between devices: 16.7 us -> 13.2 us  [across(): return lax.ppermute(x, 'frame', [(i, (i + 4) % 8) for i in range(8)])]
    all_to_all x2, starting transfers between devices: 19.6 us -> 17.5 us  [over_tile(): lax.all_to_all(x, 'tile', split_axis=0, concat_axis=0, tiled=True)]
where the time goes in v3:
time: 145 us; the launch traced here: 144 us
  starting transfers between devices  59.3 us (41%)
  waiting for transfers between devices  50.8 us (35%)
  Pallas kernels  29.3 us (20%)
  local copies, waits for them, and re-layouts  3.83 us (3%)
    ppermute x6, waiting for transfers between devices, from_partner(): return lax.ppermute(x, axis, [(i, i ^ bit) for i in range(size)])  19.7 us
    ppermute x12, starting transfers between devices, along_x(): lax.ppermute(x, 'frame', [(i, i // 4 * 4 + (i + step) % 4) for i in range...  19.5 us
    all_to_all x2, starting transfers between devices, over_tile(): lax.all_to_all(x, 'tile', split_axis=0, concat_axis=0, tiled=True)  17.5 us
    pallas_call x1, Pallas kernels, spatial(): pl.pallas_call(spatial_kernel, out_shape=[jax.ShapeDtypeStruct(x.shape, B...  14.6 us
    ppermute x3, waiting for transfers between devices, across(): return lax.ppermute(x, 'frame', [(i, (i + 4) % 8) for i in range(8)])  13.2 us
    ppermute x6, starting transfers between devices, from_partner(): return lax.ppermute(x, axis, [(i, i ^ bit) for i in range(size)])  9.4 us
    ppermute x4, waiting for transfers between devices, total_z(): got.append(lax.ppermute(x, 'tile', perm))  9.15 us
    ppermute x3, starting transfers between devices, across(): return lax.ppermute(x, 'frame', [(i, (i + 4) % 8) for i in range(8)])  8.07 us
  transfers between devices with their start and end apart: 27, of which 12 were waited for; matrix products, arithmetic and copies ran while one was open for 1% of the time, Pallas kernels for 16%

profile of v3, /device:TPU:2, one launch (start us, length us, event | category | flops | bytes accessed | tf_op | source)
XLA Modules:
  0.0 144.2 jit_solution(16484500456351932605)
XLA Ops:
  0.6 3.4 %pack.1 = (bf16[3,4,2,64,256]{4,3,2,1,0:T(8,128)(2,1)}, bf16[32,4,64,128]{3,2,1,0:T(8,128)(2,1)}) custom-call(bf16[2,64,2048]{2,1,0:T(8,128)(2,1)} %refs_0_.1, bf16[2,64,2048]{2,1,0:T(8,128)(2,1)} %refs_1_.1, bf16[2,64,2048]{2,1,0:T(8,128)(2,1)} %refs_2_.1, bf16[2,64,2048]{2,1,0:T(8,128)(2,1)} %refs_3_.1, bf16[2,64,2048]{2,1,0:T(8,128)(2,1)} %refs_4_.1, ...), custom_call_target="tpu_custom_call" | custom-call | bytes 6291456 | tf_op jit(solution)/shard_map/pack/pallas_call | solution.py:114
  4.1 3.3 %collective-permute-start.3 = (bf16[3,4,2,64,256]{4,3,2,1,0:T(8,128)(2,1)}, bf16[3,4,2,64,256]{4,3,2,1,0:T(8,128)(2,1)}, u32[]{:S(2)}, u32[]{:S(2)}) collective-permute-start(bf16[3,4,2,64,256]{4,3,2,1,0:T(8,128)(2,1)} %get-tuple-element.38), channel_id=1, source_target_pairs={{0,128},{32,160},{64,192},{96,224},{128,0},{160,32},{192,64},{224,... | collective-permute-start | bytes 2359304 | tf_op jit(solution)/shard_map/ppermute | solution.py:461
  7.3 9.0 %all-to-all-start = ((bf16[32,256,128]{2,1,0:T(8,128)(2,1)}), bf16[32,256,128]{2,1,0:T(8,128)(2,1)S(1)}, u32[]{:S(2)}, u32[]{:S(2)}) async-start(bf16[32,256,128]{2,1,0:T(8,128)(2,1)} %bitcast.6), calls=%async_computation | async-start | bytes 4194304 | tf_op jit(solution)/shard_map/all_to_all | solution.py:453
  16.3 0.0 copy-start.3
  16.3 2.4 %pack_here.1 = (bf16[1,4,2,64,256]{4,3,2,1,0:T(8,128)(2,1)}, bf16[1,4,2,64,256]{4,3,2,1,0:T(8,128)(2,1)}, bf16[1,4,2,64,256]{4,3,2,1,0:T(8,128)(2,1)}, bf16[1,4,...) custom-call(bf16[2,64,2048]{2,1,0:T(8,128)(2,1)} %refs_0_.1, bf16[2,64,2048]{2,1,0:T(8,128)(2,1)} %refs_1_.1, ...), custom_call_target="tpu_custom_call" | custom-call | bytes 2097152 | tf_op jit(solution)/shard_map/pack_here/pallas_call | solution.py:162
  18.8 1.6 %collective-permute-start = (bf16[1,4,2,64,256]{4,3,2,1,0:T(8,128)(2,1)}, bf16[1,4,2,64,256]{4,3,2,1,0:T(8,128)(2,1)S(1)}, u32[]{:S(2)}, u32[]{:S(2)}) collective-permute-start(bf16[1,4,2,64,256]{4,3,2,1,0:T(8,128)(2,1)} %get-tuple-element.35), channel_id=1, source_target_pairs={{0,32},{32,64},{64,96},{96,0},{128,160},{160,192},{192,224},{224,1... | collective-permute-start | bytes 786440 | tf_op jit(solution)/shard_map/ppermute | solution.py:457
  20.3 0.5 collective-permute-start.1
  20.9 2.1 %collective-permute-start.2 = (bf16[1,4,2,64,256]{4,3,2,1,0:T(8,128)(2,1)}, bf16[1,4,2,64,256]{4,3,2,1,0:T(8,128)(2,1)S(1)}, u32[]{:S(2)}, u32[]{:S(2)}) collective-permute-start(bf16[1,4,2,64,256]{4,3,2,1,0:T(8,128)(2,1)} %get-tuple-element.37), channel_id=1, source_target_pairs={{0,64},{32,96},{64,0},{96,32},{128,192},{160,224},{192,128},{224,1... | collective-permute-start | bytes 786440 | tf_op jit(solution)/shard_map/ppermute | solution.py:457
  23.0 1.8 %collective-permute-start.7 = (bf16[1,4,2,64,256]{4,3,2,1,0:T(8,128)(2,1)}, bf16[1,4,2,64,256]{4,3,2,1,0:T(8,128)(2,1)S(1)}, u32[]{:S(2)}, u32[]{:S(2)}) collective-permute-start(bf16[1,4,2,64,256]{4,3,2,1,0:T(8,128)(2,1)} %get-tuple-element.39), channel_id=1, source_target_pairs={{0,128},{32,160},{64,192},{96,224},{128,0},{160,32},{192,64},{224,... | collective-permute-start | bytes 786440 | tf_op jit(solution)/shard_map/ppermute | solution.py:461
  24.8 8.9 %collective-permute-done.3 = bf16[3,4,2,64,256]{4,3,2,1,0:T(8,128)(2,1)} collective-permute-done((bf16[3,4,2,64,256]{4,3,2,1,0:T(8,128)(2,1)}, bf16[3,4,2,64,256]{4,3,2,1,0:T(8,128)(2,1)}, u32[]{:S(2)}, u32[]{:S(2)}) %collective-permute-start.3) | collective-permute-done | bytes 786464 | tf_op jit(solution)/shard_map/ppermute | solution.py:461
  33.8 1.2 fusion.1
  35.0 1.6 %collective-permute-start.4 = (bf16[1,4,2,64,256]{4,3,2,1,0:T(8,128)(2,1)S(1)}, bf16[1,4,2,64,256]{4,3,2,1,0:T(8,128)(2,1)S(1)}, u32[]{:S(2)}, u32[]{:S(2)}) collective-permute-start(bf16[1,4,2,64,256]{4,3,2,1,0:T(8,128)(2,1)S(1)} %get-tuple-element.64), channel_id=1, source_target_pairs={{0,32},{32,64},{64,96},{96,0},{128,160},{160,192},{192,224},{224,1... | collective-permute-start | bytes 786440 | tf_op jit(solution)/shard_map/ppermute | solution.py:457
  36.5 0.0 collective-permute-done.refs_1_
  36.5 1.3 collective-permute-start.5
  37.8 0.0 collective-permute-done.1.refs_2_
  37.8 2.1 %collective-permute-start.6 = (bf16[1,4,2,64,256]{4,3,2,1,0:T(8,128)(2,1)S(1)}, bf16[1,4,2,64,256]{4,3,2,1,0:T(8,128)(2,1)S(1)}, u32[]{:S(2)}, u32[]{:S(2)}) collective-permute-start(bf16[1,4,2,64,256]{4,3,2,1,0:T(8,128)(2,1)S(1)} %get-tuple-element.62), channel_id=1, source_target_pairs={{0,64},{32,96},{64,0},{96,32},{128,192},{160,224},{192,128},{224,1... | collective-permute-start | bytes 786440 | tf_op jit(solution)/shard_map/ppermute | solution.py:457
  39.9 0.0 collective-permute-done.2.refs_3_
  39.9 4.2 %collective-permute-done.7.refs_7_ = bf16[1,4,2,64,256]{4,3,2,1,0:T(8,128)(2,1)S(1)} collective-permute-done((bf16[1,4,2,64,256]{4,3,2,1,0:T(8,128)(2,1)}, bf16[1,4,2,64,256]{4,3,2,1,0:T(8,128)(2,1)S(1)}, u32[]{:S(2)}, u32[]{:S(2)}) %collective-permute-start.7) | collective-permute-done | bytes 262176 | tf_op jit(solution)/shard_map/ppermute | solution.py:461
  44.1 0.0 collective-permute-done.4.refs_4_
  44.1 0.0 collective-permute-done.5.refs_5_
  44.1 2.8 %collective-permute-done.6.refs_6_ = bf16[1,4,2,64,256]{4,3,2,1,0:T(8,128)(2,1)S(1)} collective-permute-done((bf16[1,4,2,64,256]{4,3,2,1,0:T(8,128)(2,1)S(1)}, bf16[1,4,2,64,256]{4,3,2,1,0:T(8,128)(2,1)S(1)}, u32[]{:S(2)}, u32[]{:S(2)}) %collective-permute-start.6) | collective-permute-done | bytes 262176 | tf_op jit(solution)/shard_map/ppermute | solution.py:457
  46.9 0.9 copy-done.2
  47.9 4.3 %temporal_attention.1 = (bf16[1,4,2,64,256]{4,3,2,1,0:T(8,128)(2,1)S(1)}, bf16[4,4,2,64,256]{4,3,2,1,0:T(8,128)(2,1)}, bf16[1,4,2,64,256]{4,3,2,1,0:T(8,128)(2,1...) custom-call(f32[4,128]{1,0:T(4,128)S(1)} %copy-done.3, ...), custom_call_target="tpu_custom_call" | custom-call | flops 30000001024 | bytes 4194304 | tf_op jit(solution)/shard_map/temporal_attention/pallas_call | solution.py:307
  52.1 0.7 copy-done
  52.8 3.0 %collective-permute-start.8 = (bf16[4,4,2,64,256]{4,3,2,1,0:T(8,128)(2,1)}, bf16[4,4,2,64,256]{4,3,2,1,0:T(8,128)(2,1)S(1)}, u32[]{:S(2)}, u32[]{:S(2)}) collective-permute-start(bf16[4,4,2,64,256]{4,3,2,1,0:T(8,128)(2,1)} %get-tuple-element.43), channel_id=1, source_target_pairs={{0,128},{32,160},{64,192},{96,224},{128,0},{160,32},{192,64},{224,... | collective-permute-start | bytes 3145736 | tf_op jit(solution)/shard_map/ppermute | solution.py:461
  55.8 0.7 collective-permute-start.9
  56.5 1.3 collective-permute-start.10
  57.8 2.9 %collective-permute-start.11 = (bf16[1,4,2,64,256]{4,3,2,1,0:T(8,128)(2,1)}, bf16[1,4,2,64,256]{4,3,2,1,0:T(8,128)(2,1)}, u32[]{:S(2)}, u32[]{:S(2)}) collective-permute-start(bf16[1,4,2,64,256]{4,3,2,1,0:T(8,128)(2,1)} %get-tuple-element.46), channel_id=1, source_target_pairs={{0,64},{32,96},{64,0},{96,32},{128,192},{160,224},{192,128},{224,1... | collective-permute-start | bytes 786440 | tf_op jit(solution)/shard_map/ppermute | solution.py:457
  60.7 5.9 %all-to-all-done = bf16[32,256,128]{2,1,0:T(8,128)(2,1)S(1)} async-done(((bf16[32,256,128]{2,1,0:T(8,128)(2,1)}), bf16[32,256,128]{2,1,0:T(8,128)(2,1)S(1)}, u32[]{:S(2)}, u32[]{:S(2)}) %all-to-all-start) | async-done | bytes 2097184 | tf_op jit(solution)/shard_map/all_to_all | solution.py:453
  66.6 14.6 %spatial_attention.1 = (bf16[32,4,64,128]{3,2,1,0:T(8,128)(2,1)}, f32[4,128]{1,0:T(4,128)S(1)}) custom-call(f32[4,128]{1,0:T(4,128)S(1)} %copy-done.3, f32[2,128]{1,0:T(2,128)S(1)} %get-tuple-element.40.grads_t_ref, bf16[32,4,64,128]{3,2,1,0:T(8,128)(2,1)S(1)} %bitcast.5), custom_call_target="tpu_custom_call" | custom-call | flops 6442450944 | bytes 4194304 | tf_op jit(solution)/shard_map/spatial_attention/pallas_call | solution.py:407
  81.3 0.0 collective-permute-done.9.refs_1_
  81.3 0.0 collective-permute-done.10.refs_2_
  81.3 0.0 collective-permute-done.11.refs_3_
  81.3 0.0 collective-permute-done.8.refs_0_.refs_4_
  81.3 8.5 %all-to-all-start.1 = ((bf16[32,256,128]{2,1,0:T(8,128)(2,1)}), bf16[32,256,128]{2,1,0:T(8,128)(2,1)S(1)}, u32[]{:S(2)}, u32[]{:S(2)}) async-start(bf16[32,256,128]{2,1,0:T(8,128)(2,1)} %bitcast.2), calls=%async_computation.1 | async-start | bytes 4194304 | tf_op jit(solution)/shard_map/all_to_all | solution.py:453
  89.9 0.1 fusion
  89.9 0.6 collective-permute-start.17
  90.6 1.5 %collective-permute-start.18 = (bf16[1,4,2,64,256]{4,3,2,1,0:T(8,128)(2,1)S(1)}, bf16[1,4,2,64,256]{4,3,2,1,0:T(8,128)(2,1)S(1)}, u32[]{:S(2)}, u32[]{:S(2)}) collective-permute-start(bf16[1,4,2,64,256]{4,3,2,1,0:T(8,128)(2,1)S(1)} %get-tuple-element.60), channel_id=1, source_target_pairs={{0,32},{32,64},{64,96},{96,0},{128,160},{160,192},{192,224},{224,1... | collective-permute-start | bytes 786440 | tf_op jit(solution)/shard_map/ppermute | solution.py:457
  92.0 3.3 %collective-permute-start.19 = (bf16[1,4,2,64,256]{4,3,2,1,0:T(8,128)(2,1)S(1)}, bf16[1,4,2,64,256]{4,3,2,1,0:T(8,128)(2,1)S(1)}, u32[]{:S(2)}, u32[]{:S(2)}) collective-permute-start(bf16[1,4,2,64,256]{4,3,2,1,0:T(8,128)(2,1)S(1)} %get-tuple-element.59), channel_id=1, source_target_pairs={{0,64},{32,96},{64,0},{96,32},{128,192},{160,224},{192,128},{224,1... | collective-permute-start | bytes 786440 | tf_op jit(solution)/shard_map/ppermute | solution.py:457
  95.4 0.2 collective-permute-start.12
  95.6 9.8 %collective-permute-done.12 = f32[4,128]{1,0:T(4,128)S(1)} collective-permute-done((f32[4,128]{1,0:T(4,128)S(1)}, f32[4,128]{1,0:T(4,128)S(1)}, u32[]{:S(2)}, u32[]{:S(2)}) %collective-permute-start.12) | collective-permute-done | bytes 2080 | tf_op jit(solution)/shard_map/ppermute | solution.py:466
  105.4 1.4 %collective-permute-start.13 = (f32[4,128]{1,0:T(4,128)S(1)}, f32[4,128]{1,0:T(4,128)S(1)}, u32[]{:S(2)}, u32[]{:S(2)}) collective-permute-start(f32[4,128]{1,0:T(4,128)S(1)} %add.29), channel_id=1, source_target_pairs={{0,64},{32,96},{64,0},{96,32},{128,192},{160,224},{192,128},{224,1... | collective-permute-start | bytes 6152 | tf_op jit(solution)/shard_map/ppermute | solution.py:466
  106.9 3.6 %collective-permute-done.13 = f32[4,128]{1,0:T(4,128)S(1)} collective-permute-done((f32[4,128]{1,0:T(4,128)S(1)}, f32[4,128]{1,0:T(4,128)S(1)}, u32[]{:S(2)}, u32[]{:S(2)}) %collective-permute-start.13) | collective-permute-done | bytes 2080 | tf_op jit(solution)/shard_map/ppermute | solution.py:466
  110.5 2.8 %collective-permute-start.14 = (f32[4,128]{1,0:T(4,128)S(1)}, f32[4,128]{1,0:T(4,128)S(1)}, u32[]{:S(2)}, u32[]{:S(2)}) collective-permute-start(f32[4,128]{1,0:T(4,128)S(1)} %add.30), channel_id=1, source_target_pairs={{0,128},{32,160},{64,192},{96,224},{128,0},{160,32},{192,64},{224,... | collective-permute-start | bytes 6152 | tf_op jit(solution)/shard_map/ppermute | solution.py:466
  113.3 2.3 %collective-permute-done.14 = f32[4,128]{1,0:T(4,128)S(1)} collective-permute-done((f32[4,128]{1,0:T(4,128)S(1)}, f32[4,128]{1,0:T(4,128)S(1)}, u32[]{:S(2)}, u32[]{:S(2)}) %collective-permute-start.14) | collective-permute-done | bytes 2080 | tf_op jit(solution)/shard_map/ppermute | solution.py:466
  115.6 0.0 collective-permute-start.15
  115.6 1.2 collective-permute-done.15
  116.8 1.7 %collective-permute-start.16 = (f32[4,128]{1,0:T(4,128)S(1)}, f32[4,128]{1,0:T(4,128)S(1)}, u32[]{:S(2)}, u32[]{:S(2)}) collective-permute-start(f32[4,128]{1,0:T(4,128)S(1)} %add.32), channel_id=1, source_target_pairs={{0,2},{1,3},{2,0},{3,1},{4,6},{5,7},{6,4},{7,5},{8,10},{9,11},{10,... | collective-permute-start | bytes 6152 | tf_op jit(solution)/shard_map/ppermute | solution.py:466
  118.5 1.9 %collective-permute-done.16 = f32[4,128]{1,0:T(4,128)S(1)} collective-permute-done((f32[4,128]{1,0:T(4,128)S(1)}, f32[4,128]{1,0:T(4,128)S(1)}, u32[]{:S(2)}, u32[]{:S(2)}) %collective-permute-start.16) | collective-permute-done | bytes 2080 | tf_op jit(solution)/shard_map/ppermute | solution.py:466
  120.4 0.0 collective-permute-done.19.refs_7_
  120.4 0.0 copy-start.1
  120.4 0.9 copy-done.1
  121.4 2.5 %unpack_temporal.1 = (bf16[2,64,2048]{2,1,0:T(8,128)(2,1)}, bf16[2,64,2048]{2,1,0:T(8,128)(2,1)}, bf16[2,64,2048]{2,1,0:T(8,128)(2,1)}, bf16[2,64,2048]{2,1,0:T(8,128)(2,1)}, f32[4,128]{1,0:T(4,128)S(1)}) custom-call(f32[4,128]{1,0:T(4,128)S(1)} %add.33.grads_ref, bf16[1,4,2,64,256]{4,3,2,1,0:T(8,128)(2,1)S(1)} %copy-done.1, ...), custom_call_target="tpu_custom_call" | custom-call | bytes 4194304 | tf_op jit(solution)/shard_map/unpack_temporal/pallas_call | solution.py:220
  123.8 2.5 %collective-permute-start.22 = (f32[4,128]{1,0:T(4,128)S(1)}, f32[4,128]{1,0:T(4,128)S(1)}, u32[]{:S(2)}, u32[]{:S(2)}) collective-permute-start(f32[4,128]{1,0:T(4,128)S(1)} %get-tuple-element.49), channel_id=1, source_target_pairs={{1,25},{3,27},{5,29},{7,31},{9,17},{11,19},{13,21},{15,23},{17,9},... | collective-permute-start | bytes 6152 | tf_op jit(solution)/shard_map/ppermute | solution.py:481
  126.4 1.5 %collective-permute-start.23 = (f32[4,128]{1,0:T(4,128)S(1)}, f32[4,128]{1,0:T(4,128)S(1)}, u32[]{:S(2)}, u32[]{:S(2)}) collective-permute-start(f32[4,128]{1,0:T(4,128)S(1)} %get-tuple-element.49), channel_id=1, source_target_pairs={{1,29},{3,31},{5,25},{7,27},{9,21},{11,23},{13,17},{15,19},{17,13}... | collective-permute-start | bytes 6152 | tf_op jit(solution)/shard_map/ppermute | solution.py:481
  127.8 0.2 collective-permute-start.21
  128.0 0.6 collective-permute-start.20
  128.7 7.5 %collective-permute-done.22 = f32[4,128]{1,0:T(4,128)S(1)} collective-permute-done((f32[4,128]{1,0:T(4,128)S(1)}, f32[4,128]{1,0:T(4,128)S(1)}, u32[]{:S(2)}, u32[]{:S(2)}) %collective-permute-start.22) | collective-permute-done | bytes 2080 | tf_op jit(solution)/shard_map/ppermute | solution.py:481
  136.2 0.0 collective-permute-done.23
  136.2 1.6 %collective-permute-done.21 = f32[4,128]{1,0:T(4,128)S(1)} collective-permute-done((f32[4,128]{1,0:T(4,128)S(1)}, f32[4,128]{1,0:T(4,128)S(1)}, u32[]{:S(2)}, u32[]{:S(2)}) %collective-permute-start.21) | collective-permute-done | bytes 2080 | tf_op jit(solution)/shard_map/ppermute | solution.py:481
  137.9 3.3 %collective-permute-start.24 = (f32[4,128]{1,0:T(4,128)S(1)}, f32[4,128]{1,0:T(4,128)S(1)}, u32[]{:S(2)}, u32[]{:S(2)}) collective-permute-start(f32[4,128]{1,0:T(4,128)S(1)} %add_add_fusion.half_ref), channel_id=1, source_target_pairs={{0,1},{1,0},{2,3},{3,2},{4,5},{5,4},{6,7},{7,6},{8,9},{9,8},{10,11... | collective-permute-start | bytes 6152 | tf_op jit(solution)/shard_map/ppermute | solution.py:466
  141.2 0.8 collective-permute-done.24.other_ref
  142.0 0.0 all-to-all-done.1
  142.0 2.1 %unpack_spatial.1 = (bf16[2,64,2048]{2,1,0:T(8,128)(2,1)}, bf16[2,64,2048]{2,1,0:T(8,128)(2,1)}, bf16[2,64,2048]{2,1,0:T(8,128)(2,1)}, bf16[2,64,2048]{2,1,0:T(8,128)(2,1)}, f32[4,128]{1,0:T(4,128)}) custom-call(bf16[2,16,4,64,128]{4,3,2,1,0:T(8,128)(2,1)S(1)} %bitcast.4, f32[4,128]{1,0:T(4,128)S(1)} %add_add_fusion.half_ref, ...), custom_call_target="tpu_custom_call" | custom-call | bytes 4194304 | tf_op jit(solution)/shard_map/unpack_spatial/pallas_call | solution.py:191
  (13 shorter events, 0.0 us)
Async XLA Ops:
  4.1 29.7 %collective-permute-start.3 = (bf16[3,4,2,64,256]{4,3,2,1,0:T(8,128)(2,1)}, bf16[3,4,2,64,256]{4,3,2,1,0:T(8,128)(2,1)}, u32[]{:S(2)}, u32[]{:S(2)}) collective-permute-start(bf16[3,4,2,64,256]{4,3,2,1,0:T(8,128)(2,1)} %get-tuple-element.38), channel_id=1, source_target_pairs={{0,128},{32,160},{64,192},{96,224},{128,0},{160,32},{192,64},{224,... | collective-permute-start | bytes 2359304 | tf_op jit(solution)/shard_map/ppermute | solution.py:461
  7.3 59.3 %all-to-all-start = ((bf16[32,256,128]{2,1,0:T(8,128)(2,1)}), bf16[32,256,128]{2,1,0:T(8,128)(2,1)S(1)}, u32[]{:S(2)}, u32[]{:S(2)}) async-start(bf16[32,256,128]{2,1,0:T(8,128)(2,1)} %bitcast.6), calls=%async_computation | async-start | bytes 4194304 | tf_op jit(solution)/shard_map/all_to_all | solution.py:453
  16.3 30.6 %copy-start.3 = (f32[4,128]{1,0:T(4,128)S(1)}, f32[4,128]{1,0:T(4,128)}, u32[]{:S(2)}) copy-start(f32[4,128]{1,0:T(4,128)} %gains_ref.3) | copy-start | bytes 6148
  18.8 17.7 %collective-permute-start = (bf16[1,4,2,64,256]{4,3,2,1,0:T(8,128)(2,1)}, bf16[1,4,2,64,256]{4,3,2,1,0:T(8,128)(2,1)S(1)}, u32[]{:S(2)}, u32[]{:S(2)}) collective-permute-start(bf16[1,4,2,64,256]{4,3,2,1,0:T(8,128)(2,1)} %get-tuple-element.35), channel_id=1, source_target_pairs={{0,32},{32,64},{64,96},{96,0},{128,160},{160,192},{192,224},{224,1... | collective-permute-start | bytes 786440 | tf_op jit(solution)/shard_map/ppermute | solution.py:457
  20.3 17.5 %collective-permute-start.1 = (bf16[1,4,2,64,256]{4,3,2,1,0:T(8,128)(2,1)}, bf16[1,4,2,64,256]{4,3,2,1,0:T(8,128)(2,1)S(1)}, u32[]{:S(2)}, u32[]{:S(2)}) collective-permute-start(bf16[1,4,2,64,256]{4,3,2,1,0:T(8,128)(2,1)} %get-tuple-element.36), channel_id=1, source_target_pairs={{0,96},{32,0},{64,32},{96,64},{128,224},{160,128},{192,160},{224,1... | collective-permute-start | bytes 786440 | tf_op jit(solution)/shard_map/ppermute | solution.py:457
  20.9 19.0 %collective-permute-start.2 = (bf16[1,4,2,64,256]{4,3,2,1,0:T(8,128)(2,1)}, bf16[1,4,2,64,256]{4,3,2,1,0:T(8,128)(2,1)S(1)}, u32[]{:S(2)}, u32[]{:S(2)}) collective-permute-start(bf16[1,4,2,64,256]{4,3,2,1,0:T(8,128)(2,1)} %get-tuple-element.37), channel_id=1, source_target_pairs={{0,64},{32,96},{64,0},{96,32},{128,192},{160,224},{192,128},{224,1... | collective-permute-start | bytes 786440 | tf_op jit(solution)/shard_map/ppermute | solution.py:457
  23.0 21.1 %collective-permute-start.7 = (bf16[1,4,2,64,256]{4,3,2,1,0:T(8,128)(2,1)}, bf16[1,4,2,64,256]{4,3,2,1,0:T(8,128)(2,1)S(1)}, u32[]{:S(2)}, u32[]{:S(2)}) collective-permute-start(bf16[1,4,2,64,256]{4,3,2,1,0:T(8,128)(2,1)} %get-tuple-element.39), channel_id=1, source_target_pairs={{0,128},{32,160},{64,192},{96,224},{128,0},{160,32},{192,64},{224,... | collective-permute-start | bytes 786440 | tf_op jit(solution)/shard_map/ppermute | solution.py:461
  35.0 9.2 %collective-permute-start.4 = (bf16[1,4,2,64,256]{4,3,2,1,0:T(8,128)(2,1)S(1)}, bf16[1,4,2,64,256]{4,3,2,1,0:T(8,128)(2,1)S(1)}, u32[]{:S(2)}, u32[]{:S(2)}) collective-permute-start(bf16[1,4,2,64,256]{4,3,2,1,0:T(8,128)(2,1)S(1)} %get-tuple-element.64), channel_id=1, source_target_pairs={{0,32},{32,64},{64,96},{96,0},{128,160},{160,192},{192,224},{224,1... | collective-permute-start | bytes 786440 | tf_op jit(solution)/shard_map/ppermute | solution.py:457
  36.5 7.6 %collective-permute-start.5 = (bf16[1,4,2,64,256]{4,3,2,1,0:T(8,128)(2,1)S(1)}, bf16[1,4,2,64,256]{4,3,2,1,0:T(8,128)(2,1)S(1)}, u32[]{:S(2)}, u32[]{:S(2)}) collective-permute-start(bf16[1,4,2,64,256]{4,3,2,1,0:T(8,128)(2,1)S(1)} %get-tuple-element.63), channel_id=1, source_target_pairs={{0,96},{32,0},{64,32},{96,64},{128,224},{160,128},{192,160},{224,1... | collective-permute-start | bytes 786440 | tf_op jit(solution)/shard_map/ppermute | solution.py:457
  37.8 9.1 %collective-permute-start.6 = (bf16[1,4,2,64,256]{4,3,2,1,0:T(8,128)(2,1)S(1)}, bf16[1,4,2,64,256]{4,3,2,1,0:T(8,128)(2,1)S(1)}, u32[]{:S(2)}, u32[]{:S(2)}) collective-permute-start(bf16[1,4,2,64,256]{4,3,2,1,0:T(8,128)(2,1)S(1)} %get-tuple-element.62), channel_id=1, source_target_pairs={{0,64},{32,96},{64,0},{96,32},{128,192},{160,224},{192,128},{224,1... | collective-permute-start | bytes 786440 | tf_op jit(solution)/shard_map/ppermute | solution.py:457
  46.9 1.0 copy-start.2
  52.1 0.7 copy-start
  52.8 28.5 %collective-permute-start.8 = (bf16[4,4,2,64,256]{4,3,2,1,0:T(8,128)(2,1)}, bf16[4,4,2,64,256]{4,3,2,1,0:T(8,128)(2,1)S(1)}, u32[]{:S(2)}, u32[]{:S(2)}) collective-permute-start(bf16[4,4,2,64,256]{4,3,2,1,0:T(8,128)(2,1)} %get-tuple-element.43), channel_id=1, source_target_pairs={{0,128},{32,160},{64,192},{96,224},{128,0},{160,32},{192,64},{224,... | collective-permute-start | bytes 3145736 | tf_op jit(solution)/shard_map/ppermute | solution.py:461
  55.8 25.5 %collective-permute-start.9 = (bf16[1,4,2,64,256]{4,3,2,1,0:T(8,128)(2,1)}, bf16[1,4,2,64,256]{4,3,2,1,0:T(8,128)(2,1)S(1)}, u32[]{:S(2)}, u32[]{:S(2)}) collective-permute-start(bf16[1,4,2,64,256]{4,3,2,1,0:T(8,128)(2,1)} %get-tuple-element.44), channel_id=1, source_target_pairs={{0,96},{32,0},{64,32},{96,64},{128,224},{160,128},{192,160},{224,1... | collective-permute-start | bytes 786440 | tf_op jit(solution)/shard_map/ppermute | solution.py:457
  56.5 24.8 %collective-permute-start.10 = (bf16[1,4,2,64,256]{4,3,2,1,0:T(8,128)(2,1)}, bf16[1,4,2,64,256]{4,3,2,1,0:T(8,128)(2,1)}, u32[]{:S(2)}, u32[]{:S(2)}) collective-permute-start(bf16[1,4,2,64,256]{4,3,2,1,0:T(8,128)(2,1)} %get-tuple-element.45), channel_id=1, source_target_pairs={{0,32},{32,64},{64,96},{96,0},{128,160},{160,192},{192,224},{224,1... | collective-permute-start | bytes 786440 | tf_op jit(solution)/shard_map/ppermute | solution.py:457
  57.8 23.5 %collective-permute-start.11 = (bf16[1,4,2,64,256]{4,3,2,1,0:T(8,128)(2,1)}, bf16[1,4,2,64,256]{4,3,2,1,0:T(8,128)(2,1)}, u32[]{:S(2)}, u32[]{:S(2)}) collective-permute-start(bf16[1,4,2,64,256]{4,3,2,1,0:T(8,128)(2,1)} %get-tuple-element.46), channel_id=1, source_target_pairs={{0,64},{32,96},{64,0},{96,32},{128,192},{160,224},{192,128},{224,1... | collective-permute-start | bytes 786440 | tf_op jit(solution)/shard_map/ppermute | solution.py:457
  81.3 60.7 %all-to-all-start.1 = ((bf16[32,256,128]{2,1,0:T(8,128)(2,1)}), bf16[32,256,128]{2,1,0:T(8,128)(2,1)S(1)}, u32[]{:S(2)}, u32[]{:S(2)}) async-start(bf16[32,256,128]{2,1,0:T(8,128)(2,1)} %bitcast.2), calls=%async_computation.1 | async-start | bytes 4194304 | tf_op jit(solution)/shard_map/all_to_all | solution.py:453
  89.9 30.5 %collective-permute-start.17 = (bf16[1,4,2,64,256]{4,3,2,1,0:T(8,128)(2,1)S(1)}, bf16[1,4,2,64,256]{4,3,2,1,0:T(8,128)(2,1)S(1)}, u32[]{:S(2)}, u32[]{:S(2)}) collective-permute-start(bf16[1,4,2,64,256]{4,3,2,1,0:T(8,128)(2,1)S(1)} %get-tuple-element.61), channel_id=1, source_target_pairs={{0,96},{32,0},{64,32},{96,64},{128,224},{160,128},{192,160},{224,1... | collective-permute-start | bytes 786440 | tf_op jit(solution)/shard_map/ppermute | solution.py:457
  90.6 29.8 %collective-permute-start.18 = (bf16[1,4,2,64,256]{4,3,2,1,0:T(8,128)(2,1)S(1)}, bf16[1,4,2,64,256]{4,3,2,1,0:T(8,128)(2,1)S(1)}, u32[]{:S(2)}, u32[]{:S(2)}) collective-permute-start(bf16[1,4,2,64,256]{4,3,2,1,0:T(8,128)(2,1)S(1)} %get-tuple-element.60), channel_id=1, source_target_pairs={{0,32},{32,64},{64,96},{96,0},{128,160},{160,192},{192,224},{224,1... | collective-permute-start | bytes 786440 | tf_op jit(solution)/shard_map/ppermute | solution.py:457
  92.0 28.4 %collective-permute-start.19 = (bf16[1,4,2,64,256]{4,3,2,1,0:T(8,128)(2,1)S(1)}, bf16[1,4,2,64,256]{4,3,2,1,0:T(8,128)(2,1)S(1)}, u32[]{:S(2)}, u32[]{:S(2)}) collective-permute-start(bf16[1,4,2,64,256]{4,3,2,1,0:T(8,128)(2,1)S(1)} %get-tuple-element.59), channel_id=1, source_target_pairs={{0,64},{32,96},{64,0},{96,32},{128,192},{160,224},{192,128},{224,1... | collective-permute-start | bytes 786440 | tf_op jit(solution)/shard_map/ppermute | solution.py:457
  95.4 10.1 %collective-permute-start.12 = (f32[4,128]{1,0:T(4,128)S(1)}, f32[4,128]{1,0:T(4,128)S(1)}, u32[]{:S(2)}, u32[]{:S(2)}) collective-permute-start(f32[4,128]{1,0:T(4,128)S(1)} %get-tuple-element.47), channel_id=1, source_target_pairs={{0,32},{32,0},{64,96},{96,64},{128,160},{160,128},{192,224},{224,1... | collective-permute-start | bytes 6152 | tf_op jit(solution)/shard_map/ppermute | solution.py:466
  105.4 5.1 %collective-permute-start.13 = (f32[4,128]{1,0:T(4,128)S(1)}, f32[4,128]{1,0:T(4,128)S(1)}, u32[]{:S(2)}, u32[]{:S(2)}) collective-permute-start(f32[4,128]{1,0:T(4,128)S(1)} %add.29), channel_id=1, source_target_pairs={{0,64},{32,96},{64,0},{96,32},{128,192},{160,224},{192,128},{224,1... | collective-permute-start | bytes 6152 | tf_op jit(solution)/shard_map/ppermute | solution.py:466
  110.5 5.1 %collective-permute-start.14 = (f32[4,128]{1,0:T(4,128)S(1)}, f32[4,128]{1,0:T(4,128)S(1)}, u32[]{:S(2)}, u32[]{:S(2)}) collective-permute-start(f32[4,128]{1,0:T(4,128)S(1)} %add.30), channel_id=1, source_target_pairs={{0,128},{32,160},{64,192},{96,224},{128,0},{160,32},{192,64},{224,... | collective-permute-start | bytes 6152 | tf_op jit(solution)/shard_map/ppermute | solution.py:466
  115.6 1.2 collective-permute-start.15
  116.8 3.6 %collective-permute-start.16 = (f32[4,128]{1,0:T(4,128)S(1)}, f32[4,128]{1,0:T(4,128)S(1)}, u32[]{:S(2)}, u32[]{:S(2)}) collective-permute-start(f32[4,128]{1,0:T(4,128)S(1)} %add.32), channel_id=1, source_target_pairs={{0,2},{1,3},{2,0},{3,1},{4,6},{5,7},{6,4},{7,5},{8,10},{9,11},{10,... | collective-permute-start | bytes 6152 | tf_op jit(solution)/shard_map/ppermute | solution.py:466
  120.4 1.0 copy-start.1
  123.8 12.4 %collective-permute-start.22 = (f32[4,128]{1,0:T(4,128)S(1)}, f32[4,128]{1,0:T(4,128)S(1)}, u32[]{:S(2)}, u32[]{:S(2)}) collective-permute-start(f32[4,128]{1,0:T(4,128)S(1)} %get-tuple-element.49), channel_id=1, source_target_pairs={{1,25},{3,27},{5,29},{7,31},{9,17},{11,19},{13,21},{15,23},{17,9},... | collective-permute-start | bytes 6152 | tf_op jit(solution)/shard_map/ppermute | solution.py:481
  126.4 9.9 %collective-permute-start.23 = (f32[4,128]{1,0:T(4,128)S(1)}, f32[4,128]{1,0:T(4,128)S(1)}, u32[]{:S(2)}, u32[]{:S(2)}) collective-permute-start(f32[4,128]{1,0:T(4,128)S(1)} %get-tuple-element.49), channel_id=1, source_target_pairs={{1,29},{3,31},{5,25},{7,27},{9,21},{11,23},{13,17},{15,19},{17,13}... | collective-permute-start | bytes 6152 | tf_op jit(solution)/shard_map/ppermute | solution.py:481
  127.8 10.0 %collective-permute-start.21 = (f32[4,128]{1,0:T(4,128)S(1)}, f32[4,128]{1,0:T(4,128)S(1)}, u32[]{:S(2)}, u32[]{:S(2)}) collective-permute-start(f32[4,128]{1,0:T(4,128)S(1)} %get-tuple-element.49), channel_id=1, source_target_pairs={{1,21},{3,23},{5,17},{7,19},{9,29},{11,31},{13,25},{15,27},{17,5},... | collective-permute-start | bytes 6152 | tf_op jit(solution)/shard_map/ppermute | solution.py:481
  128.0 9.8 %collective-permute-start.20 = (f32[4,128]{1,0:T(4,128)S(1)}, f32[4,128]{1,0:T(4,128)S(1)}, u32[]{:S(2)}, u32[]{:S(2)}) collective-permute-start(f32[4,128]{1,0:T(4,128)S(1)} %get-tuple-element.49), channel_id=1, source_target_pairs={{1,17},{3,19},{5,21},{7,23},{9,25},{11,27},{13,29},{15,31},{17,1},... | collective-permute-start | bytes 6152 | tf_op jit(solution)/shard_map/ppermute | solution.py:481
  137.9 4.1 %collective-permute-start.24 = (f32[4,128]{1,0:T(4,128)S(1)}, f32[4,128]{1,0:T(4,128)S(1)}, u32[]{:S(2)}, u32[]{:S(2)}) collective-permute-start(f32[4,128]{1,0:T(4,128)S(1)} %add_add_fusion.half_ref), channel_id=1, source_target_pairs={{0,1},{1,0},{2,3},{3,2},{4,5},{5,4},{6,7},{7,6},{8,9},{9,8},{10,11... | collective-permute-start | bytes 6152 | tf_op jit(solution)/shard_map/ppermute | solution.py:466

commit v4 on v3

--- a/solution.py
+++ b/solution.py
@@ -19,11 +19,10 @@
 ONES = 16
 TEMPORAL_FLOPS = 30 * 10**9
 XSTEPS = (1, 3, 2)
-TEMPORAL_MIB = 24
+TEMPORAL_MIB = 56
 UNPACK_MIB = 24
 TEMPORAL_ROWS = 32
 TOGETHER = 4
-HERE_FIRST = 3
 
 
 def dot(a, b, ca, cb):
@@ -232,9 +231,8 @@
 
 def temporal_kernel(gains_ref, *refs):
     ins = [ref.at[0] for ref in refs[:8]]
-    own, there, here, dgain_ref = refs[8], refs[9], refs[10:13], refs[13]
-    there = [there.at[i] for i in range(4)]
-    outs = [own.at[0]] + [ref.at[0] for ref in here] + there[1:] + there[:1]
+    own, onward, here, there, dgain_ref = refs[8], refs[9], refs[10:13], refs[13], refs[14]
+    outs = [own.at[0]] + [ref.at[0] for ref in here] + [onward.at[i] for i in range(3)] + [there.at[0]]
     _, frames, places, width = ins[0].shape
     rows = 8 * frames * 16
     gain_q, gain_k = gains_ref[2:3, :], gains_ref[3:4, :]
@@ -299,7 +297,7 @@
 
 def temporal(gains, parts):
     _, arrays, frames, places, width = parts[0].shape
-    sizes = (1, 4, 1, 1, 1)
+    sizes = (1, 3, 1, 1, 1, 1)
 
     def block(n):
         return pl.BlockSpec((n, arrays, frames, TEMPORAL_ROWS, width), lambda i: (0, 0, 0, i, 0))
@@ -315,7 +313,7 @@
         cost_estimate=cost(TEMPORAL_FLOPS, 4 << 20, 8 * 65536),
         name="temporal_attention",
     )(gains, *parts)
-    return res[0], res[1], res[2:5], res[5]
+    return res[0], res[1], res[2:5], res[5], res[6]
 
 
 def spatial_kernel(
@@ -498,14 +496,14 @@
         parts.append(along_x(onward[i : i + 1], step))
     parts.append(across(there))
 
-    own, there, here, grads_t = temporal(gains, parts)
-    there = across(there)
+    own, onward, here, there, grads_t = temporal(gains, parts)
+    onward, there = across(onward), across(there)
     here = [along_x(part, -step) for part, step in zip(here, XSTEPS)]
-    there_x = [along_x(there[i + 1 : i + 2], -step) for i, step in enumerate(XSTEPS)]
+    onward_x = [along_x(onward[i : i + 1], -step) for i, step in enumerate(XSTEPS)]
 
     res, grads = spatial(gains, grads_t, items)
-    home = over_tile(after(res, [there, *here[:HERE_FIRST]]))
-    *outs_t, grads = unpack_t(total_off_z(grads), [own, *here, there, *there_x])
+    home = over_tile(after(res, [onward, *here]))
+    *outs_t, grads = unpack_t(total_off_z(grads), [own, *here, there, *onward_x])
     *outs_s, gain_grads = unpack_s(home, total_z(grads), frames)
     return (*outs_s, *outs_t, gain_grads)
 

time: 145 us -> 144 us (level)
  starting transfers between devices: 59.3 us -> 55.3 us
  waiting for transfers between devices: 50.8 us -> 53.2 us
    all_to_all x2, starting transfers between devices: 17.5 us -> 15.8 us  [over_tile(): lax.all_to_all(x, 'tile', split_axis=0, concat_axis=0, tiled=True)]
    ppermute x3 -> x4, waiting for transfers between devices: 13.2 us -> 14.3 us  [across(): return lax.ppermute(x, 'frame', [(i, (i + 4) % 8) for i in range(8)])]
    unnamed x8 -> x22, local copies, waits for them, and re-layouts: 2.6 us -> 3.64 us
    ppermute x3 -> x4, starting transfers between devices: 8.07 us -> 7.76 us  [across(): return lax.ppermute(x, 'frame', [(i, (i + 4) % 8) for i in range(8)])]
  transfers between devices with their start and end apart: 27 -> 28, of which waited for: 12 -> 12; matrix products, arithmetic and copies ran while one was open for 1% -> 0% of each run, Pallas kernels for 16% -> 17%
where the time goes in v4:
time: 144 us; the launch traced here: 143 us
  starting transfers between devices  55.3 us (38%)
  waiting for transfers between devices  53.2 us (37%)
  Pallas kernels  29.7 us (21%)
  local copies, waits for them, and re-layouts  3.75 us (3%)
    ppermute x6, waiting for transfers between devices, from_partner(): return lax.ppermute(x, axis, [(i, i ^ bit) for i in range(size)])  20 us
    ppermute x12, starting transfers between devices, along_x(): lax.ppermute(x, 'frame', [(i, i // 4 * 4 + (i + step) % 4) for i in range...  19.1 us
    all_to_all x2, starting transfers between devices, over_tile(): lax.all_to_all(x, 'tile', split_axis=0, concat_axis=0, tiled=True)  15.8 us
    ppermute x4, waiting for transfers between devices, across(): return lax.ppermute(x, 'frame', [(i, (i + 4) % 8) for i in range(8)])  14.3 us
    pallas_call x1, Pallas kernels, spatial(): pl.pallas_call(spatial_kernel, out_shape=[jax.ShapeDtypeStruct(x.shape, B...  14 us
    ppermute x4, waiting for transfers between devices, total_z(): got.append(lax.ppermute(x, 'tile', perm))  9.98 us
    ppermute x6, starting transfers between devices, from_partner(): return lax.ppermute(x, axis, [(i, i ^ bit) for i in range(size)])  8.12 us
    ppermute x4, starting transfers between devices, across(): return lax.ppermute(x, 'frame', [(i, (i + 4) % 8) for i in range(8)])  7.76 us
  transfers between devices with their start and end apart: 28, of which 12 were waited for; matrix products, arithmetic and copies ran while one was open for 0% of the time, Pallas kernels for 17%

profile of v4, /device:TPU:2, one launch (start us, length us, event | category | flops | bytes accessed | tf_op | source)
XLA Modules:
  0.0 143.0 jit_solution(6703590461972360029)
XLA Ops:
  0.6 3.4 %pack.1 = (bf16[3,4,2,64,256]{4,3,2,1,0:T(8,128)(2,1)}, bf16[32,4,64,128]{3,2,1,0:T(8,128)(2,1)}) custom-call(bf16[2,64,2048]{2,1,0:T(8,128)(2,1)} %refs_0_.1, bf16[2,64,2048]{2,1,0:T(8,128)(2,1)} %refs_1_.1, bf16[2,64,2048]{2,1,0:T(8,128)(2,1)} %refs_2_.1, bf16[2,64,2048]{2,1,0:T(8,128)(2,1)} %refs_3_.1, bf16[2,64,2048]{2,1,0:T(8,128)(2,1)} %refs_4_.1, ...), custom_call_target="tpu_custom_call" | custom-call | bytes 6291456 | tf_op jit(solution)/shard_map/pack/pallas_call | solution.py:113
  4.1 3.3 %collective-permute-start.3 = (bf16[3,4,2,64,256]{4,3,2,1,0:T(8,128)(2,1)}, bf16[3,4,2,64,256]{4,3,2,1,0:T(8,128)(2,1)S(1)}, u32[]{:S(2)}, u32[]{:S(2)}) collective-permute-start(bf16[3,4,2,64,256]{4,3,2,1,0:T(8,128)(2,1)} %get-tuple-element.39), channel_id=1, source_target_pairs={{0,128},{32,160},{64,192},{96,224},{128,0},{160,32},{192,64},{224,... | collective-permute-start | bytes 2359304 | tf_op jit(solution)/shard_map/ppermute | solution.py:459
  7.3 9.0 %all-to-all-start = ((bf16[32,256,128]{2,1,0:T(8,128)(2,1)}), bf16[32,256,128]{2,1,0:T(8,128)(2,1)S(1)}, u32[]{:S(2)}, u32[]{:S(2)}) async-start(bf16[32,256,128]{2,1,0:T(8,128)(2,1)} %bitcast.7), calls=%async_computation | async-start | bytes 4194304 | tf_op jit(solution)/shard_map/all_to_all | solution.py:451
  16.3 2.4 %pack_here.1 = (bf16[1,4,2,64,256]{4,3,2,1,0:T(8,128)(2,1)}, bf16[1,4,2,64,256]{4,3,2,1,0:T(8,128)(2,1)}, bf16[1,4,2,64,256]{4,3,2,1,0:T(8,128)(2,1)}, bf16[1,4,...) custom-call(bf16[2,64,2048]{2,1,0:T(8,128)(2,1)} %refs_0_.1, bf16[2,64,2048]{2,1,0:T(8,128)(2,1)} %refs_1_.1, ...), custom_call_target="tpu_custom_call" | custom-call | bytes 2097152 | tf_op jit(solution)/shard_map/pack_here/pallas_call | solution.py:161
  18.8 1.6 %collective-permute-start = (bf16[1,4,2,64,256]{4,3,2,1,0:T(8,128)(2,1)}, bf16[1,4,2,64,256]{4,3,2,1,0:T(8,128)(2,1)S(1)}, u32[]{:S(2)}, u32[]{:S(2)}) collective-permute-start(bf16[1,4,2,64,256]{4,3,2,1,0:T(8,128)(2,1)} %get-tuple-element.36), channel_id=1, source_target_pairs={{0,32},{32,64},{64,96},{96,0},{128,160},{160,192},{192,224},{224,1... | collective-permute-start | bytes 786440 | tf_op jit(solution)/shard_map/ppermute | solution.py:455
  20.3 0.5 collective-permute-start.1
  20.9 2.1 %collective-permute-start.2 = (bf16[1,4,2,64,256]{4,3,2,1,0:T(8,128)(2,1)}, bf16[1,4,2,64,256]{4,3,2,1,0:T(8,128)(2,1)S(1)}, u32[]{:S(2)}, u32[]{:S(2)}) collective-permute-start(bf16[1,4,2,64,256]{4,3,2,1,0:T(8,128)(2,1)} %get-tuple-element.38), channel_id=1, source_target_pairs={{0,64},{32,96},{64,0},{96,32},{128,192},{160,224},{192,128},{224,1... | collective-permute-start | bytes 786440 | tf_op jit(solution)/shard_map/ppermute | solution.py:455
  23.0 1.8 %collective-permute-start.7 = (bf16[1,4,2,64,256]{4,3,2,1,0:T(8,128)(2,1)}, bf16[1,4,2,64,256]{4,3,2,1,0:T(8,128)(2,1)S(1)}, u32[]{:S(2)}, u32[]{:S(2)}) collective-permute-start(bf16[1,4,2,64,256]{4,3,2,1,0:T(8,128)(2,1)} %get-tuple-element.40), channel_id=1, source_target_pairs={{0,128},{32,160},{64,192},{96,224},{128,0},{160,32},{192,64},{224,... | collective-permute-start | bytes 786440 | tf_op jit(solution)/shard_map/ppermute | solution.py:459
  24.8 8.8 %collective-permute-done.3 = bf16[3,4,2,64,256]{4,3,2,1,0:T(8,128)(2,1)S(1)} collective-permute-done((bf16[3,4,2,64,256]{4,3,2,1,0:T(8,128)(2,1)}, bf16[3,4,2,64,256]{4,3,2,1,0:T(8,128)(2,1)S(1)}, u32[]{:S(2)}, u32[]{:S(2)}) %collective-permute-start.3) | collective-permute-done | bytes 786464 | tf_op jit(solution)/shard_map/ppermute | solution.py:459
  33.7 0.1 fusion.1
  33.7 1.6 %collective-permute-start.4 = (bf16[1,4,2,64,256]{4,3,2,1,0:T(8,128)(2,1)S(1)}, bf16[1,4,2,64,256]{4,3,2,1,0:T(8,128)(2,1)S(1)}, u32[]{:S(2)}, u32[]{:S(2)}) collective-permute-start(bf16[1,4,2,64,256]{4,3,2,1,0:T(8,128)(2,1)S(1)} %get-tuple-element.66), channel_id=1, source_target_pairs={{0,32},{32,64},{64,96},{96,0},{128,160},{160,192},{192,224},{224,1... | collective-permute-start | bytes 786440 | tf_op jit(solution)/shard_map/ppermute | solution.py:455
  35.3 0.0 collective-permute-done.refs_1_
  35.3 1.3 collective-permute-start.5
  36.6 0.0 collective-permute-done.1.refs_2_
  36.6 2.1 %collective-permute-start.6 = (bf16[1,4,2,64,256]{4,3,2,1,0:T(8,128)(2,1)S(1)}, bf16[1,4,2,64,256]{4,3,2,1,0:T(8,128)(2,1)S(1)}, u32[]{:S(2)}, u32[]{:S(2)}) collective-permute-start(bf16[1,4,2,64,256]{4,3,2,1,0:T(8,128)(2,1)S(1)} %get-tuple-element.64), channel_id=1, source_target_pairs={{0,64},{32,96},{64,0},{96,32},{128,192},{160,224},{192,128},{224,1... | collective-permute-start | bytes 786440 | tf_op jit(solution)/shard_map/ppermute | solution.py:455
  38.7 0.0 collective-permute-done.2.refs_3_
  38.7 5.4 %collective-permute-done.7.refs_7_ = bf16[1,4,2,64,256]{4,3,2,1,0:T(8,128)(2,1)S(1)} collective-permute-done((bf16[1,4,2,64,256]{4,3,2,1,0:T(8,128)(2,1)}, bf16[1,4,2,64,256]{4,3,2,1,0:T(8,128)(2,1)S(1)}, u32[]{:S(2)}, u32[]{:S(2)}) %collective-permute-start.7) | collective-permute-done | bytes 262176 | tf_op jit(solution)/shard_map/ppermute | solution.py:459
  44.1 0.0 collective-permute-done.4.refs_4_
  44.1 0.0 copy-start.9
  44.1 2.1 %collective-permute-done.6.refs_6_ = bf16[1,4,2,64,256]{4,3,2,1,0:T(8,128)(2,1)S(1)} collective-permute-done((bf16[1,4,2,64,256]{4,3,2,1,0:T(8,128)(2,1)S(1)}, bf16[1,4,2,64,256]{4,3,2,1,0:T(8,128)(2,1)S(1)}, u32[]{:S(2)}, u32[]{:S(2)}) %collective-permute-start.6) | collective-permute-done | bytes 262176 | tf_op jit(solution)/shard_map/ppermute | solution.py:455
  46.3 0.7 copy-done.10
  47.0 5.5 %temporal_attention.1 = (bf16[1,4,2,64,256]{4,3,2,1,0:T(8,128)(2,1)}, bf16[3,4,2,64,256]{4,3,2,1,0:T(8,128)(2,1)}, bf16[1,4,2,64,256]{4,3,2,1,0:T(8,128)(2,1)}, ...) custom-call(f32[4,128]{1,0:T(4,128)} %gains_ref.3, ...), custom_call_target="tpu_custom_call" | custom-call | flops 30000001024 | bytes 4194304 | tf_op jit(solution)/shard_map/temporal_attention/pallas_call | solution.py:305
  52.5 2.5 %collective-permute-start.8 = (bf16[3,4,2,64,256]{4,3,2,1,0:T(8,128)(2,1)}, bf16[3,4,2,64,256]{4,3,2,1,0:T(8,128)(2,1)S(1)}, u32[]{:S(2)}, u32[]{:S(2)}) collective-permute-start(bf16[3,4,2,64,256]{4,3,2,1,0:T(8,128)(2,1)} %get-tuple-element.44), channel_id=1, source_target_pairs={{0,128},{32,160},{64,192},{96,224},{128,0},{160,32},{192,64},{224,... | collective-permute-start | bytes 2359304 | tf_op jit(solution)/shard_map/ppermute | solution.py:459
  54.9 0.7 collective-permute-start.9
  55.6 1.3 collective-permute-start.10
  56.9 3.0 %collective-permute-start.11 = (bf16[1,4,2,64,256]{4,3,2,1,0:T(8,128)(2,1)}, bf16[1,4,2,64,256]{4,3,2,1,0:T(8,128)(2,1)}, u32[]{:S(2)}, u32[]{:S(2)}) collective-permute-start(bf16[1,4,2,64,256]{4,3,2,1,0:T(8,128)(2,1)} %get-tuple-element.47), channel_id=1, source_target_pairs={{0,64},{32,96},{64,0},{96,32},{128,192},{160,224},{192,128},{224,1... | collective-permute-start | bytes 786440 | tf_op jit(solution)/shard_map/ppermute | solution.py:455
  59.9 6.7 %all-to-all-done = bf16[32,256,128]{2,1,0:T(8,128)(2,1)S(1)} async-done(((bf16[32,256,128]{2,1,0:T(8,128)(2,1)}), bf16[32,256,128]{2,1,0:T(8,128)(2,1)S(1)}, u32[]{:S(2)}, u32[]{:S(2)}) %all-to-all-start) | async-done | bytes 2097184 | tf_op jit(solution)/shard_map/all_to_all | solution.py:451
  66.7 0.7 copy-done.3
  67.3 14.0 %spatial_attention.1 = (bf16[32,4,64,128]{3,2,1,0:T(8,128)(2,1)S(1)}, f32[4,128]{1,0:T(4,128)S(1)}) custom-call(f32[4,128]{1,0:T(4,128)S(1)} %copy-done.2, f32[2,128]{1,0:T(2,128)S(1)} %copy-done.3, bf16[32,4,64,128]{3,2,1,0:T(8,128)(2,1)S(1)} %bitcast.6), custom_call_target="tpu_custom_call" | custom-call | flops 6442450944 | bytes 4194304 | tf_op jit(solution)/shard_map/spatial_attention/pallas_call | solution.py:405
  81.3 0.0 collective-permute-done.9.refs_1_
  81.3 0.0 collective-permute-done.10.refs_2_
  81.3 0.0 collective-permute-done.8.refs_0_
  81.4 1.3 copy-done
  82.7 6.8 %all-to-all-start.1 = ((bf16[32,256,128]{2,1,0:T(8,128)(2,1)}), bf16[32,256,128]{2,1,0:T(8,128)(2,1)S(1)}, u32[]{:S(2)}, u32[]{:S(2)}) async-start(bf16[32,256,128]{2,1,0:T(8,128)(2,1)} %bitcast.5), calls=%async_computation.1 | async-start | bytes 4194304 | tf_op jit(solution)/shard_map/all_to_all | solution.py:451
  89.5 0.2 collective-permute-start.17
  89.7 0.1 fusion
  89.8 0.3 collective-permute-start.18
  90.1 1.8 %collective-permute-start.19 = (bf16[1,4,2,64,256]{4,3,2,1,0:T(8,128)(2,1)S(1)}, bf16[1,4,2,64,256]{4,3,2,1,0:T(8,128)(2,1)S(1)}, u32[]{:S(2)}, u32[]{:S(2)}) collective-permute-start(bf16[1,4,2,64,256]{4,3,2,1,0:T(8,128)(2,1)S(1)} %get-tuple-element.62), channel_id=1, source_target_pairs={{0,32},{32,64},{64,96},{96,0},{128,160},{160,192},{192,224},{224,1... | collective-permute-start | bytes 786440 | tf_op jit(solution)/shard_map/ppermute | solution.py:455
  91.9 2.8 %collective-permute-start.20 = (bf16[1,4,2,64,256]{4,3,2,1,0:T(8,128)(2,1)S(1)}, bf16[1,4,2,64,256]{4,3,2,1,0:T(8,128)(2,1)S(1)}, u32[]{:S(2)}, u32[]{:S(2)}) collective-permute-start(bf16[1,4,2,64,256]{4,3,2,1,0:T(8,128)(2,1)S(1)} %get-tuple-element.61), channel_id=1, source_target_pairs={{0,64},{32,96},{64,0},{96,32},{128,192},{160,224},{192,128},{224,1... | collective-permute-start | bytes 786440 | tf_op jit(solution)/shard_map/ppermute | solution.py:455
  94.7 0.2 collective-permute-start.12
  94.9 9.6 %collective-permute-done.12 = f32[4,128]{1,0:T(4,128)S(1)} collective-permute-done((f32[4,128]{1,0:T(4,128)S(1)}, f32[4,128]{1,0:T(4,128)S(1)}, u32[]{:S(2)}, u32[]{:S(2)}) %collective-permute-start.12) | collective-permute-done | bytes 2080 | tf_op jit(solution)/shard_map/ppermute | solution.py:464
  104.5 1.4 %collective-permute-start.13 = (f32[4,128]{1,0:T(4,128)S(1)}, f32[4,128]{1,0:T(4,128)S(1)}, u32[]{:S(2)}, u32[]{:S(2)}) collective-permute-start(f32[4,128]{1,0:T(4,128)S(1)} %add.29), channel_id=1, source_target_pairs={{0,64},{32,96},{64,0},{96,32},{128,192},{160,224},{192,128},{224,1... | collective-permute-start | bytes 6152 | tf_op jit(solution)/shard_map/ppermute | solution.py:464
  105.9 3.6 %collective-permute-done.13 = f32[4,128]{1,0:T(4,128)S(1)} collective-permute-done((f32[4,128]{1,0:T(4,128)S(1)}, f32[4,128]{1,0:T(4,128)S(1)}, u32[]{:S(2)}, u32[]{:S(2)}) %collective-permute-start.13) | collective-permute-done | bytes 2080 | tf_op jit(solution)/shard_map/ppermute | solution.py:464
  109.6 2.8 %collective-permute-start.14 = (f32[4,128]{1,0:T(4,128)S(1)}, f32[4,128]{1,0:T(4,128)S(1)}, u32[]{:S(2)}, u32[]{:S(2)}) collective-permute-start(f32[4,128]{1,0:T(4,128)S(1)} %add.30), channel_id=1, source_target_pairs={{0,128},{32,160},{64,192},{96,224},{128,0},{160,32},{192,64},{224,... | collective-permute-start | bytes 6152 | tf_op jit(solution)/shard_map/ppermute | solution.py:464
  112.4 2.3 %collective-permute-done.14 = f32[4,128]{1,0:T(4,128)S(1)} collective-permute-done((f32[4,128]{1,0:T(4,128)S(1)}, f32[4,128]{1,0:T(4,128)S(1)}, u32[]{:S(2)}, u32[]{:S(2)}) %collective-permute-start.14) | collective-permute-done | bytes 2080 | tf_op jit(solution)/shard_map/ppermute | solution.py:464
  114.7 1.2 collective-permute-done.15
  115.8 1.2 collective-permute-start.16
  117.1 2.6 %collective-permute-done.16 = f32[4,128]{1,0:T(4,128)S(1)} collective-permute-done((f32[4,128]{1,0:T(4,128)S(1)}, f32[4,128]{1,0:T(4,128)S(1)}, u32[]{:S(2)}, u32[]{:S(2)}) %collective-permute-start.16) | collective-permute-done | bytes 2080 | tf_op jit(solution)/shard_map/ppermute | solution.py:464
  119.6 0.0 collective-permute-done.19.refs_6_
  119.7 0.0 collective-permute-done.20.refs_7_
  119.7 0.9 copy-done.1
  120.6 2.4 %unpack_temporal.1 = (bf16[2,64,2048]{2,1,0:T(8,128)(2,1)}, bf16[2,64,2048]{2,1,0:T(8,128)(2,1)}, bf16[2,64,2048]{2,1,0:T(8,128)(2,1)}, bf16[2,64,2048]{2,1,0:T(8,128)(2,1)}, f32[4,128]{1,0:T(4,128)S(1)}) custom-call(f32[4,128]{1,0:T(4,128)S(1)} %add.33.grads_ref, bf16[1,4,2,64,256]{4,3,2,1,0:T(8,128)(2,1)S(1)} %copy-done.1, ...), custom_call_target="tpu_custom_call" | custom-call | bytes 4194304 | tf_op jit(solution)/shard_map/unpack_temporal/pallas_call | solution.py:219
  123.0 2.4 %collective-permute-start.23 = (f32[4,128]{1,0:T(4,128)S(1)}, f32[4,128]{1,0:T(4,128)S(1)}, u32[]{:S(2)}, u32[]{:S(2)}) collective-permute-start(f32[4,128]{1,0:T(4,128)S(1)} %get-tuple-element.51), channel_id=1, source_target_pairs={{1,25},{3,27},{5,29},{7,31},{9,17},{11,19},{13,21},{15,23},{17,9},... | collective-permute-start | bytes 6152 | tf_op jit(solution)/shard_map/ppermute | solution.py:479
  125.4 1.4 %collective-permute-start.24 = (f32[4,128]{1,0:T(4,128)S(1)}, f32[4,128]{1,0:T(4,128)S(1)}, u32[]{:S(2)}, u32[]{:S(2)}) collective-permute-start(f32[4,128]{1,0:T(4,128)S(1)} %get-tuple-element.51), channel_id=1, source_target_pairs={{1,29},{3,31},{5,25},{7,27},{9,21},{11,23},{13,17},{15,19},{17,13}... | collective-permute-start | bytes 6152 | tf_op jit(solution)/shard_map/ppermute | solution.py:479
  126.8 0.0 collective-permute-start.22
  126.9 0.6 collective-permute-start.21
  127.5 8.4 %collective-permute-done.23 = f32[4,128]{1,0:T(4,128)S(1)} collective-permute-done((f32[4,128]{1,0:T(4,128)S(1)}, f32[4,128]{1,0:T(4,128)S(1)}, u32[]{:S(2)}, u32[]{:S(2)}) %collective-permute-start.23) | collective-permute-done | bytes 2080 | tf_op jit(solution)/shard_map/ppermute | solution.py:479
  135.9 0.0 collective-permute-done.24
  135.9 1.6 %collective-permute-done.22 = f32[4,128]{1,0:T(4,128)S(1)} collective-permute-done((f32[4,128]{1,0:T(4,128)S(1)}, f32[4,128]{1,0:T(4,128)S(1)}, u32[]{:S(2)}, u32[]{:S(2)}) %collective-permute-start.22) | collective-permute-done | bytes 2080 | tf_op jit(solution)/shard_map/ppermute | solution.py:479
  137.5 0.0 collective-permute-done.21
  137.5 2.4 %collective-permute-start.25 = (f32[4,128]{1,0:T(4,128)S(1)}, f32[4,128]{1,0:T(4,128)S(1)}, u32[]{:S(2)}, u32[]{:S(2)}) collective-permute-start(f32[4,128]{1,0:T(4,128)S(1)} %add_add_fusion.half_ref), channel_id=1, source_target_pairs={{0,1},{1,0},{2,3},{3,2},{4,5},{5,4},{6,7},{7,6},{8,9},{9,8},{10,11... | collective-permute-start | bytes 6152 | tf_op jit(solution)/shard_map/ppermute | solution.py:464
  139.9 0.8 collective-permute-done.25.other_ref
  140.8 0.0 all-to-all-done.1
  140.8 2.1 %unpack_spatial.1 = (bf16[2,64,2048]{2,1,0:T(8,128)(2,1)}, bf16[2,64,2048]{2,1,0:T(8,128)(2,1)}, bf16[2,64,2048]{2,1,0:T(8,128)(2,1)}, bf16[2,64,2048]{2,1,0:T(8,128)(2,1)}, f32[4,128]{1,0:T(4,128)}) custom-call(bf16[2,16,4,64,128]{4,3,2,1,0:T(8,128)(2,1)S(1)} %bitcast.4, f32[4,128]{1,0:T(4,128)S(1)} %add_add_fusion.half_ref, ...), custom_call_target="tpu_custom_call" | custom-call | bytes 4194304 | tf_op jit(solution)/shard_map/unpack_spatial/pallas_call | solution.py:190
  (29 shorter events, 0.1 us)
Async XLA Ops:
  4.1 29.6 %collective-permute-start.3 = (bf16[3,4,2,64,256]{4,3,2,1,0:T(8,128)(2,1)}, bf16[3,4,2,64,256]{4,3,2,1,0:T(8,128)(2,1)S(1)}, u32[]{:S(2)}, u32[]{:S(2)}) collective-permute-start(bf16[3,4,2,64,256]{4,3,2,1,0:T(8,128)(2,1)} %get-tuple-element.39), channel_id=1, source_target_pairs={{0,128},{32,160},{64,192},{96,224},{128,0},{160,32},{192,64},{224,... | collective-permute-start | bytes 2359304 | tf_op jit(solution)/shard_map/ppermute | solution.py:459
  7.3 59.3 %all-to-all-start = ((bf16[32,256,128]{2,1,0:T(8,128)(2,1)}), bf16[32,256,128]{2,1,0:T(8,128)(2,1)S(1)}, u32[]{:S(2)}, u32[]{:S(2)}) async-start(bf16[32,256,128]{2,1,0:T(8,128)(2,1)} %bitcast.7), calls=%async_computation | async-start | bytes 4194304 | tf_op jit(solution)/shard_map/all_to_all | solution.py:451
  18.8 16.5 %collective-permute-start = (bf16[1,4,2,64,256]{4,3,2,1,0:T(8,128)(2,1)}, bf16[1,4,2,64,256]{4,3,2,1,0:T(8,128)(2,1)S(1)}, u32[]{:S(2)}, u32[]{:S(2)}) collective-permute-start(bf16[1,4,2,64,256]{4,3,2,1,0:T(8,128)(2,1)} %get-tuple-element.36), channel_id=1, source_target_pairs={{0,32},{32,64},{64,96},{96,0},{128,160},{160,192},{192,224},{224,1... | collective-permute-start | bytes 786440 | tf_op jit(solution)/shard_map/ppermute | solution.py:455
  20.3 16.3 %collective-permute-start.1 = (bf16[1,4,2,64,256]{4,3,2,1,0:T(8,128)(2,1)}, bf16[1,4,2,64,256]{4,3,2,1,0:T(8,128)(2,1)S(1)}, u32[]{:S(2)}, u32[]{:S(2)}) collective-permute-start(bf16[1,4,2,64,256]{4,3,2,1,0:T(8,128)(2,1)} %get-tuple-element.37), channel_id=1, source_target_pairs={{0,96},{32,0},{64,32},{96,64},{128,224},{160,128},{192,160},{224,1... | collective-permute-start | bytes 786440 | tf_op jit(solution)/shard_map/ppermute | solution.py:455
  20.9 17.8 %collective-permute-start.2 = (bf16[1,4,2,64,256]{4,3,2,1,0:T(8,128)(2,1)}, bf16[1,4,2,64,256]{4,3,2,1,0:T(8,128)(2,1)S(1)}, u32[]{:S(2)}, u32[]{:S(2)}) collective-permute-start(bf16[1,4,2,64,256]{4,3,2,1,0:T(8,128)(2,1)} %get-tuple-element.38), channel_id=1, source_target_pairs={{0,64},{32,96},{64,0},{96,32},{128,192},{160,224},{192,128},{224,1... | collective-permute-start | bytes 786440 | tf_op jit(solution)/shard_map/ppermute | solution.py:455
  23.0 21.1 %collective-permute-start.7 = (bf16[1,4,2,64,256]{4,3,2,1,0:T(8,128)(2,1)}, bf16[1,4,2,64,256]{4,3,2,1,0:T(8,128)(2,1)S(1)}, u32[]{:S(2)}, u32[]{:S(2)}) collective-permute-start(bf16[1,4,2,64,256]{4,3,2,1,0:T(8,128)(2,1)} %get-tuple-element.40), channel_id=1, source_target_pairs={{0,128},{32,160},{64,192},{96,224},{128,0},{160,32},{192,64},{224,... | collective-permute-start | bytes 786440 | tf_op jit(solution)/shard_map/ppermute | solution.py:459
  33.7 10.4 %collective-permute-start.4 = (bf16[1,4,2,64,256]{4,3,2,1,0:T(8,128)(2,1)S(1)}, bf16[1,4,2,64,256]{4,3,2,1,0:T(8,128)(2,1)S(1)}, u32[]{:S(2)}, u32[]{:S(2)}) collective-permute-start(bf16[1,4,2,64,256]{4,3,2,1,0:T(8,128)(2,1)S(1)} %get-tuple-element.66), channel_id=1, source_target_pairs={{0,32},{32,64},{64,96},{96,0},{128,160},{160,192},{192,224},{224,1... | collective-permute-start | bytes 786440 | tf_op jit(solution)/shard_map/ppermute | solution.py:455
  35.3 11.0 %copy-start.4 = (bf16[1,4,2,64,256]{4,3,2,1,0:T(8,128)(2,1)}, bf16[1,4,2,64,256]{4,3,2,1,0:T(8,128)(2,1)S(1)}, u32[]{:S(2)}) copy-start(bf16[1,4,2,64,256]{4,3,2,1,0:T(8,128)(2,1)S(1)} %collective-permute-done.refs_1_) | copy-start | bytes 786436
  35.3 8.8 %collective-permute-start.5 = (bf16[1,4,2,64,256]{4,3,2,1,0:T(8,128)(2,1)S(1)}, bf16[1,4,2,64,256]{4,3,2,1,0:T(8,128)(2,1)S(1)}, u32[]{:S(2)}, u32[]{:S(2)}) collective-permute-start(bf16[1,4,2,64,256]{4,3,2,1,0:T(8,128)(2,1)S(1)} %get-tuple-element.65), channel_id=1, source_target_pairs={{0,96},{32,0},{64,32},{96,64},{128,224},{160,128},{192,160},{224,1... | collective-permute-start | bytes 786440 | tf_op jit(solution)/shard_map/ppermute | solution.py:455
  36.6 9.7 %copy-start.5 = (bf16[1,4,2,64,256]{4,3,2,1,0:T(8,128)(2,1)}, bf16[1,4,2,64,256]{4,3,2,1,0:T(8,128)(2,1)S(1)}, u32[]{:S(2)}) copy-start(bf16[1,4,2,64,256]{4,3,2,1,0:T(8,128)(2,1)S(1)} %collective-permute-done.1.refs_2_) | copy-start | bytes 786436
  36.6 9.7 %collective-permute-start.6 = (bf16[1,4,2,64,256]{4,3,2,1,0:T(8,128)(2,1)S(1)}, bf16[1,4,2,64,256]{4,3,2,1,0:T(8,128)(2,1)S(1)}, u32[]{:S(2)}, u32[]{:S(2)}) collective-permute-start(bf16[1,4,2,64,256]{4,3,2,1,0:T(8,128)(2,1)S(1)} %get-tuple-element.64), channel_id=1, source_target_pairs={{0,64},{32,96},{64,0},{96,32},{128,192},{160,224},{192,128},{224,1... | collective-permute-start | bytes 786440 | tf_op jit(solution)/shard_map/ppermute | solution.py:455
  38.7 7.6 %copy-start.6 = (bf16[1,4,2,64,256]{4,3,2,1,0:T(8,128)(2,1)}, bf16[1,4,2,64,256]{4,3,2,1,0:T(8,128)(2,1)S(1)}, u32[]{:S(2)}) copy-start(bf16[1,4,2,64,256]{4,3,2,1,0:T(8,128)(2,1)S(1)} %collective-permute-done.2.refs_3_) | copy-start | bytes 786436
  44.1 2.2 %copy-start.7 = (bf16[1,4,2,64,256]{4,3,2,1,0:T(8,128)(2,1)}, bf16[1,4,2,64,256]{4,3,2,1,0:T(8,128)(2,1)S(1)}, u32[]{:S(2)}) copy-start(bf16[1,4,2,64,256]{4,3,2,1,0:T(8,128)(2,1)S(1)} %collective-permute-done.7.refs_7_) | copy-start | bytes 786436
  44.1 2.2 %copy-start.8 = (bf16[1,4,2,64,256]{4,3,2,1,0:T(8,128)(2,1)}, bf16[1,4,2,64,256]{4,3,2,1,0:T(8,128)(2,1)S(1)}, u32[]{:S(2)}) copy-start(bf16[1,4,2,64,256]{4,3,2,1,0:T(8,128)(2,1)S(1)} %collective-permute-done.4.refs_4_) | copy-start | bytes 786436
  44.1 2.2 %copy-start.9 = (bf16[1,4,2,64,256]{4,3,2,1,0:T(8,128)(2,1)}, bf16[1,4,2,64,256]{4,3,2,1,0:T(8,128)(2,1)S(1)}, u32[]{:S(2)}) copy-start(bf16[1,4,2,64,256]{4,3,2,1,0:T(8,128)(2,1)S(1)} %collective-permute-done.5.refs_5_) | copy-start | bytes 786436
  46.3 0.7 copy-start.10
  47.0 19.7 %copy-start.2 = (f32[4,128]{1,0:T(4,128)S(1)}, f32[4,128]{1,0:T(4,128)}, u32[]{:S(2)}) copy-start(f32[4,128]{1,0:T(4,128)} %gains_ref.3) | copy-start | bytes 6148
  52.5 28.9 %collective-permute-start.8 = (bf16[3,4,2,64,256]{4,3,2,1,0:T(8,128)(2,1)}, bf16[3,4,2,64,256]{4,3,2,1,0:T(8,128)(2,1)S(1)}, u32[]{:S(2)}, u32[]{:S(2)}) collective-permute-start(bf16[3,4,2,64,256]{4,3,2,1,0:T(8,128)(2,1)} %get-tuple-element.44), channel_id=1, source_target_pairs={{0,128},{32,160},{64,192},{96,224},{128,0},{160,32},{192,64},{224,... | collective-permute-start | bytes 2359304 | tf_op jit(solution)/shard_map/ppermute | solution.py:459
  54.9 26.4 %collective-permute-start.9 = (bf16[1,4,2,64,256]{4,3,2,1,0:T(8,128)(2,1)}, bf16[1,4,2,64,256]{4,3,2,1,0:T(8,128)(2,1)S(1)}, u32[]{:S(2)}, u32[]{:S(2)}) collective-permute-start(bf16[1,4,2,64,256]{4,3,2,1,0:T(8,128)(2,1)} %get-tuple-element.45), channel_id=1, source_target_pairs={{0,96},{32,0},{64,32},{96,64},{128,224},{160,128},{192,160},{224,1... | collective-permute-start | bytes 786440 | tf_op jit(solution)/shard_map/ppermute | solution.py:455
  55.6 25.7 %collective-permute-start.10 = (bf16[1,4,2,64,256]{4,3,2,1,0:T(8,128)(2,1)}, bf16[1,4,2,64,256]{4,3,2,1,0:T(8,128)(2,1)S(1)}, u32[]{:S(2)}, u32[]{:S(2)}) collective-permute-start(bf16[1,4,2,64,256]{4,3,2,1,0:T(8,128)(2,1)} %get-tuple-element.46), channel_id=1, source_target_pairs={{0,32},{32,64},{64,96},{96,0},{128,160},{160,192},{192,224},{224,1... | collective-permute-start | bytes 786440 | tf_op jit(solution)/shard_map/ppermute | solution.py:455
  56.9 24.4 %collective-permute-start.11 = (bf16[1,4,2,64,256]{4,3,2,1,0:T(8,128)(2,1)}, bf16[1,4,2,64,256]{4,3,2,1,0:T(8,128)(2,1)}, u32[]{:S(2)}, u32[]{:S(2)}) collective-permute-start(bf16[1,4,2,64,256]{4,3,2,1,0:T(8,128)(2,1)} %get-tuple-element.47), channel_id=1, source_target_pairs={{0,64},{32,96},{64,0},{96,32},{128,192},{160,224},{192,128},{224,1... | collective-permute-start | bytes 786440 | tf_op jit(solution)/shard_map/ppermute | solution.py:455
  66.6 0.7 copy-start.3
  81.3 1.3 copy-start
  82.7 58.1 %all-to-all-start.1 = ((bf16[32,256,128]{2,1,0:T(8,128)(2,1)}), bf16[32,256,128]{2,1,0:T(8,128)(2,1)S(1)}, u32[]{:S(2)}, u32[]{:S(2)}) async-start(bf16[32,256,128]{2,1,0:T(8,128)(2,1)} %bitcast.5), calls=%async_computation.1 | async-start | bytes 4194304 | tf_op jit(solution)/shard_map/all_to_all | solution.py:451
  89.5 30.1 %collective-permute-start.17 = (bf16[1,4,2,64,256]{4,3,2,1,0:T(8,128)(2,1)}, bf16[1,4,2,64,256]{4,3,2,1,0:T(8,128)(2,1)S(1)}, u32[]{:S(2)}, u32[]{:S(2)}) collective-permute-start(bf16[1,4,2,64,256]{4,3,2,1,0:T(8,128)(2,1)} %get-tuple-element.50), channel_id=1, source_target_pairs={{0,128},{32,160},{64,192},{96,224},{128,0},{160,32},{192,64},{224,... | collective-permute-start | bytes 786440 | tf_op jit(solution)/shard_map/ppermute | solution.py:459
  89.8 29.9 %collective-permute-start.18 = (bf16[1,4,2,64,256]{4,3,2,1,0:T(8,128)(2,1)S(1)}, bf16[1,4,2,64,256]{4,3,2,1,0:T(8,128)(2,1)S(1)}, u32[]{:S(2)}, u32[]{:S(2)}) collective-permute-start(bf16[1,4,2,64,256]{4,3,2,1,0:T(8,128)(2,1)S(1)} %get-tuple-element.63), channel_id=1, source_target_pairs={{0,96},{32,0},{64,32},{96,64},{128,224},{160,128},{192,160},{224,1... | collective-permute-start | bytes 786440 | tf_op jit(solution)/shard_map/ppermute | solution.py:455
  90.1 29.6 %collective-permute-start.19 = (bf16[1,4,2,64,256]{4,3,2,1,0:T(8,128)(2,1)S(1)}, bf16[1,4,2,64,256]{4,3,2,1,0:T(8,128)(2,1)S(1)}, u32[]{:S(2)}, u32[]{:S(2)}) collective-permute-start(bf16[1,4,2,64,256]{4,3,2,1,0:T(8,128)(2,1)S(1)} %get-tuple-element.62), channel_id=1, source_target_pairs={{0,32},{32,64},{64,96},{96,0},{128,160},{160,192},{192,224},{224,1... | collective-permute-start | bytes 786440 | tf_op jit(solution)/shard_map/ppermute | solution.py:455
  91.9 27.8 %collective-permute-start.20 = (bf16[1,4,2,64,256]{4,3,2,1,0:T(8,128)(2,1)S(1)}, bf16[1,4,2,64,256]{4,3,2,1,0:T(8,128)(2,1)S(1)}, u32[]{:S(2)}, u32[]{:S(2)}) collective-permute-start(bf16[1,4,2,64,256]{4,3,2,1,0:T(8,128)(2,1)S(1)} %get-tuple-element.61), channel_id=1, source_target_pairs={{0,64},{32,96},{64,0},{96,32},{128,192},{160,224},{192,128},{224,1... | collective-permute-start | bytes 786440 | tf_op jit(solution)/shard_map/ppermute | solution.py:455
  94.7 9.8 %collective-permute-start.12 = (f32[4,128]{1,0:T(4,128)S(1)}, f32[4,128]{1,0:T(4,128)S(1)}, u32[]{:S(2)}, u32[]{:S(2)}) collective-permute-start(f32[4,128]{1,0:T(4,128)S(1)} %get-tuple-element.48), channel_id=1, source_target_pairs={{0,32},{32,0},{64,96},{96,64},{128,160},{160,128},{192,224},{224,1... | collective-permute-start | bytes 6152 | tf_op jit(solution)/shard_map/ppermute | solution.py:464
  104.5 5.1 %collective-permute-start.13 = (f32[4,128]{1,0:T(4,128)S(1)}, f32[4,128]{1,0:T(4,128)S(1)}, u32[]{:S(2)}, u32[]{:S(2)}) collective-permute-start(f32[4,128]{1,0:T(4,128)S(1)} %add.29), channel_id=1, source_target_pairs={{0,64},{32,96},{64,0},{96,32},{128,192},{160,224},{192,128},{224,1... | collective-permute-start | bytes 6152 | tf_op jit(solution)/shard_map/ppermute | solution.py:464
  109.6 5.1 %collective-permute-start.14 = (f32[4,128]{1,0:T(4,128)S(1)}, f32[4,128]{1,0:T(4,128)S(1)}, u32[]{:S(2)}, u32[]{:S(2)}) collective-permute-start(f32[4,128]{1,0:T(4,128)S(1)} %add.30), channel_id=1, source_target_pairs={{0,128},{32,160},{64,192},{96,224},{128,0},{160,32},{192,64},{224,... | collective-permute-start | bytes 6152 | tf_op jit(solution)/shard_map/ppermute | solution.py:464
  114.7 1.2 collective-permute-start.15
  115.8 3.8 %collective-permute-start.16 = (f32[4,128]{1,0:T(4,128)S(1)}, f32[4,128]{1,0:T(4,128)S(1)}, u32[]{:S(2)}, u32[]{:S(2)}) collective-permute-start(f32[4,128]{1,0:T(4,128)S(1)} %add.32), channel_id=1, source_target_pairs={{0,2},{1,3},{2,0},{3,1},{4,6},{5,7},{6,4},{7,5},{8,10},{9,11},{10,... | collective-permute-start | bytes 6152 | tf_op jit(solution)/shard_map/ppermute | solution.py:464
  119.7 1.0 copy-start.1
  123.0 12.9 %collective-permute-start.23 = (f32[4,128]{1,0:T(4,128)S(1)}, f32[4,128]{1,0:T(4,128)S(1)}, u32[]{:S(2)}, u32[]{:S(2)}) collective-permute-start(f32[4,128]{1,0:T(4,128)S(1)} %get-tuple-element.51), channel_id=1, source_target_pairs={{1,25},{3,27},{5,29},{7,31},{9,17},{11,19},{13,21},{15,23},{17,9},... | collective-permute-start | bytes 6152 | tf_op jit(solution)/shard_map/ppermute | solution.py:479
  125.4 10.5 %collective-permute-start.24 = (f32[4,128]{1,0:T(4,128)S(1)}, f32[4,128]{1,0:T(4,128)S(1)}, u32[]{:S(2)}, u32[]{:S(2)}) collective-permute-start(f32[4,128]{1,0:T(4,128)S(1)} %get-tuple-element.51), channel_id=1, source_target_pairs={{1,29},{3,31},{5,25},{7,27},{9,21},{11,23},{13,17},{15,19},{17,13}... | collective-permute-start | bytes 6152 | tf_op jit(solution)/shard_map/ppermute | solution.py:479
  126.8 10.7 %collective-permute-start.22 = (f32[4,128]{1,0:T(4,128)S(1)}, f32[4,128]{1,0:T(4,128)S(1)}, u32[]{:S(2)}, u32[]{:S(2)}) collective-permute-start(f32[4,128]{1,0:T(4,128)S(1)} %get-tuple-element.51), channel_id=1, source_target_pairs={{1,21},{3,23},{5,17},{7,19},{9,29},{11,31},{13,25},{15,27},{17,5},... | collective-permute-start | bytes 6152 | tf_op jit(solution)/shard_map/ppermute | solution.py:479
  126.9 10.7 %collective-permute-start.21 = (f32[4,128]{1,0:T(4,128)S(1)}, f32[4,128]{1,0:T(4,128)S(1)}, u32[]{:S(2)}, u32[]{:S(2)}) collective-permute-start(f32[4,128]{1,0:T(4,128)S(1)} %get-tuple-element.51), channel_id=1, source_target_pairs={{1,17},{3,19},{5,21},{7,23},{9,25},{11,27},{13,29},{15,31},{17,1},... | collective-permute-start | bytes 6152 | tf_op jit(solution)/shard_map/ppermute | solution.py:479
  137.5 3.2 %collective-permute-start.25 = (f32[4,128]{1,0:T(4,128)S(1)}, f32[4,128]{1,0:T(4,128)S(1)}, u32[]{:S(2)}, u32[]{:S(2)}) collective-permute-start(f32[4,128]{1,0:T(4,128)S(1)} %add_add_fusion.half_ref), channel_id=1, source_target_pairs={{0,1},{1,0},{2,3},{3,2},{4,5},{5,4},{6,7},{7,6},{8,9},{9,8},{10,11... | collective-permute-start | bytes 6152 | tf_op jit(solution)/shard_map/ppermute | solution.py:464
